TPU v7x, 512 devices: a whole 4x4x16 slice. The times are simulated.
512 devices in a mesh: vocab: 64 (over x, z), width: 8 (over y, core).
Axes of the slice: x: 4, y: 4, z: 16, core: 2. Of those that a mesh axis runs over, the one named last changes fastest.
Arguments:
- hidden_states: bfloat16 [512, 5120], P('vocab', 'width'), may hold values from -12 to 12
- head_weight: bfloat16 [81920, 5120], P('vocab', 'width'), may hold values from -0.26553307 to 0.26553307
- targets: int32 [512], replicated, may hold values from 0 to 81919
- terminal: int32 [512], replicated, may hold values 0 or 1
- cotangent: float32 [512], replicated, may hold values from -6 to 6
Outputs:
- rewards: float32 [512], replicated
- hidden_grad: bfloat16 [512, 5120], P('vocab', 'width')
- weight_grad: bfloat16 [81920, 5120], P('vocab', 'width')
All inputs are finite; a program needn't handle non-finite values.
Results may differ from a plain program's by a relative error of at most 0.0051.
Values may be sent and summed in bfloat16 or wider, within the bound.
No kernel may reach another device: no remote copies, remote signals or barrier semaphores. Data moves between devices by JAX's collectives and lax.ppermute only.
A program may use at most 64 MiB of HBM per device.

v0:
```python
import jax
import jax.numpy as jnp
from jax import lax
from jax.sharding import PartitionSpec as P

discount = 0.99


def row_statistics(logits, row_targets, col_start):
    columns = jnp.arange(logits.shape[1], dtype=jnp.int32)
    hit = (row_targets - col_start)[:, None] == columns[None, :]
    picked_local = jnp.sum(jnp.where(hit, logits, 0.0), axis=1)
    local_top = jnp.max(logits, axis=1)
    top = lax.pmax(local_top, "vocab")
    total, picked = lax.psum(
        (jnp.sum(jnp.exp(logits - top[:, None]), axis=1), picked_local), "vocab"
    )
    return (top + jnp.log(total), picked, hit)


def shards(hidden_states, head_weight, targets, terminal, cotangent):
    voc_rows = head_weight.shape[0]
    col_start = lax.axis_index("vocab") * voc_rows
    hidden_all = lax.all_gather(hidden_states, "vocab", axis=0, tiled=True)
    partial_logits = lax.dot_general(
        hidden_all, head_weight, (((1,), (1,)), ((), ())), preferred_element_type=jnp.float32
    )
    keep = discount * (1.0 - terminal.astype(jnp.float32))
    carried = jnp.concatenate([jnp.zeros((1,), jnp.float32), (keep * cotangent)[:-1]])
    logits = lax.psum(partial_logits, "width")
    lse, picked, hit = row_statistics(logits, targets, col_start)
    probs = jnp.exp(logits - lse[:, None])
    dlogits = (jnp.where(hit, cotangent[:, None], 0.0) - carried[:, None] * probs).astype(
        jnp.bfloat16
    )
    next_value = jnp.concatenate([lse[1:], jnp.zeros((1,), jnp.float32)])
    rewards = picked - keep * next_value
    hidden_grad = lax.psum_scatter(
        jnp.dot(dlogits, head_weight, preferred_element_type=jnp.float32),
        "vocab",
        scatter_dimension=0,
        tiled=True,
    ).astype(jnp.bfloat16)
    weight_grad = lax.dot_general(
        dlogits, hidden_all, (((0,), (0,)), ((), ())), preferred_element_type=jnp.float32
    ).astype(jnp.bfloat16)
    return (rewards, hidden_grad, weight_grad)


def solution(mesh):
    placed = (P("vocab", "width"), P("vocab", "width"), P(), P(), P())
    return jax.shard_map(
        shards,
        mesh=mesh,
        in_specs=placed,
        out_specs=(P(), P("vocab", "width"), P("vocab", "width")),
        check_vma=False,
    )
```

profile of v0, /device:TPU:24, one launch (start us, length us, event | category | flops | bytes accessed | tf_op | source)
XLA Modules:
  0.0 787.2 jit_solution(14596230555298333359)
XLA Ops:
  7.2 0.0 copy-start
  7.2 0.0 all-reduce.5.cloned.1.call-start
  7.2 107.0 %all_gather.3 = bf16[512,640]{1,0:T(8,128)(2,1)S(1)} all-gather(bf16[8,640]{1,0:T(8,128)(2,1)} %param.5), channel_id=1, replica_groups=mesh['vocab'=64,'width'=8] {'vocab'}, dimensions={0}, use_global_device_ids=true | all-gather | bytes 665600 | tf_op jit(solution)/shard_map/all_gather | solution.py:24
  114.2 0.0 copy-start.1
  114.2 0.8 copy-done.1
  115.0 0.0 copy-done
  115.0 0.0 copy-start.3
  115.0 0.0 copy-start.4
  115.0 0.0 copy-start.5
  115.0 2.8 fusion.2
  117.8 0.0 all-reduce.5.cloned.1.call-update
  117.8 1.3 dynamic-slice
  119.8 0.0 copy-done.3
  119.8 0.0 copy-done.4
  119.8 0.1 pad_maximum_fusion
  119.9 0.0 copy-done.5
  119.9 73.6 %all-reduce.5.cloned.1.call-done = f32[512,1280]{1,0:T(8,128)} async-done(((f32[512,1280]{1,0:T(8,128)}), f32[512,1280]{1,0:T(8,128)}) %all-reduce.5.cloned.1.call-update) | async-done | bytes 2621456 | tf_op jit(solution)/shard_map/psum | solution.py:30
  193.5 1.9 reduce_max.9
  195.4 144.1 %pmax.7 = f32[512]{0:T(512)S(1)} all-reduce(f32[512]{0:T(512)S(1)} %reduce_max.9), channel_id=1, replica_groups=mesh['vocab'=64,'width'=8] {'vocab'}, use_global_device_ids=true, to_apply=%region_4.5 | all-reduce | flops 512 | bytes 4096 | tf_op jit(solution)/shard_map/pmax | solution.py:14
  339.6 2.5 exponential_reduce_fusion
  342.0 138.0 %psum.23 = f32[512]{0:T(512)S(1)} all-reduce(f32[512]{0:T(512)S(1)} %get-tuple-element.3), channel_id=1, replica_groups=mesh['vocab'=64,'width'=8] {'vocab'}, use_global_device_ids=true, to_apply=%region_6.7 | all-reduce | flops 512 | bytes 4096 | tf_op jit(solution)/shard_map/psum | solution.py:15
  480.1 0.1 slice.6
  480.1 2.6 subtract_convert_fusion
  482.7 0.0 copy-start.2
  482.7 1.2 fusion.3
  483.9 0.0 copy-done.2
  483.9 2.4 convolution_convert_fusion
  486.3 292.1 %all-reduce.6 = (f32[512]{0:T(512)S(1)}, bf16[512,640]{1,0:T(8,128)(2,1)}) all-reduce(f32[512]{0:T(512)S(1)} %get-tuple-element.4, f32[512,640]{1,0:T(8,128)S(1)} %fusion.3), channel_id=1, replica_groups=mesh['vocab'=64,'width'=8] {'vocab'}, use_global_device_ids=true, to_apply=%region_2.3 | all-reduce | flops 328192 | bytes 1970176 | tf_op jit(solution)/shard_map/psum | solution.py:15
  778.4 0.7 fusion
  779.1 1.3 dynamic-slice_convert_fusion
  (3 shorter events, 0.0 us)
Async XLA Ops:
  7.2 107.9 %copy-start = (bf16[1280,640]{1,0:T(8,128)(2,1)S(1)}, bf16[1280,640]{1,0:T(8,128)(2,1)}, u32[]{:S(2)}) copy-start(bf16[1280,640]{1,0:T(8,128)(2,1)} %param.6) | copy-start | bytes 4915204
  7.2 186.3 %all-reduce.5.cloned.1.call-start = ((), (), s32[]{:S(2)}) async-start(), calls=%async_computation | async-start | bytes 5242880 | tf_op jit(solution)/shard_map/psum | solution.py:30
  114.2 0.8 copy-start.1
  115.0 4.7 copy-start.3
  115.0 4.7 copy-start.4
  115.0 4.8 copy-start.5
  482.7 1.2 copy-start.2
Sparse Core Ops, SparseCore 0:
  118.0 75.4 all-reduce.4
where the time goes:
time: 788 us; the launch traced here: 787 us
  blocking collectives  681 us (86%)
  waiting for transfers between devices  73.6 us (9%)
  between operations  14.8 us (2%)
    psum x2, blocking collectives, row_statistics(): lax.psum((jnp.sum(jnp.exp(logits - top[:, None]), axis=1), picked_local),...  430 us
    pmax x1, blocking collectives, row_statistics(): top = lax.pmax(local_top, 'vocab')  144 us
    all_gather x1, blocking collectives, shards(): hidden_all = lax.all_gather(hidden_states, 'vocab', axis=0, tiled=True)  107 us
    psum x1, waiting for transfers between devices, shards(): logits = lax.psum(partial_logits, 'width')  73.6 us
  transfers between devices with their start and end apart: 1, of which 1 were waited for; matrix products, arithmetic and copies ran while one was open for 0% of the time, Pallas kernels for 0%

commit v1 on v0

v1 whole, which is shorter than its diff:
```python
import jax
import jax.numpy as jnp
from jax import lax
from jax.sharding import Mesh, PartitionSpec as P

discount = 0.99
f32 = jnp.float32
bf16 = jnp.bfloat16


def three_parts(value):
    high = lax.reduce_precision(value, 8, 7)
    rest = value - high
    middle = lax.reduce_precision(rest, 8, 7)
    return [high, middle, rest - middle]


def shards(hidden_states, head_weight, targets, terminal, cotangent):
    rows = head_weight.shape[0]
    tokens = targets.shape[0]
    sz = {a: lax.axis_size(a) for a in ("x", "z", "y", "c")}
    n_width = sz["y"] * sz["c"]
    n_vocab = sz["x"] * sz["z"]
    own = tokens // n_width
    half = tokens // sz["c"]
    x, z, y, c = (lax.axis_index(a) for a in ("x", "z", "y", "c"))
    first_row = (x * sz["z"] + z) * rows
    first_token = (c * sz["y"] + y) * own

    keep = discount * (1.0 - terminal.astype(f32))
    carried = jnp.concatenate([jnp.zeros((1,), f32), (keep * cotangent)[:-1]])

    with jax.named_scope("gather_hidden"):
        hidden = lax.all_gather(hidden_states, "z", axis=0, tiled=True)
        hidden = lax.all_gather(hidden, "x", axis=0, tiled=True)

    with jax.named_scope("logits"):
        partial = lax.dot_general(
            hidden, head_weight, (((1,), (1,)), ((), ())), preferred_element_type=f32
        ).astype(jnp.float16)
        pieces = lax.all_to_all(
            partial.reshape(n_width, own, rows), ("c", "y"), 0, 0, tiled=True
        )
        logits = jnp.sum(pieces.astype(f32), axis=0)

    with jax.named_scope("statistics"):
        cut = lambda v: lax.dynamic_slice(v, (first_token,), (own,))
        hit = (cut(targets) - first_row)[:, None] == jnp.arange(rows, dtype=jnp.int32)
        top = jnp.max(logits, axis=1)
        total = jnp.sum(jnp.exp(logits - top[:, None]), axis=1)
        picked = jnp.sum(jnp.where(hit, logits, 0.0), axis=1)
        mine = jnp.concatenate([top, total, picked, jnp.zeros((own,), f32)])
        every = lax.all_to_all(
            jnp.broadcast_to(mine, (n_vocab, 4 * own)), ("z", "x"), 0, 0, tiled=True
        ).reshape(n_vocab, 4, own)
        top_all = jnp.max(every[:, 0], axis=0)
        total_all = jnp.sum(every[:, 1] * jnp.exp(every[:, 0] - top_all), axis=0)
        lse = top_all + jnp.log(total_all)
        picked = jnp.sum(every[:, 2], axis=0)

    with jax.named_scope("gather_dlogits"):
        dlogits = jnp.where(hit, cut(cotangent)[:, None], 0.0) - cut(carried)[
            :, None
        ] * jnp.exp(logits - lse[:, None])
        extra = jnp.stack(three_parts(lse) + three_parts(picked), axis=1)
        extra = jnp.pad(extra, ((0, 0), (0, 128 - extra.shape[1])))
        sent = jnp.concatenate([dlogits.astype(bf16), extra.astype(bf16)], axis=1)
        near = lax.all_gather(sent, "y", axis=0, tiled=True)
        far = lax.ppermute(near, "c", [(0, 1), (1, 0)])

    with jax.named_scope("products"):
        is_low = c == 0
        outer = (((0,), (0,)), ((), ()))
        low_h, high_h = hidden[:half], hidden[half:]
        near_h = jnp.where(is_low, low_h, high_h)
        far_h = jnp.where(is_low, high_h, low_h)
        near_d, far_d = near[:, :rows], far[:, :rows]
        near_g = jnp.dot(near_d, head_weight, preferred_element_type=f32).astype(bf16)
        far_g = jnp.dot(far_d, head_weight, preferred_element_type=f32).astype(bf16)
        weight_grad = (
            lax.dot_general(near_d, near_h, outer, preferred_element_type=f32)
            + lax.dot_general(far_d, far_h, outer, preferred_element_type=f32)
        ).astype(bf16)
        grad = jnp.concatenate(
            [jnp.where(is_low, near_g, far_g), jnp.where(is_low, far_g, near_g)]
        )

    with jax.named_scope("scatter_hidden_grad"):
        width = grad.shape[1]
        grad = lax.all_to_all(
            grad.reshape(sz["x"], tokens // sz["x"], width), "x", 0, 0, tiled=True
        )
        grad = jnp.sum(grad.astype(f32), axis=0).astype(bf16)
        grad = lax.all_to_all(
            grad.reshape(sz["z"], tokens // n_vocab, width), "z", 0, 0, tiled=True
        )
        hidden_grad = jnp.sum(grad.astype(f32), axis=0).astype(bf16)

    with jax.named_scope("rewards"):
        near_s = near[:, rows : rows + 8].astype(f32)
        far_s = far[:, rows : rows + 8].astype(f32)
        stats = jnp.concatenate(
            [jnp.where(is_low, near_s, far_s), jnp.where(is_low, far_s, near_s)]
        )
        lse_all = stats[:, 0] + stats[:, 1] + stats[:, 2]
        picked_all = stats[:, 3] + stats[:, 4] + stats[:, 5]
        next_value = jnp.concatenate([lse_all[1:], jnp.zeros((1,), f32)])
        rewards = picked_all - keep * next_value
    return (rewards, hidden_grad, weight_grad)


def solution(mesh):
    fine = Mesh(mesh.devices.reshape(4, 16, 4, 2), ("x", "z", "y", "c"))
    block = P(("x", "z"), ("y", "c"))
    return jax.shard_map(
        shards,
        mesh=fine,
        in_specs=(block, block, P(), P(), P()),
        out_specs=(P(), block, block),
        check_vma=False,
    )
```

time: 788 us -> 161 us (0.20)
  blocking collectives: 681 us -> 64.1 us
  starting transfers between devices: 0.04 us -> 23.9 us
  waiting for transfers between devices: 73.6 us -> 51 us
  between operations: 14.8 us -> 0.8 us
    psum x2 -> x0, blocking collectives: 430 us -> none  [row_statistics(): lax.psum((jnp.sum(jnp.exp(logits - top[:, None]), axis=1), picked_local),...]
    pmax x1 -> x0, blocking collectives: 144 us -> none  [row_statistics(): top = lax.pmax(local_top, 'vocab')]
    psum x1 -> x0, waiting for transfers between devices: 73.6 us -> none  [shards(): logits = lax.psum(partial_logits, 'width')]
    all_to_all x0 -> x4, waiting for transfers between devices: none -> 49.5 us  [the longest x1 15.9 us: shards(): lax.all_to_all(partial.reshape(n_width, own, rows), ('c', 'y'), 0, 0, til...]
    all_gather x1 -> x3, blocking collectives: 107 us -> 64.1 us  [the longest x1 36.6 us: shards(): hidden = lax.all_gather(hidden_states, 'z', axis=0, tiled=True)]
    all_to_all x0 -> x4, starting transfers between devices: none -> 22 us  [the longest x1 9.5 us: shards(): lax.all_to_all(jnp.broadcast_to(mine, (n_vocab, 4 * own)), ('z', 'x'), 0,...]
  transfers between devices with their start and end apart: 1 -> 5, of which waited for: 1 -> 5; matrix products, arithmetic and copies ran while one was open for 0% -> 6% of each run, Pallas kernels for 0% -> 0%
where the time goes in v1:
time: 161 us; the launch traced here: 159 us
  blocking collectives  64.1 us (40%)
  waiting for transfers between devices  51 us (32%)
  starting transfers between devices  23.9 us (15%)
  matrix products  11.2 us (7%)
  other arithmetic  6.94 us (4%)
    all_gather x1, blocking collectives, shards(): hidden = lax.all_gather(hidden_states, 'z', axis=0, tiled=True)  36.6 us
    all_to_all x1, waiting for transfers between devices, shards(): lax.all_to_all(partial.reshape(n_width, own, rows), ('c', 'y'), 0, 0, til...  15.9 us
    all_to_all x1, waiting for transfers between devices, shards(): lax.all_to_all(jnp.broadcast_to(mine, (n_vocab, 4 * own)), ('z', 'x'), 0,...  15 us
    all_gather x1, blocking collectives, shards(): near = lax.all_gather(sent, 'y', axis=0, tiled=True)  14.1 us
    all_gather x1, blocking collectives, shards(): hidden = lax.all_gather(hidden, 'x', axis=0, tiled=True)  13.4 us
    all_to_all x1, waiting for transfers between devices, shards(): lax.all_to_all(grad.reshape(sz['z'], tokens // n_vocab, width), 'z', 0, 0...  10.5 us
    all_to_all x1, starting transfers between devices, shards(): lax.all_to_all(jnp.broadcast_to(mine, (n_vocab, 4 * own)), ('z', 'x'), 0,...  9.5 us
    all_to_all x1, waiting for transfers between devices, shards(): lax.all_to_all(grad.reshape(sz['x'], tokens // sz['x'], width), 'x', 0, 0...  8.09 us
  transfers between devices with their start and end apart: 5, of which 5 were waited for; matrix products, arithmetic and copies ran while one was open for 6% of the time, Pallas kernels for 0%

profile of v1, /device:TPU:24, one launch (start us, length us, event | category | flops | bytes accessed | tf_op | source)
XLA Modules:
  0.0 159.3 jit_solution(15321067315414500774)
XLA Ops:
  0.6 36.6 %all_gather.9 = bf16[128,640]{1,0:T(8,128)(2,1)S(1)} all-gather(bf16[8,640]{1,0:T(8,128)(2,1)} %param.5), channel_id=1, replica_groups=mesh['x'=4,'z'=16,'y'=4,'c'=2] {'z'}, dimensions={0}, use_global_device_ids=true | all-gather | bytes 174080 | tf_op jit(solution)/shard_map/gather_hidden/all_gather | solution.py:34
  37.3 13.4 %all_gather.10 = bf16[512,640]{1,0:T(8,128)(2,1)S(1)} all-gather(bf16[128,640]{1,0:T(8,128)(2,1)S(1)} %all_gather.9), channel_id=1, replica_groups=mesh['x'=4,'z'=16,'y'=4,'c'=2] {'x'}, dimensions={0}, use_global_device_ids=true | all-gather | bytes 819200 | tf_op jit(solution)/shard_map/gather_hidden/all_gather | solution.py:35
  50.7 2.3 %convolution_convert_fusion = f16[512,1280]{1,0:T(8,128)(2,1)} fusion(bf16[512,640]{1,0:T(8,128)(2,1)S(1)} %all_gather.10, bf16[1280,640]{1,0:T(8,128)(2,1)S(1)} %copy-done), kind=kOutput, calls=%fused_computation.2 | convolution fusion | flops 839516160 | bytes 3604480 | tf_op jit(solution)/shard_map/logits/dot_general | solution.py:38
  53.0 4.8 %all-to-all-start = ((f16[8,64,1280]{2,1,0:T(8,128)(2,1)}), f16[8,64,1280]{2,1,0:T(8,128)(2,1)S(1)}, u32[]{:S(2)}, u32[]{:S(2)}) async-start(f16[8,64,1280]{2,1,0:T(8,128)(2,1)} %bitcast.30), calls=%async_computation | async-start | bytes 2621440 | tf_op jit(solution)/shard_map/logits/all_to_all | solution.py:41
  57.9 0.8 dynamic-slice_subtract_fusion
  58.6 15.9 %all-to-all-done = f16[8,64,1280]{2,1,0:T(8,128)(2,1)S(1)} async-done(((f16[8,64,1280]{2,1,0:T(8,128)(2,1)}), f16[8,64,1280]{2,1,0:T(8,128)(2,1)S(1)}, u32[]{:S(2)}, u32[]{:S(2)}) %all-to-all-start) | async-done | bytes 1310752 | tf_op jit(solution)/shard_map/logits/all_to_all | solution.py:41
  74.5 0.2 convert_reduce_fusion
  74.7 0.1 reduce_max.18
  74.8 0.2 exponential_reduce_fusion
  75.1 0.7 broadcast_in_dim.30
  75.8 9.5 %all-to-all-start.1 = ((f32[64,1,256]{2,1,0:T(1,128)}), f32[64,1,256]{2,1,0:T(1,128)S(1)}, u32[]{:S(2)}, u32[]{:S(2)}) async-start(f32[64,1,256]{2,1,0:T(1,128)} %broadcast_in_dim.30), calls=%async_computation.1 | async-start | bytes 131072 | tf_op jit(solution)/shard_map/statistics/all_to_all | solution.py:53
  85.5 15.0 %all-to-all-done.1 = f32[64,1,256]{2,1,0:T(1,128)S(1)} async-done(((f32[64,1,256]{2,1,0:T(1,128)}), f32[64,1,256]{2,1,0:T(1,128)S(1)}, u32[]{:S(2)}, u32[]{:S(2)}) %all-to-all-start.1) | async-done | bytes 65568 | tf_op jit(solution)/shard_map/statistics/all_to_all | solution.py:53
  100.5 0.2 reduce.4
  100.7 0.1 reshape.106
  101.0 0.1 copy.30
  101.2 0.2 subtract_convert_fusion
  101.4 14.1 %all_gather.11 = bf16[256,1408]{1,0:T(8,128)(2,1)S(1)} all-gather(bf16[64,1408]{1,0:T(8,128)(2,1)S(1)} %fusion.15), channel_id=1, replica_groups=mesh['x'=4,'z'=16,'y'=4,'c'=2] {'y'}, dimensions={0}, use_global_device_ids=true | all-gather | bytes 901120 | tf_op jit(solution)/shard_map/gather_dlogits/all_gather | solution.py:68
  115.4 1.9 %collective-permute-start = (bf16[256,1408]{1,0:T(8,128)(2,1)S(1)}, bf16[256,1408]{1,0:T(8,128)(2,1)}, u32[]{:S(2)}, u32[]{:S(2)}) collective-permute-start(bf16[256,1408]{1,0:T(8,128)(2,1)S(1)} %all_gather.11), channel_id=1, source_target_pairs={{0,1},{1,0},{2,3},{3,2},{4,5},{5,4},{6,7},{7,6},{8,9},{9,8},{10,11... | collective-permute-start | bytes 2162696 | tf_op jit(solution)/shard_map/gather_dlogits/ppermute | solution.py:69
  117.4 0.7 convolution_convert_fusion.2
  118.0 1.6 %collective-permute-done = bf16[256,1408]{1,0:T(8,128)(2,1)} collective-permute-done((bf16[256,1408]{1,0:T(8,128)(2,1)S(1)}, bf16[256,1408]{1,0:T(8,128)(2,1)}, u32[]{:S(2)}, u32[]{:S(2)}) %collective-permute-start) | collective-permute-done | bytes 720928 | tf_op jit(solution)/shard_map/gather_dlogits/ppermute | solution.py:69
  119.6 1.8 %broadcast_select_fusion.1 = (bf16[256,640]{1,0:T(8,128)(2,1)S(1)}, bf16[256,640]{1,0:T(8,128)(2,1)S(1)}) fusion(bf16[256,640]{1,0:T(8,128)(2,1)S(1)} %convolution_convert_fusion.2, pred[]{:T(512)S(6)} %eq.16, bf16[1280,640]{1,0:T(8,128)(2,1)S(1)} %copy-done, bf16[256,1408]{1,0:T(8,128)(2,1)} %collective-permute-done), kind=kOutput, calls=%fused_computation.23 | convolution fusion | flops 419921920 | bytes 3276801 | tf_op jit(solution)/shard_map/products/dot_general | solution.py:79
  121.4 0.9 pad_maximum_fusion
  122.3 4.2 %all-to-all-start.2 = ((bf16[4,128,640]{2,1,0:T(8,128)(2,1)}), bf16[4,128,640]{2,1,0:T(8,128)(2,1)}, u32[]{:S(2)}, u32[]{:S(2)}) async-start(bf16[4,128,640]{2,1,0:T(8,128)(2,1)} %bitcast.29), calls=%async_computation.2 | async-start | bytes 1310720 | tf_op jit(solution)/shard_map/scatter_hidden_grad/all_to_all | solution.py:90
  126.5 2.4 %fusion.3 = f32[1280,640]{1,0:T(8,128)} fusion(bf16[256,1408]{1,0:T(8,128)(2,1)S(1)} %all_gather.11, pred[]{:T(512)S(6)} %eq.16, bf16[512,640]{1,0:T(8,128)(2,1)S(1)} %copy-done.2), kind=kOutput, calls=%fused_computation.9 | convolution fusion | flops 419594240 | bytes 4587521 | tf_op jit(solution)/shard_map/products/dot_general | solution.py:81
  128.9 0.9 convert_select_fusion.1
  129.9 8.1 %all-to-all-done.2 = bf16[4,128,640]{2,1,0:T(8,128)(2,1)} async-done(((bf16[4,128,640]{2,1,0:T(8,128)(2,1)}), bf16[4,128,640]{2,1,0:T(8,128)(2,1)}, u32[]{:S(2)}, u32[]{:S(2)}) %all-to-all-start.2) | async-done | bytes 655392 | tf_op jit(solution)/shard_map/scatter_hidden_grad/all_to_all | solution.py:90
  138.0 1.9 %reduce_sum.77 = bf16[128,640]{1,0:T(8,128)(2,1)} reduce(bf16[4,128,640]{2,1,0:T(8,128)(2,1)} %all-to-all-done.2, bf16[]{:T(256)} %constant.44.clone.1), dimensions={0}, to_apply=%region_7.8 | reduce | flops 245760 | bytes 819202 | tf_op jit(solution)/shard_map/scatter_hidden_grad/reduce_sum | solution.py:93
  139.9 3.5 %all-to-all-start.3 = ((bf16[16,8,640]{2,1,0:T(8,128)(2,1)}), bf16[16,8,640]{2,1,0:T(8,128)(2,1)S(1)}, u32[]{:S(2)}, u32[]{:S(2)}) async-start(bf16[16,8,640]{2,1,0:T(8,128)(2,1)} %bitcast.9), calls=%async_computation.3 | async-start | bytes 327680 | tf_op jit(solution)/shard_map/scatter_hidden_grad/all_to_all | solution.py:94
  143.5 0.7 fusion.18
  144.2 4.0 %fusion = bf16[1280,640]{1,0:T(8,128)(2,1)} fusion(f32[1280,640]{1,0:T(8,128)} %fusion.3, bf16[256,1408]{1,0:T(8,128)(2,1)} %collective-permute-done, pred[]{:T(512)S(6)} %eq.16, bf16[512,640]{1,0:T(8,128)(2,1)S(1)} %copy-done.2), kind=kOutput, calls=%fused_computation.1 | convolution fusion | flops 421232640 | bytes 6225921 | tf_op jit(solution)/shard_map/products/dot_general | solution.py:82
  148.2 10.5 %all-to-all-done.3 = bf16[16,8,640]{2,1,0:T(8,128)(2,1)S(1)} async-done(((bf16[16,8,640]{2,1,0:T(8,128)(2,1)}), bf16[16,8,640]{2,1,0:T(8,128)(2,1)S(1)}, u32[]{:S(2)}, u32[]{:S(2)}) %all-to-all-start.3) | async-done | bytes 163872 | tf_op jit(solution)/shard_map/scatter_hidden_grad/all_to_all | solution.py:94
  158.7 0.6 reduce_sum.78
  (28 shorter events, 0.8 us)
Async XLA Ops:
  0.6 50.0 %copy-start = (bf16[1280,640]{1,0:T(8,128)(2,1)S(1)}, bf16[1280,640]{1,0:T(8,128)(2,1)}, u32[]{:S(2)}) copy-start(bf16[1280,640]{1,0:T(8,128)(2,1)} %param.6) | copy-start | bytes 4915204
  50.7 2.3 %copy-start.1 = (bf16[512,640]{1,0:T(8,128)(2,1)}, bf16[512,640]{1,0:T(8,128)(2,1)S(1)}, u32[]{:S(2)}) copy-start(bf16[512,640]{1,0:T(8,128)(2,1)S(1)} %all_gather.10) | copy-start | bytes 1966084
  53.0 4.8 %copy-start.4 = (f32[512]{0:T(512)S(1)}, f32[512]{0:T(512)}, u32[]{:S(2)}) copy-start(f32[512]{0:T(512)} %param.9) | copy-start | bytes 6148
  53.0 21.5 %all-to-all-start = ((f16[8,64,1280]{2,1,0:T(8,128)(2,1)}), f16[8,64,1280]{2,1,0:T(8,128)(2,1)S(1)}, u32[]{:S(2)}, u32[]{:S(2)}) async-start(f16[8,64,1280]{2,1,0:T(8,128)(2,1)} %bitcast.30), calls=%async_computation | async-start | bytes 2621440 | tf_op jit(solution)/shard_map/logits/all_to_all | solution.py:41
  57.8 27.5 %copy-start.3 = (s32[512]{0:T(512)S(1)}, s32[512]{0:T(512)}, u32[]{:S(2)}) copy-start(s32[512]{0:T(512)} %param.8) | copy-start | bytes 6148
  75.8 24.7 %all-to-all-start.1 = ((f32[64,1,256]{2,1,0:T(1,128)}), f32[64,1,256]{2,1,0:T(1,128)S(1)}, u32[]{:S(2)}, u32[]{:S(2)}) async-start(f32[64,1,256]{2,1,0:T(1,128)} %broadcast_in_dim.30), calls=%async_computation.1 | async-start | bytes 131072 | tf_op jit(solution)/shard_map/statistics/all_to_all | solution.py:53
  115.4 4.2 %collective-permute-start = (bf16[256,1408]{1,0:T(8,128)(2,1)S(1)}, bf16[256,1408]{1,0:T(8,128)(2,1)}, u32[]{:S(2)}, u32[]{:S(2)}) collective-permute-start(bf16[256,1408]{1,0:T(8,128)(2,1)S(1)} %all_gather.11), channel_id=1, source_target_pairs={{0,1},{1,0},{2,3},{3,2},{4,5},{5,4},{6,7},{7,6},{8,9},{9,8},{10,11... | collective-permute-start | bytes 2162696 | tf_op jit(solution)/shard_map/gather_dlogits/ppermute | solution.py:69
  121.4 5.1 %copy-start.2 = (bf16[512,640]{1,0:T(8,128)(2,1)S(1)}, bf16[512,640]{1,0:T(8,128)(2,1)}, u32[]{:S(2)}) copy-start(bf16[512,640]{1,0:T(8,128)(2,1)} %copy-done.1) | copy-start | bytes 1966084
  122.3 15.7 %all-to-all-start.2 = ((bf16[4,128,640]{2,1,0:T(8,128)(2,1)}), bf16[4,128,640]{2,1,0:T(8,128)(2,1)}, u32[]{:S(2)}, u32[]{:S(2)}) async-start(bf16[4,128,640]{2,1,0:T(8,128)(2,1)} %bitcast.29), calls=%async_computation.2 | async-start | bytes 1310720 | tf_op jit(solution)/shard_map/scatter_hidden_grad/all_to_all | solution.py:90
  139.9 18.7 %all-to-all-start.3 = ((bf16[16,8,640]{2,1,0:T(8,128)(2,1)}), bf16[16,8,640]{2,1,0:T(8,128)(2,1)S(1)}, u32[]{:S(2)}, u32[]{:S(2)}) async-start(bf16[16,8,640]{2,1,0:T(8,128)(2,1)} %bitcast.9), calls=%async_computation.3 | async-start | bytes 327680 | tf_op jit(solution)/shard_map/scatter_hidden_grad/all_to_all | solution.py:94

commit v2 on v1

--- a/solution.py
+++ b/solution.py
@@ -6,6 +6,7 @@
 discount = 0.99
 f32 = jnp.float32
 bf16 = jnp.bfloat16
+f16 = jnp.float16
 
 
 def three_parts(value):
@@ -13,6 +14,12 @@
     rest = value - high
     middle = lax.reduce_precision(rest, 8, 7)
     return [high, middle, rest - middle]
+
+
+def spread(block, axis):
+    copies = jnp.broadcast_to(block, (lax.axis_size(axis), *block.shape))
+    copies = lax.all_to_all(copies, axis, 0, 0, tiled=True)
+    return copies.reshape(-1, block.shape[-1])
 
 
 def shards(hidden_states, head_weight, targets, terminal, cotangent):
@@ -31,16 +38,19 @@
     carried = jnp.concatenate([jnp.zeros((1,), f32), (keep * cotangent)[:-1]])
 
     with jax.named_scope("gather_hidden"):
-        hidden = lax.all_gather(hidden_states, "z", axis=0, tiled=True)
-        hidden = lax.all_gather(hidden, "x", axis=0, tiled=True)
+        hidden = spread(spread(hidden_states, "z"), "x")
+        hidden = hidden.reshape(tokens, hidden.shape[-1])
 
     with jax.named_scope("logits"):
-        partial = lax.dot_general(
-            hidden, head_weight, (((1,), (1,)), ((), ())), preferred_element_type=f32
-        ).astype(jnp.float16)
-        pieces = lax.all_to_all(
-            partial.reshape(n_width, own, rows), ("c", "y"), 0, 0, tiled=True
-        )
+        is_low = c == 0
+        near_h = lax.dynamic_slice_in_dim(hidden, c * half, half)
+        far_h = lax.dynamic_slice_in_dim(hidden, (1 - c) * half, half)
+        inner = (((1,), (1,)), ((), ()))
+        far_l = lax.dot_general(far_h, head_weight, inner, preferred_element_type=f32)
+        far_l = lax.ppermute(far_l.astype(f16), "c", [(0, 1), (1, 0)])
+        near_l = lax.dot_general(near_h, head_weight, inner, preferred_element_type=f32)
+        chip_l = (near_l + far_l.astype(f32)).astype(f16)
+        pieces = lax.all_to_all(chip_l.reshape(sz["y"], own, rows), "y", 0, 0, tiled=True)
         logits = jnp.sum(pieces.astype(f32), axis=0)
 
     with jax.named_scope("statistics"):
@@ -49,14 +59,13 @@
         top = jnp.max(logits, axis=1)
         total = jnp.sum(jnp.exp(logits - top[:, None]), axis=1)
         picked = jnp.sum(jnp.where(hit, logits, 0.0), axis=1)
-        mine = jnp.concatenate([top, total, picked, jnp.zeros((own,), f32)])
+        mine = jnp.concatenate([top + jnp.log(total), picked])
         every = lax.all_to_all(
-            jnp.broadcast_to(mine, (n_vocab, 4 * own)), ("z", "x"), 0, 0, tiled=True
-        ).reshape(n_vocab, 4, own)
-        top_all = jnp.max(every[:, 0], axis=0)
-        total_all = jnp.sum(every[:, 1] * jnp.exp(every[:, 0] - top_all), axis=0)
-        lse = top_all + jnp.log(total_all)
-        picked = jnp.sum(every[:, 2], axis=0)
+            jnp.broadcast_to(mine, (n_vocab, 2 * own)), ("z", "x"), 0, 0, tiled=True
+        )
+        top = jnp.max(every[:, :own], axis=0)
+        lse = top + jnp.log(jnp.sum(jnp.exp(every[:, :own] - top), axis=0))
+        picked = jnp.sum(every[:, own:], axis=0)
 
     with jax.named_scope("gather_dlogits"):
         dlogits = jnp.where(hit, cut(cotangent)[:, None], 0.0) - cut(carried)[
@@ -69,14 +78,10 @@
         far = lax.ppermute(near, "c", [(0, 1), (1, 0)])
 
     with jax.named_scope("products"):
-        is_low = c == 0
         outer = (((0,), (0,)), ((), ()))
-        low_h, high_h = hidden[:half], hidden[half:]
-        near_h = jnp.where(is_low, low_h, high_h)
-        far_h = jnp.where(is_low, high_h, low_h)
         near_d, far_d = near[:, :rows], far[:, :rows]
-        near_g = jnp.dot(near_d, head_weight, preferred_element_type=f32).astype(bf16)
-        far_g = jnp.dot(far_d, head_weight, preferred_element_type=f32).astype(bf16)
+        near_g = jnp.dot(near_d, head_weight, preferred_element_type=f32).astype(f16)
+        far_g = jnp.dot(far_d, head_weight, preferred_element_type=f32).astype(f16)
         weight_grad = (
             lax.dot_general(near_d, near_h, outer, preferred_element_type=f32)
             + lax.dot_general(far_d, far_h, outer, preferred_element_type=f32)
@@ -90,7 +95,7 @@
         grad = lax.all_to_all(
             grad.reshape(sz["x"], tokens // sz["x"], width), "x", 0, 0, tiled=True
         )
-        grad = jnp.sum(grad.astype(f32), axis=0).astype(bf16)
+        grad = jnp.sum(grad.astype(f32), axis=0).astype(f16)
         grad = lax.all_to_all(
             grad.reshape(sz["z"], tokens // n_vocab, width), "z", 0, 0, tiled=True
         )

time: 161 us -> 151 us (0.938)
  blocking collectives: 64.1 us -> 44.3 us
  starting transfers between devices: 23.9 us -> 28.5 us
  waiting for transfers between devices: 51 us -> 53.9 us
    all_gather x2 -> x0, blocking collectives: 50 us -> none  [the longest x1 36.6 us: shards(): hidden = lax.all_gather(hidden_states, 'z', axis=0, tiled=True)]
    all_to_all x0 -> x1, blocking collectives: none -> 30.6 us  [spread(): copies = lax.all_to_all(copies, axis, 0, 0, tiled=True)]
    all_to_all x2 -> x3, starting transfers between devices: 14.3 us -> 17 us  [the longest x1 7.9 us: shards(): lax.all_to_all(jnp.broadcast_to(mine, (n_vocab, 2 * own)), ('z', 'x'), 0,...]
    ppermute x0 -> x1, waiting for transfers between devices: none -> 2.27 us  [shards(): far_l = lax.ppermute(far_l.astype(f16), 'c', [(0, 1), (1, 0)])]
    ppermute x0 -> x1, starting transfers between devices: none -> 1.91 us  [shards(): far_l = lax.ppermute(far_l.astype(f16), 'c', [(0, 1), (1, 0)])]
    broadcast_in_dim x2 -> x3, local copies, waits for them, and re-layouts: 0.67 us -> 2.37 us  [the longest x2 1.73 us: spread(): copies = jnp.broadcast_to(block, (lax.axis_size(axis), *block.shape))]
    dot_general x3 -> x4, matrix products: 4.74 us -> 5.55 us  [the longest x1 1.77 us: shards(): far_g = jnp.dot(far_d, head_weight, preferred_element_type=f32).astype(f16)]
    all_to_all x2 -> x3, waiting for transfers between devices: 30.9 us -> 31.5 us  [the longest x1 14.3 us: shards(): lax.all_to_all(jnp.broadcast_to(mine, (n_vocab, 2 * own)), ('z', 'x'), 0,...]
  transfers between devices with their start and end apart: 5 -> 7, of which waited for: 5 -> 7; matrix products, arithmetic and copies ran while one was open for 6% -> 7% of each run, Pallas kernels for 0% -> 0%
where the time goes in v2:
time: 151 us; the launch traced here: 149 us
  waiting for transfers between devices  53.9 us (36%)
  blocking collectives  44.3 us (29%)
  starting transfers between devices  28.5 us (19%)
  matrix products  12 us (8%)
  other arithmetic  6.84 us (5%)
  local copies, waits for them, and re-layouts  2.82 us (2%)
    all_to_all x1, blocking collectives, spread(): copies = lax.all_to_all(copies, axis, 0, 0, tiled=True)  30.6 us
    all_to_all x1, waiting for transfers between devices, shards(): lax.all_to_all(jnp.broadcast_to(mine, (n_vocab, 2 * own)), ('z', 'x'), 0,...  14.3 us
    all_gather x1, blocking collectives, shards(): near = lax.all_gather(sent, 'y', axis=0, tiled=True)  13.7 us
    all_to_all x1, waiting for transfers between devices, shards(): lax.all_to_all(grad.reshape(sz['z'], tokens // n_vocab, width), 'z', 0, 0...  10.5 us
    all_to_all x1, waiting for transfers between devices, spread(): copies = lax.all_to_all(copies, axis, 0, 0, tiled=True)  8.79 us
    all_to_all x1, waiting for transfers between devices, shards(): lax.all_to_all(chip_l.reshape(sz['y'], own, rows), 'y', 0, 0, tiled=True)  8.37 us
    all_to_all x1, waiting for transfers between devices, shards(): lax.all_to_all(grad.reshape(sz['x'], tokens // sz['x'], width), 'x', 0, 0...  8.1 us
    all_to_all x1, starting transfers between devices, shards(): lax.all_to_all(jnp.broadcast_to(mine, (n_vocab, 2 * own)), ('z', 'x'), 0,...  7.9 us
  transfers between devices with their start and end apart: 7, of which 7 were waited for; matrix products, arithmetic and copies ran while one was open for 7% of the time, Pallas kernels for 0%

profile of v2, /device:TPU:24, one launch (start us, length us, event | category | flops | bytes accessed | tf_op | source)
XLA Modules:
  0.0 149.1 jit_solution(7604766966299506193)
XLA Ops:
  0.6 0.8 broadcast_in_dim.32
  1.5 30.6 %all_to_all.34 = bf16[16,8,640]{2,1,0:T(8,128)(2,1)S(1)} all-to-all(bf16[16,8,640]{2,1,0:T(8,128)(2,1)S(1)} %broadcast_in_dim.32), channel_id=1, replica_groups=mesh['x'=4,'z'=16,'y'=4,'c'=2] {'z'}, dimensions={0} | all-to-all | bytes 327680 | tf_op jit(solution)/shard_map/gather_hidden/all_to_all | solution.py:21
  32.1 0.9 broadcast_in_dim.33
  33.0 4.3 %all-to-all-start.1 = ((bf16[4,128,640]{2,1,0:T(8,128)(2,1)}), bf16[4,128,640]{2,1,0:T(8,128)(2,1)S(1)}, u32[]{:S(2)}, u32[]{:S(2)}) async-start(bf16[4,128,640]{2,1,0:T(8,128)(2,1)} %broadcast_in_dim.33), calls=%async_computation.1 | async-start | bytes 1310720 | tf_op jit(solution)/shard_map/gather_hidden/all_to_all | solution.py:21
  37.3 8.8 %all-to-all-done.1 = bf16[4,128,640]{2,1,0:T(8,128)(2,1)S(1)} async-done(((bf16[4,128,640]{2,1,0:T(8,128)(2,1)}), bf16[4,128,640]{2,1,0:T(8,128)(2,1)S(1)}, u32[]{:S(2)}, u32[]{:S(2)}) %all-to-all-start.1) | async-done | bytes 655392 | tf_op jit(solution)/shard_map/gather_hidden/all_to_all | solution.py:21
  46.1 1.5 %convolution_convert_fusion = f16[256,1280]{1,0:T(8,128)(2,1)} fusion(bf16[1280,640]{1,0:T(8,128)(2,1)S(1)} %copy-done, bf16[512,640]{1,0:T(8,128)(2,1)S(1)} %bitcast.28, s32[]{:T(128)S(6)} %select_n.47), kind=kOutput, calls=%fused_computation.2 | convolution fusion | flops 419758080 | bytes 2621444 | tf_op jit(solution)/shard_map/logits/dot_general | solution.py:49
  47.6 1.9 %collective-permute-start = (f16[256,1280]{1,0:T(8,128)(2,1)}, f16[256,1280]{1,0:T(8,128)(2,1)S(1)}, u32[]{:S(2)}, u32[]{:S(2)}) collective-permute-start(f16[256,1280]{1,0:T(8,128)(2,1)} %convolution_convert_fusion), channel_id=1, source_target_pairs={{0,1},{1,0},{2,3},{3,2},{4,5},{5,4},{6,7},{7,6},{8,9},{9,8},{10,11... | collective-permute-start | bytes 1966088 | tf_op jit(solution)/shard_map/logits/ppermute | solution.py:50
  49.6 2.3 %collective-permute-done = f16[256,1280]{1,0:T(8,128)(2,1)S(1)} collective-permute-done((f16[256,1280]{1,0:T(8,128)(2,1)}, f16[256,1280]{1,0:T(8,128)(2,1)S(1)}, u32[]{:S(2)}, u32[]{:S(2)}) %collective-permute-start) | collective-permute-done | bytes 655392 | tf_op jit(solution)/shard_map/logits/ppermute | solution.py:50
  51.8 1.5 %add_convert_fusion = f16[256,1280]{1,0:T(8,128)(2,1)} fusion(f16[256,1280]{1,0:T(8,128)(2,1)S(1)} %collective-permute-done, bf16[1280,640]{1,0:T(8,128)(2,1)S(1)} %copy-done, bf16[512,640]{1,0:T(8,128)(2,1)S(1)} %bitcast.29, s32[]{:T(128)S(6)} %select_n.46), kind=kOutput, calls=%fused_computation.5 | convolution fusion | flops 420413440 | bytes 3276804 | tf_op jit(solution)/shard_map/logits/dot_general | solution.py:51
  53.4 4.8 %all-to-all-start.2 = ((f16[4,64,1280]{2,1,0:T(8,128)(2,1)}), f16[4,64,1280]{2,1,0:T(8,128)(2,1)S(1)}, u32[]{:S(2)}, u32[]{:S(2)}) async-start(f16[4,64,1280]{2,1,0:T(8,128)(2,1)} %bitcast.33), calls=%async_computation.2 | async-start | bytes 1310720 | tf_op jit(solution)/shard_map/logits/all_to_all | solution.py:53
  58.2 0.8 dynamic-slice_subtract_fusion
  58.9 8.4 %all-to-all-done.2 = f16[4,64,1280]{2,1,0:T(8,128)(2,1)S(1)} async-done(((f16[4,64,1280]{2,1,0:T(8,128)(2,1)}), f16[4,64,1280]{2,1,0:T(8,128)(2,1)S(1)}, u32[]{:S(2)}, u32[]{:S(2)}) %all-to-all-start.2) | async-done | bytes 655392 | tf_op jit(solution)/shard_map/logits/all_to_all | solution.py:53
  67.9 0.6 broadcast_in_dim.34
  68.5 7.9 %all-to-all-start.3 = ((f32[64,1,128]{2,1,0:T(1,128)}), f32[64,1,128]{2,1,0:T(1,128)S(1)}, u32[]{:S(2)}, u32[]{:S(2)}) async-start(f32[64,1,128]{2,1,0:T(1,128)} %broadcast_in_dim.34), calls=%async_computation.3 | async-start | bytes 65536 | tf_op jit(solution)/shard_map/statistics/all_to_all | solution.py:63
  76.7 14.3 %all-to-all-done.3 = f32[64,1,128]{2,1,0:T(1,128)S(1)} async-done(((f32[64,1,128]{2,1,0:T(1,128)}), f32[64,1,128]{2,1,0:T(1,128)S(1)}, u32[]{:S(2)}, u32[]{:S(2)}) %all-to-all-start.3) | async-done | bytes 32800 | tf_op jit(solution)/shard_map/statistics/all_to_all | solution.py:63
  91.5 13.7 %all_gather.3 = bf16[256,1408]{1,0:T(8,128)(2,1)S(1)} all-gather(bf16[64,1408]{1,0:T(8,128)(2,1)S(1)} %fusion.14), channel_id=1, replica_groups=mesh['x'=4,'z'=16,'y'=4,'c'=2] {'y'}, dimensions={0}, use_global_device_ids=true | all-gather | bytes 901120 | tf_op jit(solution)/shard_map/gather_dlogits/all_gather | solution.py:77
  105.1 1.9 %collective-permute-start.1 = (bf16[256,1408]{1,0:T(8,128)(2,1)S(1)}, bf16[256,1408]{1,0:T(8,128)(2,1)}, u32[]{:S(2)}, u32[]{:S(2)}) collective-permute-start(bf16[256,1408]{1,0:T(8,128)(2,1)S(1)} %all_gather.3), channel_id=1, source_target_pairs={{0,1},{1,0},{2,3},{3,2},{4,5},{5,4},{6,7},{7,6},{8,9},{9,8},{10,11... | collective-permute-start | bytes 2162696 | tf_op jit(solution)/shard_map/gather_dlogits/ppermute | solution.py:78
  107.1 0.7 convolution_convert_fusion.2
  107.8 1.6 %collective-permute-done.1 = bf16[256,1408]{1,0:T(8,128)(2,1)} collective-permute-done((bf16[256,1408]{1,0:T(8,128)(2,1)S(1)}, bf16[256,1408]{1,0:T(8,128)(2,1)}, u32[]{:S(2)}, u32[]{:S(2)}) %collective-permute-start.1) | collective-permute-done | bytes 720928 | tf_op jit(solution)/shard_map/gather_dlogits/ppermute | solution.py:78
  109.4 1.8 %broadcast_select_fusion.1 = (f16[256,640]{1,0:T(8,128)(2,1)S(1)}, f16[256,640]{1,0:T(8,128)(2,1)S(1)}) fusion(f16[256,640]{1,0:T(8,128)(2,1)S(1)} %convolution_convert_fusion.2, pred[]{:T(512)S(6)} %eq.16, bf16[1280,640]{1,0:T(8,128)(2,1)S(1)} %copy-done, bf16[256,1408]{1,0:T(8,128)(2,1)} %collective-permute-done.1), kind=kOutput, calls=%fused_computation.22 | convolution fusion | flops 419921920 | bytes 3276801 | tf_op jit(solution)/shard_map/products/dot_general | solution.py:84
  111.1 1.0 pad_maximum_fusion
  112.1 4.2 %all-to-all-start.4 = ((f16[4,128,640]{2,1,0:T(8,128)(2,1)}), f16[4,128,640]{2,1,0:T(8,128)(2,1)}, u32[]{:S(2)}, u32[]{:S(2)}) async-start(f16[4,128,640]{2,1,0:T(8,128)(2,1)} %bitcast.32), calls=%async_computation.4 | async-start | bytes 1310720 | tf_op jit(solution)/shard_map/scatter_hidden_grad/all_to_all | solution.py:95
  116.3 2.4 %fusion.3 = f32[1280,640]{1,0:T(8,128)} fusion(bf16[256,1408]{1,0:T(8,128)(2,1)S(1)} %all_gather.3, bf16[512,640]{1,0:T(8,128)(2,1)S(1)} %bitcast.30, s32[]{:T(128)S(6)} %select_n.46), kind=kOutput, calls=%fused_computation.11 | convolution fusion | flops 419430400 | bytes 4259844 | tf_op jit(solution)/shard_map/products/dot_general | solution.py:86
  118.7 0.9 convert_select_fusion.1
  119.7 8.1 %all-to-all-done.4 = f16[4,128,640]{2,1,0:T(8,128)(2,1)} async-done(((f16[4,128,640]{2,1,0:T(8,128)(2,1)}), f16[4,128,640]{2,1,0:T(8,128)(2,1)}, u32[]{:S(2)}, u32[]{:S(2)}) %all-to-all-start.4) | async-done | bytes 655392 | tf_op jit(solution)/shard_map/scatter_hidden_grad/all_to_all | solution.py:95
  127.8 1.2 convert_reduce_fusion
  129.0 0.7 convert_bitcast_fusion
  129.7 3.5 %all-to-all-start.5 = ((f16[16,8,640]{2,1,0:T(8,128)(2,1)}), f16[16,8,640]{2,1,0:T(8,128)(2,1)S(1)}, u32[]{:S(2)}, u32[]{:S(2)}) async-start(f16[16,8,640]{2,1,0:T(8,128)(2,1)} %convert_bitcast_fusion), calls=%async_computation.5 | async-start | bytes 327680 | tf_op jit(solution)/shard_map/scatter_hidden_grad/all_to_all | solution.py:99
  133.3 0.7 fusion.17
  134.0 4.0 %fusion = bf16[1280,640]{1,0:T(8,128)(2,1)} fusion(f32[1280,640]{1,0:T(8,128)} %fusion.3, bf16[256,1408]{1,0:T(8,128)(2,1)} %collective-permute-done.1, bf16[512,640]{1,0:T(8,128)(2,1)S(1)} %bitcast.31, s32[]{:T(128)S(6)} %select_n.47), kind=kOutput, calls=%fused_computation.1 | convolution fusion | flops 421068800 | bytes 5898244 | tf_op jit(solution)/shard_map/products/dot_general | solution.py:87
  138.0 10.5 %all-to-all-done.5 = f16[16,8,640]{2,1,0:T(8,128)(2,1)S(1)} async-done(((f16[16,8,640]{2,1,0:T(8,128)(2,1)}), f16[16,8,640]{2,1,0:T(8,128)(2,1)S(1)}, u32[]{:S(2)}, u32[]{:S(2)}) %all-to-all-start.5) | async-done | bytes 163872 | tf_op jit(solution)/shard_map/scatter_hidden_grad/all_to_all | solution.py:99
  148.5 0.6 convert_reduce_fusion.2
  (27 shorter events, 1.5 us)
Async XLA Ops:
  0.6 45.5 %copy-start = (bf16[1280,640]{1,0:T(8,128)(2,1)S(1)}, bf16[1280,640]{1,0:T(8,128)(2,1)}, u32[]{:S(2)}) copy-start(bf16[1280,640]{1,0:T(8,128)(2,1)} %param.6) | copy-start | bytes 4915204
  33.0 13.1 %all-to-all-start.1 = ((bf16[4,128,640]{2,1,0:T(8,128)(2,1)}), bf16[4,128,640]{2,1,0:T(8,128)(2,1)S(1)}, u32[]{:S(2)}, u32[]{:S(2)}) async-start(bf16[4,128,640]{2,1,0:T(8,128)(2,1)} %broadcast_in_dim.33), calls=%async_computation.1 | async-start | bytes 1310720 | tf_op jit(solution)/shard_map/gather_hidden/all_to_all | solution.py:21
  47.6 4.2 %collective-permute-start = (f16[256,1280]{1,0:T(8,128)(2,1)}, f16[256,1280]{1,0:T(8,128)(2,1)S(1)}, u32[]{:S(2)}, u32[]{:S(2)}) collective-permute-start(f16[256,1280]{1,0:T(8,128)(2,1)} %convolution_convert_fusion), channel_id=1, source_target_pairs={{0,1},{1,0},{2,3},{3,2},{4,5},{5,4},{6,7},{7,6},{8,9},{9,8},{10,11... | collective-permute-start | bytes 1966088 | tf_op jit(solution)/shard_map/logits/ppermute | solution.py:50
  53.4 23.1 %copy-start.1 = (s32[512]{0:T(512)S(1)}, s32[512]{0:T(512)}, u32[]{:S(2)}) copy-start(s32[512]{0:T(512)} %param.8) | copy-start | bytes 6148
  53.4 23.1 %copy-start.2 = (f32[512]{0:T(512)S(1)}, f32[512]{0:T(512)}, u32[]{:S(2)}) copy-start(f32[512]{0:T(512)} %param.9) | copy-start | bytes 6148
  53.4 13.9 %all-to-all-start.2 = ((f16[4,64,1280]{2,1,0:T(8,128)(2,1)}), f16[4,64,1280]{2,1,0:T(8,128)(2,1)S(1)}, u32[]{:S(2)}, u32[]{:S(2)}) async-start(f16[4,64,1280]{2,1,0:T(8,128)(2,1)} %bitcast.33), calls=%async_computation.2 | async-start | bytes 1310720 | tf_op jit(solution)/shard_map/logits/all_to_all | solution.py:53
  68.5 22.5 %all-to-all-start.3 = ((f32[64,1,128]{2,1,0:T(1,128)}), f32[64,1,128]{2,1,0:T(1,128)S(1)}, u32[]{:S(2)}, u32[]{:S(2)}) async-start(f32[64,1,128]{2,1,0:T(1,128)} %broadcast_in_dim.34), calls=%async_computation.3 | async-start | bytes 65536 | tf_op jit(solution)/shard_map/statistics/all_to_all | solution.py:63
  105.1 4.2 %collective-permute-start.1 = (bf16[256,1408]{1,0:T(8,128)(2,1)S(1)}, bf16[256,1408]{1,0:T(8,128)(2,1)}, u32[]{:S(2)}, u32[]{:S(2)}) collective-permute-start(bf16[256,1408]{1,0:T(8,128)(2,1)S(1)} %all_gather.3), channel_id=1, source_target_pairs={{0,1},{1,0},{2,3},{3,2},{4,5},{5,4},{6,7},{7,6},{8,9},{9,8},{10,11... | collective-permute-start | bytes 2162696 | tf_op jit(solution)/shard_map/gather_dlogits/ppermute | solution.py:78
  112.1 15.7 %all-to-all-start.4 = ((f16[4,128,640]{2,1,0:T(8,128)(2,1)}), f16[4,128,640]{2,1,0:T(8,128)(2,1)}, u32[]{:S(2)}, u32[]{:S(2)}) async-start(f16[4,128,640]{2,1,0:T(8,128)(2,1)} %bitcast.32), calls=%async_computation.4 | async-start | bytes 1310720 | tf_op jit(solution)/shard_map/scatter_hidden_grad/all_to_all | solution.py:95
  129.7 18.7 %all-to-all-start.5 = ((f16[16,8,640]{2,1,0:T(8,128)(2,1)}), f16[16,8,640]{2,1,0:T(8,128)(2,1)S(1)}, u32[]{:S(2)}, u32[]{:S(2)}) async-start(f16[16,8,640]{2,1,0:T(8,128)(2,1)} %convert_bitcast_fusion), calls=%async_computation.5 | async-start | bytes 327680 | tf_op jit(solution)/shard_map/scatter_hidden_grad/all_to_all | solution.py:99

commit v3 on v2

--- a/solution.py
+++ b/solution.py
@@ -30,26 +30,36 @@
     n_vocab = sz["x"] * sz["z"]
     own = tokens // n_width
     half = tokens // sz["c"]
+    part = (sz["c"], sz["x"], own)
     x, z, y, c = (lax.axis_index(a) for a in ("x", "z", "y", "c"))
     first_row = (x * sz["z"] + z) * rows
-    first_token = (c * sz["y"] + y) * own
+    first_token = (y * sz["c"] + c) * own
+    width = head_weight.shape[1]
+    is_low = c == 0
+    swap = lambda v: lax.ppermute(v, "c", [(0, 1), (1, 0)])
+
+    with jax.named_scope("partner_weight"):
+        other_weight = swap(head_weight)
+        low_weight = jnp.where(is_low, head_weight, other_weight)
+        high_weight = jnp.where(is_low, other_weight, head_weight)
 
     keep = discount * (1.0 - terminal.astype(f32))
     carried = jnp.concatenate([jnp.zeros((1,), f32), (keep * cotangent)[:-1]])
 
     with jax.named_scope("gather_hidden"):
-        hidden = spread(spread(hidden_states, "z"), "x")
-        hidden = hidden.reshape(tokens, hidden.shape[-1])
+        hidden = spread(hidden_states, "z").reshape(sz["c"], 1, own, width)
+        hidden = jnp.broadcast_to(hidden, (*part, width)).reshape(-1, own, width)
+        hidden = lax.all_to_all(hidden, ("c", "x"), 0, 0, tiled=True)
+        hidden = hidden.reshape(sz["c"], half, width)
+        near_h = lax.dynamic_index_in_dim(hidden, c, keepdims=False)
+        far_h = swap(lax.dynamic_index_in_dim(hidden, 1 - c, keepdims=False))
 
     with jax.named_scope("logits"):
-        is_low = c == 0
-        near_h = lax.dynamic_slice_in_dim(hidden, c * half, half)
-        far_h = lax.dynamic_slice_in_dim(hidden, (1 - c) * half, half)
         inner = (((1,), (1,)), ((), ()))
-        far_l = lax.dot_general(far_h, head_weight, inner, preferred_element_type=f32)
-        far_l = lax.ppermute(far_l.astype(f16), "c", [(0, 1), (1, 0)])
-        near_l = lax.dot_general(near_h, head_weight, inner, preferred_element_type=f32)
-        chip_l = (near_l + far_l.astype(f32)).astype(f16)
+        chip_l = (
+            lax.dot_general(hidden[0], low_weight, inner, preferred_element_type=f32)
+            + lax.dot_general(hidden[1], high_weight, inner, preferred_element_type=f32)
+        ).astype(f16)
         pieces = lax.all_to_all(chip_l.reshape(sz["y"], own, rows), "y", 0, 0, tiled=True)
         logits = jnp.sum(pieces.astype(f32), axis=0)
 
@@ -75,27 +85,25 @@
         extra = jnp.pad(extra, ((0, 0), (0, 128 - extra.shape[1])))
         sent = jnp.concatenate([dlogits.astype(bf16), extra.astype(bf16)], axis=1)
         near = lax.all_gather(sent, "y", axis=0, tiled=True)
-        far = lax.ppermute(near, "c", [(0, 1), (1, 0)])
+        far = swap(near)
 
     with jax.named_scope("products"):
         outer = (((0,), (0,)), ((), ()))
         near_d, far_d = near[:, :rows], far[:, :rows]
-        near_g = jnp.dot(near_d, head_weight, preferred_element_type=f32).astype(f16)
-        far_g = jnp.dot(far_d, head_weight, preferred_element_type=f32).astype(f16)
+        grad = jnp.stack(
+            [
+                jnp.dot(near_d, low_weight, preferred_element_type=f32).astype(f16),
+                jnp.dot(near_d, high_weight, preferred_element_type=f32).astype(f16),
+            ]
+        )
         weight_grad = (
             lax.dot_general(near_d, near_h, outer, preferred_element_type=f32)
             + lax.dot_general(far_d, far_h, outer, preferred_element_type=f32)
         ).astype(bf16)
-        grad = jnp.concatenate(
-            [jnp.where(is_low, near_g, far_g), jnp.where(is_low, far_g, near_g)]
-        )
 
     with jax.named_scope("scatter_hidden_grad"):
-        width = grad.shape[1]
-        grad = lax.all_to_all(
-            grad.reshape(sz["x"], tokens // sz["x"], width), "x", 0, 0, tiled=True
-        )
-        grad = jnp.sum(grad.astype(f32), axis=0).astype(f16)
+        grad = lax.all_to_all(grad.reshape(-1, own, width), ("c", "x"), 0, 0, tiled=True)
+        grad = jnp.sum(grad.reshape(*part, width).astype(f32), axis=1).astype(f16)
         grad = lax.all_to_all(
             grad.reshape(sz["z"], tokens // n_vocab, width), "z", 0, 0, tiled=True
         )
@@ -104,9 +112,10 @@
     with jax.named_scope("rewards"):
         near_s = near[:, rows : rows + 8].astype(f32)
         far_s = far[:, rows : rows + 8].astype(f32)
-        stats = jnp.concatenate(
-            [jnp.where(is_low, near_s, far_s), jnp.where(is_low, far_s, near_s)]
-        )
+        near_s, far_s = (v.reshape(sz["x"], own, -1) for v in (near_s, far_s))
+        low_s = jnp.where(is_low, near_s, far_s)
+        high_s = jnp.where(is_low, far_s, near_s)
+        stats = jnp.stack([low_s, high_s], axis=1).reshape(tokens, -1)
         lse_all = stats[:, 0] + stats[:, 1] + stats[:, 2]
         picked_all = stats[:, 3] + stats[:, 4] + stats[:, 5]
         next_value = jnp.concatenate([lse_all[1:], jnp.zeros((1,), f32)])

time: 151 us -> 156 us (1.033)
  waiting for transfers between devices: 53.9 us -> 46.5 us
  other arithmetic: 6.84 us -> 12.4 us
  local copies, waits for them, and re-layouts: 2.82 us -> 7.51 us
  starting transfers between devices: 28.5 us -> 30.5 us
    ppermute x2 -> x3, waiting for transfers between devices: 3.87 us -> 0.01 us  [shards(): swap = lambda v: lax.ppermute(v, 'c', [(0, 1), (1, 0)])]
    all_to_all x1, waiting for transfers between devices: 10.5 us -> 7.17 us  [shards(): lax.all_to_all(grad.reshape(sz['z'], tokens // n_vocab, width), 'z', 0, 0...]
    ppermute x2 -> x3, starting transfers between devices: 3.82 us -> 6.18 us  [shards(): swap = lambda v: lax.ppermute(v, 'c', [(0, 1), (1, 0)])]
    select_n x2, local copies, waits for them, and re-layouts: 0.13 us -> 1.98 us  [the longest x1 1 us: shards(): high_s = jnp.where(is_low, far_s, near_s)]
    reduce_sum x1, other arithmetic: 0.09 us -> 1.93 us  [shards(): logits = jnp.sum(pieces.astype(f32), axis=0)]
    squeeze x0 -> x1, local copies, waits for them, and re-layouts: none -> 1.76 us  [shards(): far_h = swap(lax.dynamic_index_in_dim(hidden, 1 - c, keepdims=False))]
  transfers between devices with their start and end apart: 7 -> 8, of which waited for: 7 -> 5; matrix products, arithmetic and copies ran while one was open for 7% -> 14% of each run, Pallas kernels for 0% -> 0%
where the time goes in v3:
time: 156 us; the launch traced here: 153 us
  waiting for transfers between devices  46.5 us (30%)
  blocking collectives  44.2 us (28%)
  starting transfers between devices  30.5 us (20%)
  other arithmetic  12.4 us (8%)
  matrix products  11.1 us (7%)
  local copies, waits for them, and re-layouts  7.51 us (5%)
    all_to_all x1, blocking collectives, spread(): copies = lax.all_to_all(copies, axis, 0, 0, tiled=True)  29.7 us
    all_to_all x1, waiting for transfers between devices, shards(): lax.all_to_all(jnp.broadcast_to(mine, (n_vocab, 2 * own)), ('z', 'x'), 0,...  14.5 us
    all_gather x1, blocking collectives, shards(): near = lax.all_gather(sent, 'y', axis=0, tiled=True)  14.5 us
    all_to_all x1, waiting for transfers between devices, shards(): hidden = lax.all_to_all(hidden, ('c', 'x'), 0, 0, tiled=True)  11.2 us
    all_to_all x1, waiting for transfers between devices, shards(): lax.all_to_all(chip_l.reshape(sz['y'], own, rows), 'y', 0, 0, tiled=True)  8.47 us
    all_to_all x1, starting transfers between devices, shards(): lax.all_to_all(jnp.broadcast_to(mine, (n_vocab, 2 * own)), ('z', 'x'), 0,...  7.52 us
    all_to_all x1, waiting for transfers between devices, shards(): lax.all_to_all(grad.reshape(sz['z'], tokens // n_vocab, width), 'z', 0, 0...  7.17 us
    ppermute x3, starting transfers between devices, shards(): swap = lambda v: lax.ppermute(v, 'c', [(0, 1), (1, 0)])  6.18 us
  transfers between devices with their start and end apart: 8, of which 5 were waited for; matrix products, arithmetic and copies ran while one was open for 14% of the time, Pallas kernels for 0%

profile of v3, /device:TPU:24, one launch (start us, length us, event | category | flops | bytes accessed | tf_op | source)
XLA Modules:
  0.0 153.1 jit_solution(6695047348674919557)
XLA Ops:
  0.6 1.9 %collective-permute-start = (bf16[1280,640]{1,0:T(8,128)(2,1)}, bf16[1280,640]{1,0:T(8,128)(2,1)S(1)}, u32[]{:S(2)}, u32[]{:S(2)}) collective-permute-start(bf16[1280,640]{1,0:T(8,128)(2,1)} %param.6), channel_id=1, source_target_pairs={{0,1},{1,0},{2,3},{3,2},{4,5},{5,4},{6,7},{7,6},{8,9},{9,8},{10,11... | collective-permute-start | bytes 4915208 | tf_op jit(solution)/shard_map/partner_weight/ppermute | solution.py:39
  3.3 29.7 %all_to_all.34 = bf16[16,8,640]{2,1,0:T(8,128)(2,1)S(1)} all-to-all(bf16[16,8,640]{2,1,0:T(8,128)(2,1)S(1)} %broadcast_in_dim.36), channel_id=1, replica_groups=mesh['x'=4,'z'=16,'y'=4,'c'=2] {'z'}, dimensions={0} | all-to-all | bytes 327680 | tf_op jit(solution)/shard_map/gather_hidden/all_to_all | solution.py:21
  33.0 0.9 broadcast_in_dim.38
  33.9 4.3 %all-to-all-start.1 = ((bf16[8,64,640]{2,1,0:T(8,128)(2,1)}), bf16[8,64,640]{2,1,0:T(8,128)(2,1)}, u32[]{:S(2)}, u32[]{:S(2)}) async-start(bf16[8,64,640]{2,1,0:T(8,128)(2,1)} %bitcast.47), calls=%async_computation.1 | async-start | bytes 1310720 | tf_op jit(solution)/shard_map/gather_hidden/all_to_all | solution.py:52
  38.2 11.2 %all-to-all-done.1 = bf16[8,64,640]{2,1,0:T(8,128)(2,1)} async-done(((bf16[8,64,640]{2,1,0:T(8,128)(2,1)}), bf16[8,64,640]{2,1,0:T(8,128)(2,1)}, u32[]{:S(2)}, u32[]{:S(2)}) %all-to-all-start.1) | async-done | bytes 655392 | tf_op jit(solution)/shard_map/gather_hidden/all_to_all | solution.py:52
  49.4 1.1 fusion.19
  51.4 1.7 %fusion.1 = f16[1280,256]{0,1:T(8,128)(2,1)} fusion(f32[1280,256]{0,1:T(8,128)S(1)} %fusion.5, bf16[256,640]{1,0:T(8,128)(2,1)S(1)} %bitcast.49, bf16[1280,640]{1,0:T(8,128)(2,1)S(1)} %copy-done, bf16[1280,640]{1,0:T(8,128)(2,1)S(1)} %collective-permute-done, pred[]{:T(512)S(6)} %eq.16), kind=kOutput, calls=%fused_computation.3 | convolution fusion | flops 420904960 | bytes 5570561 | tf_op jit(solution)/shard_map/logits/dot_general | solution.py:60
  53.0 4.8 %all-to-all-start.2 = ((f16[4,64,1280]{2,1,0:T(8,128)(2,1)}), f16[4,64,1280]{2,1,0:T(8,128)(2,1)}, u32[]{:S(2)}, u32[]{:S(2)}) async-start(f16[4,64,1280]{2,1,0:T(8,128)(2,1)} %bitcast.48), calls=%async_computation.2 | async-start | bytes 1310720 | tf_op jit(solution)/shard_map/logits/all_to_all | solution.py:63
  58.6 8.5 %all-to-all-done.2 = f16[4,64,1280]{2,1,0:T(8,128)(2,1)} async-done(((f16[4,64,1280]{2,1,0:T(8,128)(2,1)}), f16[4,64,1280]{2,1,0:T(8,128)(2,1)}, u32[]{:S(2)}, u32[]{:S(2)}) %all-to-all-start.2) | async-done | bytes 655392 | tf_op jit(solution)/shard_map/logits/all_to_all | solution.py:63
  67.1 1.9 %convert_reduce_fusion.1 = f32[64,1280]{1,0:T(8,128)} fusion(f16[4,64,1280]{2,1,0:T(8,128)(2,1)} %all-to-all-done.2), kind=kLoop, calls=%fused_computation.7 | loop fusion | flops 573440 | bytes 983040 | tf_op jit(solution)/shard_map/logits/reduce_sum | solution.py:64
  69.0 1.1 reduce_max.18
  70.1 1.2 exponential_reduce_fusion
  72.1 7.5 %all-to-all-start.3 = ((f32[64,1,128]{2,1,0:T(1,128)}), f32[64,1,128]{2,1,0:T(1,128)S(1)}, u32[]{:S(2)}, u32[]{:S(2)}) async-start(f32[64,1,128]{2,1,0:T(1,128)} %broadcast_in_dim.39), calls=%async_computation.3 | async-start | bytes 65536 | tf_op jit(solution)/shard_map/statistics/all_to_all | solution.py:73
  79.9 14.5 %all-to-all-done.3 = f32[64,1,128]{2,1,0:T(1,128)S(1)} async-done(((f32[64,1,128]{2,1,0:T(1,128)}), f32[64,1,128]{2,1,0:T(1,128)S(1)}, u32[]{:S(2)}, u32[]{:S(2)}) %all-to-all-start.3) | async-done | bytes 32800 | tf_op jit(solution)/shard_map/statistics/all_to_all | solution.py:73
  94.7 1.1 subtract_convert_fusion
  95.8 14.5 %all_gather.3 = bf16[256,1408]{1,0:T(8,128)(2,1)} all-gather(bf16[64,1408]{1,0:T(8,128)(2,1)S(1)} %fusion.13), channel_id=1, replica_groups=mesh['x'=4,'z'=16,'y'=4,'c'=2] {'y'}, dimensions={0}, use_global_device_ids=true | all-gather | bytes 901120 | tf_op jit(solution)/shard_map/gather_dlogits/all_gather | solution.py:87
  110.3 1.9 %collective-permute-start.1 = (bf16[256,1408]{1,0:T(8,128)(2,1)}, bf16[256,1408]{1,0:T(8,128)(2,1)}, u32[]{:S(2)}, u32[]{:S(2)}) collective-permute-start(bf16[256,1408]{1,0:T(8,128)(2,1)} %all_gather.3), channel_id=1, source_target_pairs={{0,1},{1,0},{2,3},{3,2},{4,5},{5,4},{6,7},{7,6},{8,9},{9,8},{10,11... | collective-permute-start | bytes 2162696 | tf_op jit(solution)/shard_map/gather_dlogits/ppermute | solution.py:39
  112.2 1.9 %fusion.3 = f16[1,256,640]{2,1,0:T(8,128)(2,1)S(1)} fusion(bf16[1280,640]{1,0:T(8,128)(2,1)S(1)} %collective-permute-done, bf16[1280,640]{1,0:T(8,128)(2,1)S(1)} %copy-done, pred[]{:T(512)S(6)} %eq.16, bf16[256,1408]{1,0:T(8,128)(2,1)} %all_gather.3), kind=kOutput, calls=%fused_computation.11 | convolution fusion | flops 420413440 | bytes 4259841 | tf_op jit(solution)/shard_map/products/dot_general | solution.py:96
  114.1 1.9 %fusion.2 = f16[1,256,640]{2,1,0:T(8,128)(2,1)S(1)} fusion(bf16[1280,640]{1,0:T(8,128)(2,1)S(1)} %copy-done, bf16[1280,640]{1,0:T(8,128)(2,1)S(1)} %collective-permute-done, pred[]{:T(512)S(6)} %eq.16, bf16[256,1408]{1,0:T(8,128)(2,1)} %all_gather.3), kind=kOutput, calls=%fused_computation.10 | convolution fusion | flops 420413440 | bytes 4259841 | tf_op jit(solution)/shard_map/products/dot_general | solution.py:95
  116.0 1.0 pad_maximum_fusion
  117.0 4.2 %all-to-all-start.4 = ((f16[8,64,640]{2,1,0:T(8,128)(2,1)}), f16[8,64,640]{2,1,0:T(8,128)(2,1)}, u32[]{:S(2)}, u32[]{:S(2)}) async-start(f16[8,64,640]{2,1,0:T(8,128)(2,1)} %bitcast.15), calls=%async_computation.4 | async-start | bytes 1310720 | tf_op jit(solution)/shard_map/scatter_hidden_grad/all_to_all | solution.py:105
  121.2 1.8 %dynamic-slice_bitcast_fusion = bf16[256,640]{1,0:T(8,128)(2,1)} fusion(bf16[2,256,640]{2,1,0:T(8,128)(2,1)} %bitcast.18, s32[]{:T(128)S(6)} %select_n.76), kind=kLoop, calls=%fused_computation.22 | loop fusion | bytes 655364 | tf_op jit(solution)/shard_map/gather_hidden/jit(dynamic_index_in_dim)/squeeze | solution.py:55
  123.0 2.3 %collective-permute-start.2 = (bf16[256,640]{1,0:T(8,128)(2,1)}, bf16[256,640]{1,0:T(8,128)(2,1)}, u32[]{:S(2)}, u32[]{:S(2)}) collective-permute-start(bf16[256,640]{1,0:T(8,128)(2,1)} %dynamic-slice_bitcast_fusion), channel_id=1, source_target_pairs={{0,1},{1,0},{2,3},{3,2},{4,5},{5,4},{6,7},{7,6},{8,9},{9,8},{10,11... | collective-permute-start | bytes 983048 | tf_op jit(solution)/shard_map/gather_hidden/ppermute | solution.py:39
  125.3 1.9 %fusion.6 = f32[1280,640]{1,0:T(8,128)S(1)} fusion(bf16[256,1408]{1,0:T(8,128)(2,1)} %all_gather.3, bf16[2,256,640]{2,1,0:T(8,128)(2,1)} %bitcast.18, s32[]{:T(128)S(6)} %select_n.75), kind=kOutput, calls=%fused_computation.15 | convolution fusion | flops 419430400 | bytes 4259844 | tf_op jit(solution)/shard_map/products/dot_general | solution.py:100
  127.2 5.1 %all-to-all-done.4 = f16[8,64,640]{2,1,0:T(8,128)(2,1)} async-done(((f16[8,64,640]{2,1,0:T(8,128)(2,1)}), f16[8,64,640]{2,1,0:T(8,128)(2,1)}, u32[]{:S(2)}, u32[]{:S(2)}) %all-to-all-start.4) | async-done | bytes 655392 | tf_op jit(solution)/shard_map/scatter_hidden_grad/all_to_all | solution.py:105
  132.4 1.2 convert_reduce_fusion
  134.3 3.5 %all-to-all-start.5 = ((f16[16,8,640]{2,1,0:T(8,128)(2,1)}), f16[16,8,640]{2,1,0:T(8,128)(2,1)S(1)}, u32[]{:S(2)}, u32[]{:S(2)}) async-start(f16[16,8,640]{2,1,0:T(8,128)(2,1)} %bitcast.51), calls=%async_computation.5 | async-start | bytes 327680 | tf_op jit(solution)/shard_map/scatter_hidden_grad/all_to_all | solution.py:107
  137.8 1.6 %convert_select_fusion.1 = (f32[256,8]{1,0:T(8,128)}, f32[256,8]{1,0:T(8,128)}) fusion(pred[]{:T(512)S(6)} %eq.16, bf16[256,1408]{1,0:T(8,128)(2,1)} %collective-permute-done.1, bf16[256,1408]{1,0:T(8,128)(2,1)} %all_gather.3), kind=kLoop, calls=%fused_computation.31 | loop fusion | flops 8192 | bytes 24577 | tf_op jit(solution)/shard_map/rewards/jit(_where)/select_n | solution.py:116
  139.4 1.0 copy.22
  140.4 1.0 copy.23
  142.3 3.0 %fusion = bf16[1280,640]{1,0:T(8,128)(2,1)} fusion(f32[1280,640]{1,0:T(8,128)S(1)} %fusion.6, bf16[256,640]{1,0:T(8,128)(2,1)} %collective-permute-done.2, bf16[256,1408]{1,0:T(8,128)(2,1)} %collective-permute-done.1), kind=kOutput, calls=%fused_computation.1 | convolution fusion | flops 421068800 | bytes 5898240 | tf_op jit(solution)/shard_map/products/dot_general | solution.py:101
  145.3 7.2 %all-to-all-done.5 = f16[16,8,640]{2,1,0:T(8,128)(2,1)S(1)} async-done(((f16[16,8,640]{2,1,0:T(8,128)(2,1)}), f16[16,8,640]{2,1,0:T(8,128)(2,1)S(1)}, u32[]{:S(2)}, u32[]{:S(2)}) %all-to-all-start.5) | async-done | bytes 163872 | tf_op jit(solution)/shard_map/scatter_hidden_grad/all_to_all | solution.py:107
  (33 shorter events, 5.7 us)
Async XLA Ops:
  0.6 49.9 %collective-permute-start = (bf16[1280,640]{1,0:T(8,128)(2,1)}, bf16[1280,640]{1,0:T(8,128)(2,1)S(1)}, u32[]{:S(2)}, u32[]{:S(2)}) collective-permute-start(bf16[1280,640]{1,0:T(8,128)(2,1)} %param.6), channel_id=1, source_target_pairs={{0,1},{1,0},{2,3},{3,2},{4,5},{5,4},{6,7},{7,6},{8,9},{9,8},{10,11... | collective-permute-start | bytes 4915208 | tf_op jit(solution)/shard_map/partner_weight/ppermute | solution.py:39
  33.0 17.6 %copy-start = (bf16[1280,640]{1,0:T(8,128)(2,1)S(1)}, bf16[1280,640]{1,0:T(8,128)(2,1)}, u32[]{:S(2)}) copy-start(bf16[1280,640]{1,0:T(8,128)(2,1)} %param.6) | copy-start | bytes 4915204
  33.9 15.5 %all-to-all-start.1 = ((bf16[8,64,640]{2,1,0:T(8,128)(2,1)}), bf16[8,64,640]{2,1,0:T(8,128)(2,1)}, u32[]{:S(2)}, u32[]{:S(2)}) async-start(bf16[8,64,640]{2,1,0:T(8,128)(2,1)} %bitcast.47), calls=%async_computation.1 | async-start | bytes 1310720 | tf_op jit(solution)/shard_map/gather_hidden/all_to_all | solution.py:52
  53.0 26.6 %copy-start.1 = (s32[512]{0:T(512)S(1)}, s32[512]{0:T(512)}, u32[]{:S(2)}) copy-start(s32[512]{0:T(512)} %param.8) | copy-start | bytes 6148
  53.0 26.6 %copy-start.2 = (f32[512]{0:T(512)S(1)}, f32[512]{0:T(512)}, u32[]{:S(2)}) copy-start(f32[512]{0:T(512)} %param.9) | copy-start | bytes 6148
  53.0 14.0 %all-to-all-start.2 = ((f16[4,64,1280]{2,1,0:T(8,128)(2,1)}), f16[4,64,1280]{2,1,0:T(8,128)(2,1)}, u32[]{:S(2)}, u32[]{:S(2)}) async-start(f16[4,64,1280]{2,1,0:T(8,128)(2,1)} %bitcast.48), calls=%async_computation.2 | async-start | bytes 1310720 | tf_op jit(solution)/shard_map/logits/all_to_all | solution.py:63
  72.1 22.3 %all-to-all-start.3 = ((f32[64,1,128]{2,1,0:T(1,128)}), f32[64,1,128]{2,1,0:T(1,128)S(1)}, u32[]{:S(2)}, u32[]{:S(2)}) async-start(f32[64,1,128]{2,1,0:T(1,128)} %broadcast_in_dim.39), calls=%async_computation.3 | async-start | bytes 65536 | tf_op jit(solution)/shard_map/statistics/all_to_all | solution.py:73
  110.3 27.5 %collective-permute-start.1 = (bf16[256,1408]{1,0:T(8,128)(2,1)}, bf16[256,1408]{1,0:T(8,128)(2,1)}, u32[]{:S(2)}, u32[]{:S(2)}) collective-permute-start(bf16[256,1408]{1,0:T(8,128)(2,1)} %all_gather.3), channel_id=1, source_target_pairs={{0,1},{1,0},{2,3},{3,2},{4,5},{5,4},{6,7},{7,6},{8,9},{9,8},{10,11... | collective-permute-start | bytes 2162696 | tf_op jit(solution)/shard_map/gather_dlogits/ppermute | solution.py:39
  117.0 15.4 %all-to-all-start.4 = ((f16[8,64,640]{2,1,0:T(8,128)(2,1)}), f16[8,64,640]{2,1,0:T(8,128)(2,1)}, u32[]{:S(2)}, u32[]{:S(2)}) async-start(f16[8,64,640]{2,1,0:T(8,128)(2,1)} %bitcast.15), calls=%async_computation.4 | async-start | bytes 1310720 | tf_op jit(solution)/shard_map/scatter_hidden_grad/all_to_all | solution.py:105
  123.0 19.3 %collective-permute-start.2 = (bf16[256,640]{1,0:T(8,128)(2,1)}, bf16[256,640]{1,0:T(8,128)(2,1)}, u32[]{:S(2)}, u32[]{:S(2)}) collective-permute-start(bf16[256,640]{1,0:T(8,128)(2,1)} %dynamic-slice_bitcast_fusion), channel_id=1, source_target_pairs={{0,1},{1,0},{2,3},{3,2},{4,5},{5,4},{6,7},{7,6},{8,9},{9,8},{10,11... | collective-permute-start | bytes 983048 | tf_op jit(solution)/shard_map/gather_hidden/ppermute | solution.py:39
  134.3 18.2 %all-to-all-start.5 = ((f16[16,8,640]{2,1,0:T(8,128)(2,1)}), f16[16,8,640]{2,1,0:T(8,128)(2,1)S(1)}, u32[]{:S(2)}, u32[]{:S(2)}) async-start(f16[16,8,640]{2,1,0:T(8,128)(2,1)} %bitcast.51), calls=%async_computation.5 | async-start | bytes 327680 | tf_op jit(solution)/shard_map/scatter_hidden_grad/all_to_all | solution.py:107

commit v4 on v2

v4 whole, which is shorter than its diff:
```python
import jax
import jax.numpy as jnp
from jax import lax
from jax.sharding import Mesh, PartitionSpec as P

discount = 0.99
f32 = jnp.float32
bf16 = jnp.bfloat16
f16 = jnp.float16


def spread(block, axis):
    copies = jnp.broadcast_to(block, (lax.axis_size(axis), *block.shape))
    copies = lax.all_to_all(copies, axis, 0, 0, tiled=True)
    return copies.reshape(-1, block.shape[-1])


def shards(hidden_states, head_weight, targets, terminal, cotangent):
    rows, width = head_weight.shape
    tokens = targets.shape[0]
    sz = {a: lax.axis_size(a) for a in ("x", "z", "y", "c")}
    n_width = sz["y"] * sz["c"]
    n_vocab = sz["x"] * sz["z"]
    own = tokens // n_width
    half = tokens // sz["c"]
    x, z, y, c = (lax.axis_index(a) for a in ("x", "z", "y", "c"))
    first_row = (x * sz["z"] + z) * rows
    first_token = (c * sz["y"] + y) * own
    is_low = c == 0
    swap = lambda v: lax.ppermute(v, "c", [(0, 1), (1, 0)])
    turn = lambda v, axis: lax.all_to_all(v, axis, 0, 0, tiled=True)
    cut = lambda v: lax.dynamic_slice(v, (first_token,), (own,))

    keep = discount * (1.0 - terminal.astype(f32))
    carried = jnp.concatenate([jnp.zeros((1,), f32), (keep * cotangent)[:-1]])
    column = jnp.arange(rows, dtype=jnp.int32)

    with jax.named_scope("gather_hidden"):
        hidden = spread(spread(hidden_states, "z"), "x")

    with jax.named_scope("logits"):
        near_h = lax.dynamic_slice_in_dim(hidden, c * half, half)
        far_h = lax.dynamic_slice_in_dim(hidden, (1 - c) * half, half)
        inner = (((1,), (1,)), ((), ()))
        far_l = lax.dot_general(far_h, head_weight, inner, preferred_element_type=f32)
        far_l = swap(far_l.astype(f16))
        near_l = lax.dot_general(near_h, head_weight, inner, preferred_element_type=f32)
        chip_l = (near_l + far_l.astype(f32)).astype(f16)
        pieces = turn(chip_l.reshape(sz["y"], own, rows), "y")
        logits = jnp.sum(pieces.astype(f32), axis=0)

    with jax.named_scope("own_statistics"):
        hit = (cut(targets) - first_row)[:, None] == column
        own_top = jnp.max(logits, axis=1)
        raised = jnp.exp(logits - own_top[:, None])
        picked = jnp.sum(jnp.where(hit, logits, 0.0), axis=1)
        mine = jnp.concatenate([own_top + jnp.log(jnp.sum(raised, axis=1)), picked])
        mine = jnp.broadcast_to(mine, (n_vocab, 2 * own))

    with jax.named_scope("gather_raised"):
        near = lax.all_gather(raised.astype(bf16), "y", axis=0, tiled=True)
        far = swap(near)
        raised = jnp.concatenate([jnp.where(is_low, near, far), jnp.where(is_low, far, near)])

    with jax.named_scope("statistics"):
        every = turn(mine, ("z", "x"))
        top = jnp.max(every[:, :own], axis=0)
        lse = top + jnp.log(jnp.sum(jnp.exp(every[:, :own] - top), axis=0))
        picked = jnp.sum(every[:, own:], axis=0)
        parts = jnp.concatenate([lse, picked, jnp.exp(own_top - lse), lse])
        parts, _ = lax.optimization_barrier((parts, near))
        parts = turn(jnp.broadcast_to(parts, (n_width, 4 * own)), ("c", "y"))
        lse, picked, factor, _ = (
            parts[:, i * own : (i + 1) * own].reshape(tokens) for i in range(4)
        )

    with jax.named_scope("products"):
        hit_all = (targets - first_row)[:, None] == column
        dlogits = jnp.where(hit_all, cotangent[:, None], 0.0)
        dlogits = (dlogits - (carried * factor)[:, None] * raised.astype(f32)).astype(bf16)
        grad = jnp.dot(dlogits, head_weight, preferred_element_type=f32).astype(f16)
        outer = (((0,), (0,)), ((), ()))
        weight_grad = lax.dot_general(dlogits, hidden, outer, preferred_element_type=f32)
        weight_grad = weight_grad.astype(bf16)

    with jax.named_scope("scatter_hidden_grad"):
        grad = turn(grad.reshape(sz["x"], -1, width), "x")
        grad = jnp.sum(grad.astype(f32), axis=0).astype(f16)
        grad = turn(grad.reshape(sz["z"], -1, width), "z")
        hidden_grad = jnp.sum(grad.astype(f32), axis=0).astype(bf16)

    with jax.named_scope("rewards"):
        next_value = jnp.concatenate([lse[1:], jnp.zeros((1,), f32)])
        rewards = picked - keep * next_value
    return (rewards, hidden_grad, weight_grad)


def solution(mesh):
    fine = Mesh(mesh.devices.reshape(4, 16, 4, 2), ("x", "z", "y", "c"))
    block = P(("x", "z"), ("y", "c"))
    return jax.shard_map(
        shards,
        mesh=fine,
        in_specs=(block, block, P(), P(), P()),
        out_specs=(P(), block, block),
        check_vma=False,
    )
```

time: 151 us -> 148 us (0.980)
  waiting for transfers between devices: 53.9 us -> 33 us
  blocking collectives: 44.3 us -> 58.5 us
  starting transfers between devices: 28.5 us -> 37.8 us
  matrix products: 12 us -> 8.57 us
  other arithmetic: 6.84 us -> 4.13 us
    all_to_all x4, waiting for transfers between devices: 41.2 us -> 22 us  [shards(): turn = lambda v, axis: lax.all_to_all(v, axis, 0, 0, tiled=True)]
    all_to_all x0 -> x1, blocking collectives: none -> 14.3 us  [shards(): turn = lambda v, axis: lax.all_to_all(v, axis, 0, 0, tiled=True)]
    all_to_all x4, starting transfers between devices: 20.4 us -> 29.6 us  [shards(): turn = lambda v, axis: lax.all_to_all(v, axis, 0, 0, tiled=True)]
    dot_general x4 -> x2, matrix products: 8.88 us -> 5.22 us  [the longest x1 3.76 us: shards(): lax.dot_general(dlogits, hidden, outer, preferred_element_type=f32)]
    ppermute x2, waiting for transfers between devices: 3.87 us -> 2.18 us  [shards(): swap = lambda v: lax.ppermute(v, 'c', [(0, 1), (1, 0)])]
  transfers between devices with their start and end apart: 7 -> 7, of which waited for: 7 -> 6; matrix products, arithmetic and copies ran while one was open for 7% -> 3% of each run, Pallas kernels for 0% -> 0%
where the time goes in v4:
time: 148 us; the launch traced here: 146 us
  blocking collectives  58.5 us (40%)
  starting transfers between devices  37.8 us (26%)
  waiting for transfers between devices  33 us (22%)
  matrix products  8.57 us (6%)
  other arithmetic  4.13 us (3%)
  local copies, waits for them, and re-layouts  3.4 us (2%)
    all_to_all x1, blocking collectives, spread(): copies = lax.all_to_all(copies, axis, 0, 0, tiled=True)  30.6 us
    all_to_all x4, starting transfers between devices, shards(): turn = lambda v, axis: lax.all_to_all(v, axis, 0, 0, tiled=True)  29.6 us
    all_to_all x4, waiting for transfers between devices, shards(): turn = lambda v, axis: lax.all_to_all(v, axis, 0, 0, tiled=True)  22 us
    all_to_all x1, blocking collectives, shards(): turn = lambda v, axis: lax.all_to_all(v, axis, 0, 0, tiled=True)  14.3 us
    all_gather x1, blocking collectives, shards(): near = lax.all_gather(raised.astype(bf16), 'y', axis=0, tiled=True)  13.6 us
    all_to_all x1, waiting for transfers between devices, spread(): copies = lax.all_to_all(copies, axis, 0, 0, tiled=True)  8.79 us
    all_to_all x1, starting transfers between devices, spread(): copies = lax.all_to_all(copies, axis, 0, 0, tiled=True)  4.29 us
    ppermute x2, starting transfers between devices, shards(): swap = lambda v: lax.ppermute(v, 'c', [(0, 1), (1, 0)])  3.98 us
  transfers between devices with their start and end apart: 7, of which 6 were waited for; matrix products, arithmetic and copies ran while one was open for 3% of the time, Pallas kernels for 0%

profile of v4, /device:TPU:24, one launch (start us, length us, event | category | flops | bytes accessed | tf_op | source)
XLA Modules:
  0.0 146.2 jit_solution(2215056945677457355)
XLA Ops:
  0.6 0.8 broadcast_in_dim.36
  1.5 30.6 %all_to_all.43 = bf16[16,8,640]{2,1,0:T(8,128)(2,1)S(1)} all-to-all(bf16[16,8,640]{2,1,0:T(8,128)(2,1)S(1)} %broadcast_in_dim.36), channel_id=1, replica_groups=mesh['x'=4,'z'=16,'y'=4,'c'=2] {'z'}, dimensions={0} | all-to-all | bytes 327680 | tf_op jit(solution)/shard_map/gather_hidden/all_to_all | solution.py:14
  32.1 0.9 broadcast_in_dim.37
  33.0 4.3 %all-to-all-start.1 = ((bf16[4,128,640]{2,1,0:T(8,128)(2,1)}), bf16[4,128,640]{2,1,0:T(8,128)(2,1)S(1)}, u32[]{:S(2)}, u32[]{:S(2)}) async-start(bf16[4,128,640]{2,1,0:T(8,128)(2,1)} %broadcast_in_dim.37), calls=%async_computation.1 | async-start | bytes 1310720 | tf_op jit(solution)/shard_map/gather_hidden/all_to_all | solution.py:14
  37.3 8.8 %all-to-all-done.1 = bf16[4,128,640]{2,1,0:T(8,128)(2,1)S(1)} async-done(((bf16[4,128,640]{2,1,0:T(8,128)(2,1)}), bf16[4,128,640]{2,1,0:T(8,128)(2,1)S(1)}, u32[]{:S(2)}, u32[]{:S(2)}) %all-to-all-start.1) | async-done | bytes 655392 | tf_op jit(solution)/shard_map/gather_hidden/all_to_all | solution.py:14
  46.1 0.7 convolution_convert_fusion.1
  46.8 1.9 %collective-permute-start = (f16[256,1280]{1,0:T(8,128)(2,1)S(1)}, f16[256,1280]{1,0:T(8,128)(2,1)}, u32[]{:S(2)}, u32[]{:S(2)}) collective-permute-start(f16[256,1280]{1,0:T(8,128)(2,1)S(1)} %convolution_convert_fusion.1), channel_id=1, source_target_pairs={{0,1},{1,0},{2,3},{3,2},{4,5},{5,4},{6,7},{7,6},{8,9},{9,8},{10,11... | collective-permute-start | bytes 1966088 | tf_op jit(solution)/shard_map/logits/ppermute | solution.py:30
  48.7 2.2 %collective-permute-done = f16[256,1280]{1,0:T(8,128)(2,1)} collective-permute-done((f16[256,1280]{1,0:T(8,128)(2,1)S(1)}, f16[256,1280]{1,0:T(8,128)(2,1)}, u32[]{:S(2)}, u32[]{:S(2)}) %collective-permute-start) | collective-permute-done | bytes 655392 | tf_op jit(solution)/shard_map/logits/ppermute | solution.py:30
  50.9 2.6 %add_convert_fusion = f16[256,1280]{1,0:T(8,128)(2,1)} fusion(f16[256,1280]{1,0:T(8,128)(2,1)} %collective-permute-done, bf16[1280,640]{1,0:T(8,128)(2,1)S(1)} %copy-done, bf16[512,640]{1,0:T(8,128)(2,1)S(1)} %bitcast.16, s32[]{:T(128)S(6)} %select_n.29), kind=kOutput, calls=%fused_computation.7 | convolution fusion | flops 420413440 | bytes 3276804 | tf_op jit(solution)/shard_map/logits/dot_general | solution.py:47
  53.6 4.7 %all-to-all-start.2 = ((f16[4,64,1280]{2,1,0:T(8,128)(2,1)}), f16[4,64,1280]{2,1,0:T(8,128)(2,1)S(1)}, u32[]{:S(2)}, u32[]{:S(2)}) async-start(f16[4,64,1280]{2,1,0:T(8,128)(2,1)} %bitcast.2), calls=%async_computation.2 | async-start | bytes 1310720 | tf_op jit(solution)/shard_map/logits/all_to_all | solution.py:31
  58.3 9.0 %all-to-all-done.2 = f16[4,64,1280]{2,1,0:T(8,128)(2,1)S(1)} async-done(((f16[4,64,1280]{2,1,0:T(8,128)(2,1)}), f16[4,64,1280]{2,1,0:T(8,128)(2,1)S(1)}, u32[]{:S(2)}, u32[]{:S(2)}) %all-to-all-start.2) | async-done | bytes 655392 | tf_op jit(solution)/shard_map/logits/all_to_all | solution.py:31
  67.5 0.1 reduce_max.18
  67.6 0.3 fusion.6
  67.9 0.6 broadcast_in_dim.39
  68.6 7.9 %all-to-all-start.3 = ((f32[64,1,128]{2,1,0:T(1,128)}), f32[64,1,128]{2,1,0:T(1,128)S(1)}, u32[]{:S(2)}, u32[]{:S(2)}) async-start(f32[64,1,128]{2,1,0:T(1,128)} %broadcast_in_dim.39), calls=%async_computation.3 | async-start | bytes 65536 | tf_op jit(solution)/shard_map/statistics/all_to_all | solution.py:31
  76.5 13.6 %all_gather.3 = bf16[256,1280]{1,0:T(8,128)(2,1)S(1)} all-gather(bf16[64,1280]{1,0:T(8,128)(2,1)S(1)} %get-tuple-element.13), channel_id=1, replica_groups=mesh['x'=4,'z'=16,'y'=4,'c'=2] {'y'}, dimensions={0}, use_global_device_ids=true | all-gather | bytes 819200 | tf_op jit(solution)/shard_map/gather_raised/all_gather | solution.py:61
  90.1 0.9 all-to-all-done.3
  91.1 0.1 slice_reduce_fusion
  91.3 0.6 broadcast_in_dim.40
  91.9 5.3 %all-to-all-start.4 = ((f32[8,1,256]{2,1,0:T(1,128)}), f32[8,1,256]{2,1,0:T(1,128)S(1)}, u32[]{:S(2)}, u32[]{:S(2)}) async-start(f32[8,1,256]{2,1,0:T(1,128)} %broadcast_in_dim.40), calls=%async_computation.4 | async-start | bytes 16384 | tf_op jit(solution)/shard_map/statistics/all_to_all | solution.py:31
  97.2 2.1 %collective-permute-start.1 = (bf16[256,1280]{1,0:T(8,128)(2,1)S(1)}, bf16[256,1280]{1,0:T(8,128)(2,1)}, u32[]{:S(2)}, u32[]{:S(2)}) collective-permute-start(bf16[256,1280]{1,0:T(8,128)(2,1)S(1)} %all_gather.3), channel_id=1, source_target_pairs={{0,1},{1,0},{2,3},{3,2},{4,5},{5,4},{6,7},{7,6},{8,9},{9,8},{10,11... | collective-permute-start | bytes 1966088 | tf_op jit(solution)/shard_map/gather_raised/ppermute | solution.py:30
  99.3 1.2 all-to-all-done.4
  100.8 0.7 fusion.8
  101.6 1.2 broadcast_select_fusion.1
  102.8 1.5 convolution_convert_fusion.2
  104.2 14.3 %all_to_all.44 = f16[4,128,640]{2,1,0:T(8,128)(2,1)S(1)} all-to-all(f16[4,128,640]{2,1,0:T(8,128)(2,1)S(1)} %bitcast.18), channel_id=1, replica_groups=mesh['x'=4,'z'=16,'y'=4,'c'=2] {'x'}, dimensions={0} | all-to-all | bytes 1310720 | tf_op jit(solution)/shard_map/scatter_hidden_grad/all_to_all | solution.py:31
  118.5 0.1 convert_reduce_fusion
  118.6 0.7 convert_bitcast_fusion
  119.3 11.7 %all-to-all-start.6 = ((f16[16,8,640]{2,1,0:T(8,128)(2,1)}), f16[16,8,640]{2,1,0:T(8,128)(2,1)S(1)}, u32[]{:S(2)}, u32[]{:S(2)}) async-start(f16[16,8,640]{2,1,0:T(8,128)(2,1)} %convert_bitcast_fusion), calls=%async_computation.6 | async-start | bytes 327680 | tf_op jit(solution)/shard_map/scatter_hidden_grad/all_to_all | solution.py:31
  131.0 3.8 %convolution_convert_fusion = bf16[1280,640]{1,0:T(8,128)(2,1)} fusion(bf16[512,640]{1,0:T(8,128)(2,1)S(1)} %bitcast.17, bf16[256,1280]{1,0:T(8,128)(2,1)} %copy-done.3, bf16[256,1280]{1,0:T(8,128)(2,1)S(1)} %copy-done.2, f32[512]{0:T(512)S(1)} %maximum_multiply_fusion.1, f32[512]{0:T(512)S(1)} %copy-done.6, s32[512]{0:T(512)S(1)} %broadcast_subtract_fusion), kind=kOutput, calls=%fused_computation | convolution fusion | flops 845578240 | bytes 3610624 | tf_op jit(solution)/shard_map/products/dot_general | solution.py:83
  134.7 10.9 %all-to-all-done.6 = f16[16,8,640]{2,1,0:T(8,128)(2,1)S(1)} async-done(((f16[16,8,640]{2,1,0:T(8,128)(2,1)}), f16[16,8,640]{2,1,0:T(8,128)(2,1)S(1)}, u32[]{:S(2)}, u32[]{:S(2)}) %all-to-all-start.6) | async-done | bytes 163872 | tf_op jit(solution)/shard_map/scatter_hidden_grad/all_to_all | solution.py:31
  145.6 0.6 convert_reduce_fusion.2
  (30 shorter events, 0.9 us)
Async XLA Ops:
  0.6 45.5 %copy-start = (bf16[1280,640]{1,0:T(8,128)(2,1)S(1)}, bf16[1280,640]{1,0:T(8,128)(2,1)}, u32[]{:S(2)}) copy-start(bf16[1280,640]{1,0:T(8,128)(2,1)} %param.6) | copy-start | bytes 4915204
  33.0 13.1 %all-to-all-start.1 = ((bf16[4,128,640]{2,1,0:T(8,128)(2,1)}), bf16[4,128,640]{2,1,0:T(8,128)(2,1)S(1)}, u32[]{:S(2)}, u32[]{:S(2)}) async-start(bf16[4,128,640]{2,1,0:T(8,128)(2,1)} %broadcast_in_dim.37), calls=%async_computation.1 | async-start | bytes 1310720 | tf_op jit(solution)/shard_map/gather_hidden/all_to_all | solution.py:14
  46.8 4.1 %collective-permute-start = (f16[256,1280]{1,0:T(8,128)(2,1)S(1)}, f16[256,1280]{1,0:T(8,128)(2,1)}, u32[]{:S(2)}, u32[]{:S(2)}) collective-permute-start(f16[256,1280]{1,0:T(8,128)(2,1)S(1)} %convolution_convert_fusion.1), channel_id=1, source_target_pairs={{0,1},{1,0},{2,3},{3,2},{4,5},{5,4},{6,7},{7,6},{8,9},{9,8},{10,11... | collective-permute-start | bytes 1966088 | tf_op jit(solution)/shard_map/logits/ppermute | solution.py:30
  48.7 9.5 %copy-start.4 = (s32[512]{0:T(512)S(1)}, s32[512]{0:T(512)}, u32[]{:S(2)}) copy-start(s32[512]{0:T(512)} %param.7) | copy-start | bytes 6148
  53.6 13.8 %all-to-all-start.2 = ((f16[4,64,1280]{2,1,0:T(8,128)(2,1)}), f16[4,64,1280]{2,1,0:T(8,128)(2,1)S(1)}, u32[]{:S(2)}, u32[]{:S(2)}) async-start(f16[4,64,1280]{2,1,0:T(8,128)(2,1)} %bitcast.2), calls=%async_computation.2 | async-start | bytes 1310720 | tf_op jit(solution)/shard_map/logits/all_to_all | solution.py:31
  58.2 42.6 %copy-start.5 = (s32[512]{0:T(512)S(1)}, s32[512]{0:T(512)}, u32[]{:S(2)}) copy-start(s32[512]{0:T(512)} %param.8) | copy-start | bytes 6148
  58.3 42.6 %copy-start.6 = (f32[512]{0:T(512)S(1)}, f32[512]{0:T(512)}, u32[]{:S(2)}) copy-start(f32[512]{0:T(512)} %param.9) | copy-start | bytes 6148
  68.6 22.5 %all-to-all-start.3 = ((f32[64,1,128]{2,1,0:T(1,128)}), f32[64,1,128]{2,1,0:T(1,128)S(1)}, u32[]{:S(2)}, u32[]{:S(2)}) async-start(f32[64,1,128]{2,1,0:T(1,128)} %broadcast_in_dim.39), calls=%async_computation.3 | async-start | bytes 65536 | tf_op jit(solution)/shard_map/statistics/all_to_all | solution.py:31
  91.9 8.5 %all-to-all-start.4 = ((f32[8,1,256]{2,1,0:T(1,128)}), f32[8,1,256]{2,1,0:T(1,128)S(1)}, u32[]{:S(2)}, u32[]{:S(2)}) async-start(f32[8,1,256]{2,1,0:T(1,128)} %broadcast_in_dim.40), calls=%async_computation.4 | async-start | bytes 16384 | tf_op jit(solution)/shard_map/statistics/all_to_all | solution.py:31
  97.2 4.3 %collective-permute-start.1 = (bf16[256,1280]{1,0:T(8,128)(2,1)S(1)}, bf16[256,1280]{1,0:T(8,128)(2,1)}, u32[]{:S(2)}, u32[]{:S(2)}) collective-permute-start(bf16[256,1280]{1,0:T(8,128)(2,1)S(1)} %all_gather.3), channel_id=1, source_target_pairs={{0,1},{1,0},{2,3},{3,2},{4,5},{5,4},{6,7},{7,6},{8,9},{9,8},{10,11... | collective-permute-start | bytes 1966088 | tf_op jit(solution)/shard_map/gather_raised/ppermute | solution.py:30
  102.7 1.5 %copy-start.1 = (bf16[256,1280]{1,0:T(8,128)(2,1)}, bf16[256,1280]{1,0:T(8,128)(2,1)S(1)}, u32[]{:S(2)}) copy-start(bf16[256,1280]{1,0:T(8,128)(2,1)S(1)} %get-tuple-element.11) | copy-start | bytes 1966084
  102.7 1.5 %copy-start.3 = (bf16[256,1280]{1,0:T(8,128)(2,1)}, bf16[256,1280]{1,0:T(8,128)(2,1)S(1)}, u32[]{:S(2)}) copy-start(bf16[256,1280]{1,0:T(8,128)(2,1)S(1)} %get-tuple-element.12) | copy-start | bytes 1966084
  118.5 12.4 %copy-start.2 = (bf16[256,1280]{1,0:T(8,128)(2,1)S(1)}, bf16[256,1280]{1,0:T(8,128)(2,1)}, u32[]{:S(2)}) copy-start(bf16[256,1280]{1,0:T(8,128)(2,1)} %copy-done.1) | copy-start | bytes 1966084
  119.3 26.3 %all-to-all-start.6 = ((f16[16,8,640]{2,1,0:T(8,128)(2,1)}), f16[16,8,640]{2,1,0:T(8,128)(2,1)S(1)}, u32[]{:S(2)}, u32[]{:S(2)}) async-start(f16[16,8,640]{2,1,0:T(8,128)(2,1)} %convert_bitcast_fusion), calls=%async_computation.6 | async-start | bytes 327680 | tf_op jit(solution)/shard_map/scatter_hidden_grad/all_to_all | solution.py:31

commit v5 on v4

--- a/solution.py
+++ b/solution.py
@@ -13,6 +13,16 @@
     copies = jnp.broadcast_to(block, (lax.axis_size(axis), *block.shape))
     copies = lax.all_to_all(copies, axis, 0, 0, tiled=True)
     return copies.reshape(-1, block.shape[-1])
+
+
+def gather_by_pairs(block, axis):
+    me = lax.axis_index(axis)
+    by_pair = [block]
+    for other in range(1, 4):
+        by_pair.append(lax.ppermute(block, axis, [(i, i ^ other) for i in range(4)]))
+    odd, late = me % 2 == 1, me >= 2
+    even_first = [jnp.where(odd, by_pair[i ^ 1], by_pair[i]) for i in range(4)]
+    return jnp.stack([jnp.where(late, even_first[i ^ 2], even_first[i]) for i in range(4)])
 
 
 def shards(hidden_states, head_weight, targets, terminal, cotangent):
@@ -45,6 +55,7 @@
         far_l = lax.dot_general(far_h, head_weight, inner, preferred_element_type=f32)
         far_l = swap(far_l.astype(f16))
         near_l = lax.dot_general(near_h, head_weight, inner, preferred_element_type=f32)
+        near_l = lax.optimization_barrier(near_l)
         chip_l = (near_l + far_l.astype(f32)).astype(f16)
         pieces = turn(chip_l.reshape(sz["y"], own, rows), "y")
         logits = jnp.sum(pieces.astype(f32), axis=0)
@@ -58,7 +69,7 @@
         mine = jnp.broadcast_to(mine, (n_vocab, 2 * own))
 
     with jax.named_scope("gather_raised"):
-        near = lax.all_gather(raised.astype(bf16), "y", axis=0, tiled=True)
+        near = gather_by_pairs(raised.astype(bf16), "y").reshape(half, rows)
         far = swap(near)
         raised = jnp.concatenate([jnp.where(is_low, near, far), jnp.where(is_low, far, near)])
 

time: 148 us -> 148 us (level)
  blocking collectives: 58.5 us -> 45 us
  starting transfers between devices: 37.8 us -> 47.7 us
  waiting for transfers between devices: 33 us -> 36.1 us
    all_gather x1 -> x0, blocking collectives: 13.6 us -> none  [shards(): near = lax.all_gather(raised.astype(bf16), 'y', axis=0, tiled=True)]
    ppermute x0 -> x3, starting transfers between devices: none -> 9.82 us  [gather_by_pairs(): lax.ppermute(block, axis, [(i, i ^ other) for i in range(4)])]
    all_to_all x4, waiting for transfers between devices: 22 us -> 25.8 us  [shards(): turn = lambda v, axis: lax.all_to_all(v, axis, 0, 0, tiled=True)]
    dot_general x1, matrix products: 2.64 us -> 0.71 us  [shards(): lax.dot_general(near_h, head_weight, inner, preferred_element_type=f32)]
  transfers between devices with their start and end apart: 7 -> 10, of which waited for: 6 -> 6; matrix products, arithmetic and copies ran while one was open for 3% -> 4% of each run, Pallas kernels for 0% -> 0%
where the time goes in v5:
time: 148 us; the launch traced here: 146 us
  starting transfers between devices  47.7 us (32%)
  blocking collectives  45 us (30%)
  waiting for transfers between devices  36.1 us (24%)
  matrix products  7.48 us (5%)
  other arithmetic  5.32 us (4%)
  local copies, waits for them, and re-layouts  3.39 us (2%)
    all_to_all x1, blocking collectives, spread(): copies = lax.all_to_all(copies, axis, 0, 0, tiled=True)  30.6 us
    all_to_all x4, starting transfers between devices, shards(): turn = lambda v, axis: lax.all_to_all(v, axis, 0, 0, tiled=True)  29.6 us
    all_to_all x4, waiting for transfers between devices, shards(): turn = lambda v, axis: lax.all_to_all(v, axis, 0, 0, tiled=True)  25.8 us
    all_to_all x1, blocking collectives, shards(): turn = lambda v, axis: lax.all_to_all(v, axis, 0, 0, tiled=True)  14.4 us
    ppermute x3, starting transfers between devices, gather_by_pairs(): lax.ppermute(block, axis, [(i, i ^ other) for i in range(4)])  9.82 us
    all_to_all x1, waiting for transfers between devices, spread(): copies = lax.all_to_all(copies, axis, 0, 0, tiled=True)  8.79 us
    all_to_all x1, starting transfers between devices, spread(): copies = lax.all_to_all(copies, axis, 0, 0, tiled=True)  4.29 us
    ppermute x2, starting transfers between devices, shards(): swap = lambda v: lax.ppermute(v, 'c', [(0, 1), (1, 0)])  3.96 us
  transfers between devices with their start and end apart: 10, of which 6 were waited for; matrix products, arithmetic and copies ran while one was open for 4% of the time, Pallas kernels for 0%

profile of v5, /device:TPU:24, one launch (start us, length us, event | category | flops | bytes accessed | tf_op | source)
XLA Modules:
  0.0 145.8 jit_solution(1471428369086148891)
XLA Ops:
  0.6 0.8 broadcast_in_dim.36
  1.5 30.6 %all_to_all.43 = bf16[16,8,640]{2,1,0:T(8,128)(2,1)S(1)} all-to-all(bf16[16,8,640]{2,1,0:T(8,128)(2,1)S(1)} %broadcast_in_dim.36), channel_id=1, replica_groups=mesh['x'=4,'z'=16,'y'=4,'c'=2] {'z'}, dimensions={0} | all-to-all | bytes 327680 | tf_op jit(solution)/shard_map/gather_hidden/all_to_all | solution.py:14
  32.1 0.9 broadcast_in_dim.37
  33.0 4.3 %all-to-all-start.1 = ((bf16[4,128,640]{2,1,0:T(8,128)(2,1)}), bf16[4,128,640]{2,1,0:T(8,128)(2,1)S(1)}, u32[]{:S(2)}, u32[]{:S(2)}) async-start(bf16[4,128,640]{2,1,0:T(8,128)(2,1)} %broadcast_in_dim.37), calls=%async_computation.1 | async-start | bytes 1310720 | tf_op jit(solution)/shard_map/gather_hidden/all_to_all | solution.py:14
  37.3 8.8 %all-to-all-done.1 = bf16[4,128,640]{2,1,0:T(8,128)(2,1)S(1)} async-done(((bf16[4,128,640]{2,1,0:T(8,128)(2,1)}), bf16[4,128,640]{2,1,0:T(8,128)(2,1)S(1)}, u32[]{:S(2)}, u32[]{:S(2)}) %all-to-all-start.1) | async-done | bytes 655392 | tf_op jit(solution)/shard_map/gather_hidden/all_to_all | solution.py:14
  46.1 1.5 %convolution_convert_fusion.1 = f16[256,1280]{1,0:T(8,128)(2,1)} fusion(bf16[1280,640]{1,0:T(8,128)(2,1)S(1)} %copy-done, bf16[512,640]{1,0:T(8,128)(2,1)S(1)} %bitcast.27, s32[]{:T(128)S(6)} %select_n.75), kind=kOutput, calls=%fused_computation.3 | convolution fusion | flops 419758080 | bytes 2621444 | tf_op jit(solution)/shard_map/logits/dot_general | solution.py:55
  47.6 1.9 %collective-permute-start = (f16[256,1280]{1,0:T(8,128)(2,1)}, f16[256,1280]{1,0:T(8,128)(2,1)S(1)}, u32[]{:S(2)}, u32[]{:S(2)}) collective-permute-start(f16[256,1280]{1,0:T(8,128)(2,1)} %convolution_convert_fusion.1), channel_id=1, source_target_pairs={{0,1},{1,0},{2,3},{3,2},{4,5},{5,4},{6,7},{7,6},{8,9},{9,8},{10,11... | collective-permute-start | bytes 1966088 | tf_op jit(solution)/shard_map/logits/ppermute | solution.py:40
  49.6 0.7 fusion.1
  50.3 1.5 %collective-permute-done = f16[256,1280]{1,0:T(8,128)(2,1)S(1)} collective-permute-done((f16[256,1280]{1,0:T(8,128)(2,1)}, f16[256,1280]{1,0:T(8,128)(2,1)S(1)}, u32[]{:S(2)}, u32[]{:S(2)}) %collective-permute-start) | collective-permute-done | bytes 655392 | tf_op jit(solution)/shard_map/logits/ppermute | solution.py:40
  51.8 1.0 add_convert_fusion
  52.9 4.7 %all-to-all-start.2 = ((f16[4,64,1280]{2,1,0:T(8,128)(2,1)}), f16[4,64,1280]{2,1,0:T(8,128)(2,1)S(1)}, u32[]{:S(2)}, u32[]{:S(2)}) async-start(f16[4,64,1280]{2,1,0:T(8,128)(2,1)} %bitcast.2), calls=%async_computation.2 | async-start | bytes 1310720 | tf_op jit(solution)/shard_map/logits/all_to_all | solution.py:41
  57.6 9.0 %all-to-all-done.2 = f16[4,64,1280]{2,1,0:T(8,128)(2,1)S(1)} async-done(((f16[4,64,1280]{2,1,0:T(8,128)(2,1)}), f16[4,64,1280]{2,1,0:T(8,128)(2,1)S(1)}, u32[]{:S(2)}, u32[]{:S(2)}) %all-to-all-start.2) | async-done | bytes 655392 | tf_op jit(solution)/shard_map/logits/all_to_all | solution.py:41
  66.9 0.2 fusion.4
  67.2 0.6 broadcast_in_dim.39
  67.9 7.9 %all-to-all-start.3 = ((f32[64,1,128]{2,1,0:T(1,128)}), f32[64,1,128]{2,1,0:T(1,128)S(1)}, u32[]{:S(2)}, u32[]{:S(2)}) async-start(f32[64,1,128]{2,1,0:T(1,128)} %broadcast_in_dim.39), calls=%async_computation.3 | async-start | bytes 65536 | tf_op jit(solution)/shard_map/statistics/all_to_all | solution.py:41
  75.8 4.0 %collective-permute-start.1 = (bf16[64,1280]{1,0:T(8,128)(2,1)S(1)}, bf16[64,1280]{1,0:T(8,128)(2,1)S(1)}, u32[]{:S(2)}, u32[]{:S(2)}) collective-permute-start(bf16[64,1280]{1,0:T(8,128)(2,1)S(1)} %get-tuple-element.17), channel_id=1, source_target_pairs={{0,6},{2,4},{4,2},{6,0},{1,7},{3,5},{5,3},{7,1},{8,14},{10,12},{12... | collective-permute-start | bytes 491528 | tf_op jit(solution)/shard_map/gather_raised/ppermute | solution.py:22
  79.8 1.9 %collective-permute-start.2 = (bf16[64,1280]{1,0:T(8,128)(2,1)S(1)}, bf16[64,1280]{1,0:T(8,128)(2,1)S(1)}, u32[]{:S(2)}, u32[]{:S(2)}) collective-permute-start(bf16[64,1280]{1,0:T(8,128)(2,1)S(1)} %get-tuple-element.17), channel_id=1, source_target_pairs={{0,4},{2,6},{4,0},{6,2},{1,5},{3,7},{5,1},{7,3},{8,12},{10,14},{12... | collective-permute-start | bytes 491528 | tf_op jit(solution)/shard_map/gather_raised/ppermute | solution.py:22
  81.7 3.9 %collective-permute-start.3 = (bf16[64,1280]{1,0:T(8,128)(2,1)S(1)}, bf16[64,1280]{1,0:T(8,128)(2,1)S(1)}, u32[]{:S(2)}, u32[]{:S(2)}) collective-permute-start(bf16[64,1280]{1,0:T(8,128)(2,1)S(1)} %get-tuple-element.17), channel_id=1, source_target_pairs={{0,2},{2,0},{4,6},{6,4},{1,3},{3,1},{5,7},{7,5},{8,10},{10,8},{12,... | collective-permute-start | bytes 491528 | tf_op jit(solution)/shard_map/gather_raised/ppermute | solution.py:22
  85.7 4.7 %all-to-all-done.3 = f32[64,1,128]{2,1,0:T(1,128)S(1)} async-done(((f32[64,1,128]{2,1,0:T(1,128)}), f32[64,1,128]{2,1,0:T(1,128)S(1)}, u32[]{:S(2)}, u32[]{:S(2)}) %all-to-all-start.3) | async-done | bytes 32800 | tf_op jit(solution)/shard_map/statistics/all_to_all | solution.py:41
  90.8 0.6 broadcast_in_dim.40
  91.4 5.3 %all-to-all-start.4 = ((f32[8,1,256]{2,1,0:T(1,128)}), f32[8,1,256]{2,1,0:T(1,128)S(1)}, u32[]{:S(2)}, u32[]{:S(2)}) async-start(f32[8,1,256]{2,1,0:T(1,128)} %broadcast_in_dim.40), calls=%async_computation.4 | async-start | bytes 16384 | tf_op jit(solution)/shard_map/statistics/all_to_all | solution.py:41
  96.7 2.1 %collective-permute-start.4 = (bf16[256,1280]{1,0:T(8,128)(2,1)S(1)}, bf16[256,1280]{1,0:T(8,128)(2,1)}, u32[]{:S(2)}, u32[]{:S(2)}) collective-permute-start(bf16[256,1280]{1,0:T(8,128)(2,1)S(1)} %bitcast.26), channel_id=1, source_target_pairs={{0,1},{1,0},{2,3},{3,2},{4,5},{5,4},{6,7},{7,6},{8,9},{9,8},{10,11... | collective-permute-start | bytes 1966088 | tf_op jit(solution)/shard_map/gather_raised/ppermute | solution.py:40
  98.8 1.2 all-to-all-done.4
  100.3 0.7 fusion.6
  101.0 1.2 broadcast_select_fusion.1
  102.2 1.5 %convolution_convert_fusion.2 = f16[512,640]{1,0:T(8,128)(2,1)S(1)} fusion(bf16[1280,640]{1,0:T(8,128)(2,1)S(1)} %copy-done, bf16[256,1280]{1,0:T(8,128)(2,1)S(1)} %get-tuple-element.12, bf16[256,1280]{1,0:T(8,128)(2,1)S(1)} %get-tuple-element.11, f32[512]{0:T(512)S(1)} %maximum_multiply_fusion.1, f32[512]{0:T(512)S(1)} %copy-done.6, ...), kind=kOutput, calls=%fused_computation.4 | convolution fusion | flops 845086720 | bytes 3610624 | tf_op jit(solution)/shard_map/products/dot_general | solution.py:92
  103.7 14.4 %all_to_all.44 = f16[4,128,640]{2,1,0:T(8,128)(2,1)S(1)} all-to-all(f16[4,128,640]{2,1,0:T(8,128)(2,1)S(1)} %bitcast.30), channel_id=1, replica_groups=mesh['x'=4,'z'=16,'y'=4,'c'=2] {'x'}, dimensions={0} | all-to-all | bytes 1310720 | tf_op jit(solution)/shard_map/scatter_hidden_grad/all_to_all | solution.py:41
  118.2 0.7 convert_bitcast_fusion
  118.9 11.7 %all-to-all-start.6 = ((f16[16,8,640]{2,1,0:T(8,128)(2,1)}), f16[16,8,640]{2,1,0:T(8,128)(2,1)S(1)}, u32[]{:S(2)}, u32[]{:S(2)}) async-start(f16[16,8,640]{2,1,0:T(8,128)(2,1)} %convert_bitcast_fusion), calls=%async_computation.6 | async-start | bytes 327680 | tf_op jit(solution)/shard_map/scatter_hidden_grad/all_to_all | solution.py:41
  130.6 3.8 %convolution_convert_fusion = bf16[1280,640]{1,0:T(8,128)(2,1)} fusion(bf16[512,640]{1,0:T(8,128)(2,1)S(1)} %bitcast.29, bf16[256,1280]{1,0:T(8,128)(2,1)} %copy-done.3, bf16[256,1280]{1,0:T(8,128)(2,1)S(1)} %copy-done.2, f32[512]{0:T(512)S(1)} %maximum_multiply_fusion.1, f32[512]{0:T(512)S(1)} %copy-done.6, s32[512]{0:T(512)S(1)} %broadcast_subtract_fusion), kind=kOutput, calls=%fused_computation | convolution fusion | flops 845578240 | bytes 3610624 | tf_op jit(solution)/shard_map/products/dot_general | solution.py:94
  134.3 10.9 %all-to-all-done.6 = f16[16,8,640]{2,1,0:T(8,128)(2,1)S(1)} async-done(((f16[16,8,640]{2,1,0:T(8,128)(2,1)}), f16[16,8,640]{2,1,0:T(8,128)(2,1)S(1)}, u32[]{:S(2)}, u32[]{:S(2)}) %all-to-all-start.6) | async-done | bytes 163872 | tf_op jit(solution)/shard_map/scatter_hidden_grad/all_to_all | solution.py:41
  145.2 0.6 convert_reduce_fusion.2
  (38 shorter events, 1.3 us)
Async XLA Ops:
  0.6 45.5 %copy-start = (bf16[1280,640]{1,0:T(8,128)(2,1)S(1)}, bf16[1280,640]{1,0:T(8,128)(2,1)}, u32[]{:S(2)}) copy-start(bf16[1280,640]{1,0:T(8,128)(2,1)} %param.6) | copy-start | bytes 4915204
  33.0 13.1 %all-to-all-start.1 = ((bf16[4,128,640]{2,1,0:T(8,128)(2,1)}), bf16[4,128,640]{2,1,0:T(8,128)(2,1)S(1)}, u32[]{:S(2)}, u32[]{:S(2)}) async-start(bf16[4,128,640]{2,1,0:T(8,128)(2,1)} %broadcast_in_dim.37), calls=%async_computation.1 | async-start | bytes 1310720 | tf_op jit(solution)/shard_map/gather_hidden/all_to_all | solution.py:14
  47.6 4.2 %collective-permute-start = (f16[256,1280]{1,0:T(8,128)(2,1)}, f16[256,1280]{1,0:T(8,128)(2,1)S(1)}, u32[]{:S(2)}, u32[]{:S(2)}) collective-permute-start(f16[256,1280]{1,0:T(8,128)(2,1)} %convolution_convert_fusion.1), channel_id=1, source_target_pairs={{0,1},{1,0},{2,3},{3,2},{4,5},{5,4},{6,7},{7,6},{8,9},{9,8},{10,11... | collective-permute-start | bytes 1966088 | tf_op jit(solution)/shard_map/logits/ppermute | solution.py:40
  50.3 7.3 %copy-start.4 = (s32[512]{0:T(512)S(1)}, s32[512]{0:T(512)}, u32[]{:S(2)}) copy-start(s32[512]{0:T(512)} %param.7) | copy-start | bytes 6148
  52.9 13.8 %all-to-all-start.2 = ((f16[4,64,1280]{2,1,0:T(8,128)(2,1)}), f16[4,64,1280]{2,1,0:T(8,128)(2,1)S(1)}, u32[]{:S(2)}, u32[]{:S(2)}) async-start(f16[4,64,1280]{2,1,0:T(8,128)(2,1)} %bitcast.2), calls=%async_computation.2 | async-start | bytes 1310720 | tf_op jit(solution)/shard_map/logits/all_to_all | solution.py:41
  66.9 33.4 %copy-start.5 = (s32[512]{0:T(512)S(1)}, s32[512]{0:T(512)}, u32[]{:S(2)}) copy-start(s32[512]{0:T(512)} %param.8) | copy-start | bytes 6148
  66.9 33.4 %copy-start.6 = (f32[512]{0:T(512)S(1)}, f32[512]{0:T(512)}, u32[]{:S(2)}) copy-start(f32[512]{0:T(512)} %param.9) | copy-start | bytes 6148
  67.9 22.5 %all-to-all-start.3 = ((f32[64,1,128]{2,1,0:T(1,128)}), f32[64,1,128]{2,1,0:T(1,128)S(1)}, u32[]{:S(2)}, u32[]{:S(2)}) async-start(f32[64,1,128]{2,1,0:T(1,128)} %broadcast_in_dim.39), calls=%async_computation.3 | async-start | bytes 65536 | tf_op jit(solution)/shard_map/statistics/all_to_all | solution.py:41
  75.8 14.8 %collective-permute-start.1 = (bf16[64,1280]{1,0:T(8,128)(2,1)S(1)}, bf16[64,1280]{1,0:T(8,128)(2,1)S(1)}, u32[]{:S(2)}, u32[]{:S(2)}) collective-permute-start(bf16[64,1280]{1,0:T(8,128)(2,1)S(1)} %get-tuple-element.17), channel_id=1, source_target_pairs={{0,6},{2,4},{4,2},{6,0},{1,7},{3,5},{5,3},{7,1},{8,14},{10,12},{12... | collective-permute-start | bytes 491528 | tf_op jit(solution)/shard_map/gather_raised/ppermute | solution.py:22
  79.8 10.8 %collective-permute-start.2 = (bf16[64,1280]{1,0:T(8,128)(2,1)S(1)}, bf16[64,1280]{1,0:T(8,128)(2,1)S(1)}, u32[]{:S(2)}, u32[]{:S(2)}) collective-permute-start(bf16[64,1280]{1,0:T(8,128)(2,1)S(1)} %get-tuple-element.17), channel_id=1, source_target_pairs={{0,4},{2,6},{4,0},{6,2},{1,5},{3,7},{5,1},{7,3},{8,12},{10,14},{12... | collective-permute-start | bytes 491528 | tf_op jit(solution)/shard_map/gather_raised/ppermute | solution.py:22
  81.7 8.9 %collective-permute-start.3 = (bf16[64,1280]{1,0:T(8,128)(2,1)S(1)}, bf16[64,1280]{1,0:T(8,128)(2,1)S(1)}, u32[]{:S(2)}, u32[]{:S(2)}) collective-permute-start(bf16[64,1280]{1,0:T(8,128)(2,1)S(1)} %get-tuple-element.17), channel_id=1, source_target_pairs={{0,2},{2,0},{4,6},{6,4},{1,3},{3,1},{5,7},{7,5},{8,10},{10,8},{12,... | collective-permute-start | bytes 491528 | tf_op jit(solution)/shard_map/gather_raised/ppermute | solution.py:22
  91.4 8.5 %all-to-all-start.4 = ((f32[8,1,256]{2,1,0:T(1,128)}), f32[8,1,256]{2,1,0:T(1,128)S(1)}, u32[]{:S(2)}, u32[]{:S(2)}) async-start(f32[8,1,256]{2,1,0:T(1,128)} %broadcast_in_dim.40), calls=%async_computation.4 | async-start | bytes 16384 | tf_op jit(solution)/shard_map/statistics/all_to_all | solution.py:41
  96.7 4.3 %collective-permute-start.4 = (bf16[256,1280]{1,0:T(8,128)(2,1)S(1)}, bf16[256,1280]{1,0:T(8,128)(2,1)}, u32[]{:S(2)}, u32[]{:S(2)}) collective-permute-start(bf16[256,1280]{1,0:T(8,128)(2,1)S(1)} %bitcast.26), channel_id=1, source_target_pairs={{0,1},{1,0},{2,3},{3,2},{4,5},{5,4},{6,7},{7,6},{8,9},{9,8},{10,11... | collective-permute-start | bytes 1966088 | tf_op jit(solution)/shard_map/gather_raised/ppermute | solution.py:40
  102.2 1.5 %copy-start.1 = (bf16[256,1280]{1,0:T(8,128)(2,1)}, bf16[256,1280]{1,0:T(8,128)(2,1)S(1)}, u32[]{:S(2)}) copy-start(bf16[256,1280]{1,0:T(8,128)(2,1)S(1)} %get-tuple-element.11) | copy-start | bytes 1966084
  102.2 1.5 %copy-start.3 = (bf16[256,1280]{1,0:T(8,128)(2,1)}, bf16[256,1280]{1,0:T(8,128)(2,1)S(1)}, u32[]{:S(2)}) copy-start(bf16[256,1280]{1,0:T(8,128)(2,1)S(1)} %get-tuple-element.12) | copy-start | bytes 1966084
  118.1 12.5 %copy-start.2 = (bf16[256,1280]{1,0:T(8,128)(2,1)S(1)}, bf16[256,1280]{1,0:T(8,128)(2,1)}, u32[]{:S(2)}) copy-start(bf16[256,1280]{1,0:T(8,128)(2,1)} %copy-done.1) | copy-start | bytes 1966084
  118.9 26.3 %all-to-all-start.6 = ((f16[16,8,640]{2,1,0:T(8,128)(2,1)}), f16[16,8,640]{2,1,0:T(8,128)(2,1)S(1)}, u32[]{:S(2)}, u32[]{:S(2)}) async-start(f16[16,8,640]{2,1,0:T(8,128)(2,1)} %convert_bitcast_fusion), calls=%async_computation.6 | async-start | bytes 327680 | tf_op jit(solution)/shard_map/scatter_hidden_grad/all_to_all | solution.py:41

commit v6 on v4

--- a/solution.py
+++ b/solution.py
@@ -45,6 +45,7 @@
         far_l = lax.dot_general(far_h, head_weight, inner, preferred_element_type=f32)
         far_l = swap(far_l.astype(f16))
         near_l = lax.dot_general(near_h, head_weight, inner, preferred_element_type=f32)
+        near_l = lax.optimization_barrier(near_l)
         chip_l = (near_l + far_l.astype(f32)).astype(f16)
         pieces = turn(chip_l.reshape(sz["y"], own, rows), "y")
         logits = jnp.sum(pieces.astype(f32), axis=0)

time: 148 us -> 148 us (level)
    dot_general x1, matrix products: 2.64 us -> 0.71 us  [shards(): lax.dot_general(near_h, head_weight, inner, preferred_element_type=f32)]
  transfers between devices with their start and end apart: 7 -> 7, of which waited for: 6 -> 6; matrix products, arithmetic and copies ran while one was open for 3% -> 4% of each run, Pallas kernels for 0% -> 0%
where the time goes in v6:
time: 148 us; the launch traced here: 146 us
  blocking collectives  58.5 us (40%)
  starting transfers between devices  37.8 us (26%)
  waiting for transfers between devices  32.3 us (22%)
  matrix products  7.48 us (5%)
  other arithmetic  5.17 us (3%)
  local copies, waits for them, and re-layouts  3.4 us (2%)
    all_to_all x1, blocking collectives, spread(): copies = lax.all_to_all(copies, axis, 0, 0, tiled=True)  30.6 us
    all_to_all x4, starting transfers between devices, shards(): turn = lambda v, axis: lax.all_to_all(v, axis, 0, 0, tiled=True)  29.6 us
    all_to_all x4, waiting for transfers between devices, shards(): turn = lambda v, axis: lax.all_to_all(v, axis, 0, 0, tiled=True)  22 us
    all_to_all x1, blocking collectives, shards(): turn = lambda v, axis: lax.all_to_all(v, axis, 0, 0, tiled=True)  14.3 us
    all_gather x1, blocking collectives, shards(): near = lax.all_gather(raised.astype(bf16), 'y', axis=0, tiled=True)  13.6 us
    all_to_all x1, waiting for transfers between devices, spread(): copies = lax.all_to_all(copies, axis, 0, 0, tiled=True)  8.79 us
    all_to_all x1, starting transfers between devices, spread(): copies = lax.all_to_all(copies, axis, 0, 0, tiled=True)  4.29 us
    ppermute x2, starting transfers between devices, shards(): swap = lambda v: lax.ppermute(v, 'c', [(0, 1), (1, 0)])  3.96 us
  transfers between devices with their start and end apart: 7, of which 6 were waited for; matrix products, arithmetic and copies ran while one was open for 4% of the time, Pallas kernels for 0%

profile of v6, /device:TPU:24, one launch (start us, length us, event | category | flops | bytes accessed | tf_op | source)
XLA Modules:
  0.0 145.5 jit_solution(6446871161254759329)
XLA Ops:
  0.6 0.8 broadcast_in_dim.36
  1.5 30.6 %all_to_all.43 = bf16[16,8,640]{2,1,0:T(8,128)(2,1)S(1)} all-to-all(bf16[16,8,640]{2,1,0:T(8,128)(2,1)S(1)} %broadcast_in_dim.36), channel_id=1, replica_groups=mesh['x'=4,'z'=16,'y'=4,'c'=2] {'z'}, dimensions={0} | all-to-all | bytes 327680 | tf_op jit(solution)/shard_map/gather_hidden/all_to_all | solution.py:14
  32.1 0.9 broadcast_in_dim.37
  33.0 4.3 %all-to-all-start.1 = ((bf16[4,128,640]{2,1,0:T(8,128)(2,1)}), bf16[4,128,640]{2,1,0:T(8,128)(2,1)S(1)}, u32[]{:S(2)}, u32[]{:S(2)}) async-start(bf16[4,128,640]{2,1,0:T(8,128)(2,1)} %broadcast_in_dim.37), calls=%async_computation.1 | async-start | bytes 1310720 | tf_op jit(solution)/shard_map/gather_hidden/all_to_all | solution.py:14
  37.3 8.8 %all-to-all-done.1 = bf16[4,128,640]{2,1,0:T(8,128)(2,1)S(1)} async-done(((bf16[4,128,640]{2,1,0:T(8,128)(2,1)}), bf16[4,128,640]{2,1,0:T(8,128)(2,1)S(1)}, u32[]{:S(2)}, u32[]{:S(2)}) %all-to-all-start.1) | async-done | bytes 655392 | tf_op jit(solution)/shard_map/gather_hidden/all_to_all | solution.py:14
  46.1 1.5 %convolution_convert_fusion.1 = f16[256,1280]{1,0:T(8,128)(2,1)} fusion(bf16[1280,640]{1,0:T(8,128)(2,1)S(1)} %copy-done, bf16[512,640]{1,0:T(8,128)(2,1)S(1)} %bitcast.15, s32[]{:T(128)S(6)} %select_n.30), kind=kOutput, calls=%fused_computation.3 | convolution fusion | flops 419758080 | bytes 2621444 | tf_op jit(solution)/shard_map/logits/dot_general | solution.py:45
  47.6 1.9 %collective-permute-start = (f16[256,1280]{1,0:T(8,128)(2,1)}, f16[256,1280]{1,0:T(8,128)(2,1)S(1)}, u32[]{:S(2)}, u32[]{:S(2)}) collective-permute-start(f16[256,1280]{1,0:T(8,128)(2,1)} %convolution_convert_fusion.1), channel_id=1, source_target_pairs={{0,1},{1,0},{2,3},{3,2},{4,5},{5,4},{6,7},{7,6},{8,9},{9,8},{10,11... | collective-permute-start | bytes 1966088 | tf_op jit(solution)/shard_map/logits/ppermute | solution.py:30
  49.6 0.7 fusion.1
  50.3 1.5 %collective-permute-done = f16[256,1280]{1,0:T(8,128)(2,1)S(1)} collective-permute-done((f16[256,1280]{1,0:T(8,128)(2,1)}, f16[256,1280]{1,0:T(8,128)(2,1)S(1)}, u32[]{:S(2)}, u32[]{:S(2)}) %collective-permute-start) | collective-permute-done | bytes 655392 | tf_op jit(solution)/shard_map/logits/ppermute | solution.py:30
  51.8 1.0 add_convert_fusion
  52.9 4.7 %all-to-all-start.2 = ((f16[4,64,1280]{2,1,0:T(8,128)(2,1)}), f16[4,64,1280]{2,1,0:T(8,128)(2,1)S(1)}, u32[]{:S(2)}, u32[]{:S(2)}) async-start(f16[4,64,1280]{2,1,0:T(8,128)(2,1)} %bitcast.2), calls=%async_computation.2 | async-start | bytes 1310720 | tf_op jit(solution)/shard_map/logits/all_to_all | solution.py:31
  57.6 9.0 %all-to-all-done.2 = f16[4,64,1280]{2,1,0:T(8,128)(2,1)S(1)} async-done(((f16[4,64,1280]{2,1,0:T(8,128)(2,1)}), f16[4,64,1280]{2,1,0:T(8,128)(2,1)S(1)}, u32[]{:S(2)}, u32[]{:S(2)}) %all-to-all-start.2) | async-done | bytes 655392 | tf_op jit(solution)/shard_map/logits/all_to_all | solution.py:31
  66.8 0.1 reduce_max.18
  66.9 0.3 fusion.4
  67.2 0.6 broadcast_in_dim.39
  67.9 7.9 %all-to-all-start.3 = ((f32[64,1,128]{2,1,0:T(1,128)}), f32[64,1,128]{2,1,0:T(1,128)S(1)}, u32[]{:S(2)}, u32[]{:S(2)}) async-start(f32[64,1,128]{2,1,0:T(1,128)} %broadcast_in_dim.39), calls=%async_computation.3 | async-start | bytes 65536 | tf_op jit(solution)/shard_map/statistics/all_to_all | solution.py:31
  75.8 13.6 %all_gather.3 = bf16[256,1280]{1,0:T(8,128)(2,1)S(1)} all-gather(bf16[64,1280]{1,0:T(8,128)(2,1)S(1)} %get-tuple-element.13), channel_id=1, replica_groups=mesh['x'=4,'z'=16,'y'=4,'c'=2] {'y'}, dimensions={0}, use_global_device_ids=true | all-gather | bytes 819200 | tf_op jit(solution)/shard_map/gather_raised/all_gather | solution.py:62
  89.4 0.9 all-to-all-done.3
  90.4 0.1 slice_reduce_fusion
  90.6 0.6 broadcast_in_dim.40
  91.2 5.3 %all-to-all-start.4 = ((f32[8,1,256]{2,1,0:T(1,128)}), f32[8,1,256]{2,1,0:T(1,128)S(1)}, u32[]{:S(2)}, u32[]{:S(2)}) async-start(f32[8,1,256]{2,1,0:T(1,128)} %broadcast_in_dim.40), calls=%async_computation.4 | async-start | bytes 16384 | tf_op jit(solution)/shard_map/statistics/all_to_all | solution.py:31
  96.5 2.1 %collective-permute-start.1 = (bf16[256,1280]{1,0:T(8,128)(2,1)S(1)}, bf16[256,1280]{1,0:T(8,128)(2,1)}, u32[]{:S(2)}, u32[]{:S(2)}) collective-permute-start(bf16[256,1280]{1,0:T(8,128)(2,1)S(1)} %all_gather.3), channel_id=1, source_target_pairs={{0,1},{1,0},{2,3},{3,2},{4,5},{5,4},{6,7},{7,6},{8,9},{9,8},{10,11... | collective-permute-start | bytes 1966088 | tf_op jit(solution)/shard_map/gather_raised/ppermute | solution.py:30
  98.6 1.2 all-to-all-done.4
  100.1 0.7 fusion.6
  100.9 1.2 broadcast_select_fusion.1
  102.1 1.5 %convolution_convert_fusion.2 = f16[512,640]{1,0:T(8,128)(2,1)S(1)} fusion(bf16[1280,640]{1,0:T(8,128)(2,1)S(1)} %copy-done, bf16[256,1280]{1,0:T(8,128)(2,1)S(1)} %get-tuple-element.12, bf16[256,1280]{1,0:T(8,128)(2,1)S(1)} %get-tuple-element.11, f32[512]{0:T(512)S(1)} %maximum_multiply_fusion.1, f32[512]{0:T(512)S(1)} %copy-done.6, ...), kind=kOutput, calls=%fused_computation.4 | convolution fusion | flops 845086720 | bytes 3610624 | tf_op jit(solution)/shard_map/products/dot_general | solution.py:82
  103.5 14.3 %all_to_all.44 = f16[4,128,640]{2,1,0:T(8,128)(2,1)S(1)} all-to-all(f16[4,128,640]{2,1,0:T(8,128)(2,1)S(1)} %bitcast.18), channel_id=1, replica_groups=mesh['x'=4,'z'=16,'y'=4,'c'=2] {'x'}, dimensions={0} | all-to-all | bytes 1310720 | tf_op jit(solution)/shard_map/scatter_hidden_grad/all_to_all | solution.py:31
  117.9 0.7 convert_bitcast_fusion
  118.6 11.7 %all-to-all-start.6 = ((f16[16,8,640]{2,1,0:T(8,128)(2,1)}), f16[16,8,640]{2,1,0:T(8,128)(2,1)S(1)}, u32[]{:S(2)}, u32[]{:S(2)}) async-start(f16[16,8,640]{2,1,0:T(8,128)(2,1)} %convert_bitcast_fusion), calls=%async_computation.6 | async-start | bytes 327680 | tf_op jit(solution)/shard_map/scatter_hidden_grad/all_to_all | solution.py:31
  130.3 3.8 %convolution_convert_fusion = bf16[1280,640]{1,0:T(8,128)(2,1)} fusion(bf16[512,640]{1,0:T(8,128)(2,1)S(1)} %bitcast.17, bf16[256,1280]{1,0:T(8,128)(2,1)} %copy-done.3, bf16[256,1280]{1,0:T(8,128)(2,1)S(1)} %copy-done.2, f32[512]{0:T(512)S(1)} %maximum_multiply_fusion.1, f32[512]{0:T(512)S(1)} %copy-done.6, s32[512]{0:T(512)S(1)} %broadcast_subtract_fusion), kind=kOutput, calls=%fused_computation | convolution fusion | flops 845578240 | bytes 3610624 | tf_op jit(solution)/shard_map/products/dot_general | solution.py:84
  134.0 10.9 %all-to-all-done.6 = f16[16,8,640]{2,1,0:T(8,128)(2,1)S(1)} async-done(((f16[16,8,640]{2,1,0:T(8,128)(2,1)}), f16[16,8,640]{2,1,0:T(8,128)(2,1)S(1)}, u32[]{:S(2)}, u32[]{:S(2)}) %all-to-all-start.6) | async-done | bytes 163872 | tf_op jit(solution)/shard_map/scatter_hidden_grad/all_to_all | solution.py:31
  144.9 0.6 convert_reduce_fusion.2
  (31 shorter events, 0.9 us)
Async XLA Ops:
  0.6 45.5 %copy-start = (bf16[1280,640]{1,0:T(8,128)(2,1)S(1)}, bf16[1280,640]{1,0:T(8,128)(2,1)}, u32[]{:S(2)}) copy-start(bf16[1280,640]{1,0:T(8,128)(2,1)} %param.6) | copy-start | bytes 4915204
  33.0 13.1 %all-to-all-start.1 = ((bf16[4,128,640]{2,1,0:T(8,128)(2,1)}), bf16[4,128,640]{2,1,0:T(8,128)(2,1)S(1)}, u32[]{:S(2)}, u32[]{:S(2)}) async-start(bf16[4,128,640]{2,1,0:T(8,128)(2,1)} %broadcast_in_dim.37), calls=%async_computation.1 | async-start | bytes 1310720 | tf_op jit(solution)/shard_map/gather_hidden/all_to_all | solution.py:14
  47.6 4.2 %collective-permute-start = (f16[256,1280]{1,0:T(8,128)(2,1)}, f16[256,1280]{1,0:T(8,128)(2,1)S(1)}, u32[]{:S(2)}, u32[]{:S(2)}) collective-permute-start(f16[256,1280]{1,0:T(8,128)(2,1)} %convolution_convert_fusion.1), channel_id=1, source_target_pairs={{0,1},{1,0},{2,3},{3,2},{4,5},{5,4},{6,7},{7,6},{8,9},{9,8},{10,11... | collective-permute-start | bytes 1966088 | tf_op jit(solution)/shard_map/logits/ppermute | solution.py:30
  50.3 7.3 %copy-start.4 = (s32[512]{0:T(512)S(1)}, s32[512]{0:T(512)}, u32[]{:S(2)}) copy-start(s32[512]{0:T(512)} %param.7) | copy-start | bytes 6148
  52.9 13.8 %all-to-all-start.2 = ((f16[4,64,1280]{2,1,0:T(8,128)(2,1)}), f16[4,64,1280]{2,1,0:T(8,128)(2,1)S(1)}, u32[]{:S(2)}, u32[]{:S(2)}) async-start(f16[4,64,1280]{2,1,0:T(8,128)(2,1)} %bitcast.2), calls=%async_computation.2 | async-start | bytes 1310720 | tf_op jit(solution)/shard_map/logits/all_to_all | solution.py:31
  57.5 42.6 %copy-start.5 = (s32[512]{0:T(512)S(1)}, s32[512]{0:T(512)}, u32[]{:S(2)}) copy-start(s32[512]{0:T(512)} %param.8) | copy-start | bytes 6148
  57.5 42.6 %copy-start.6 = (f32[512]{0:T(512)S(1)}, f32[512]{0:T(512)}, u32[]{:S(2)}) copy-start(f32[512]{0:T(512)} %param.9) | copy-start | bytes 6148
  67.9 22.5 %all-to-all-start.3 = ((f32[64,1,128]{2,1,0:T(1,128)}), f32[64,1,128]{2,1,0:T(1,128)S(1)}, u32[]{:S(2)}, u32[]{:S(2)}) async-start(f32[64,1,128]{2,1,0:T(1,128)} %broadcast_in_dim.39), calls=%async_computation.3 | async-start | bytes 65536 | tf_op jit(solution)/shard_map/statistics/all_to_all | solution.py:31
  91.2 8.5 %all-to-all-start.4 = ((f32[8,1,256]{2,1,0:T(1,128)}), f32[8,1,256]{2,1,0:T(1,128)S(1)}, u32[]{:S(2)}, u32[]{:S(2)}) async-start(f32[8,1,256]{2,1,0:T(1,128)} %broadcast_in_dim.40), calls=%async_computation.4 | async-start | bytes 16384 | tf_op jit(solution)/shard_map/statistics/all_to_all | solution.py:31
  96.5 4.3 %collective-permute-start.1 = (bf16[256,1280]{1,0:T(8,128)(2,1)S(1)}, bf16[256,1280]{1,0:T(8,128)(2,1)}, u32[]{:S(2)}, u32[]{:S(2)}) collective-permute-start(bf16[256,1280]{1,0:T(8,128)(2,1)S(1)} %all_gather.3), channel_id=1, source_target_pairs={{0,1},{1,0},{2,3},{3,2},{4,5},{5,4},{6,7},{7,6},{8,9},{9,8},{10,11... | collective-permute-start | bytes 1966088 | tf_op jit(solution)/shard_map/gather_raised/ppermute | solution.py:30
  102.0 1.5 %copy-start.1 = (bf16[256,1280]{1,0:T(8,128)(2,1)}, bf16[256,1280]{1,0:T(8,128)(2,1)S(1)}, u32[]{:S(2)}) copy-start(bf16[256,1280]{1,0:T(8,128)(2,1)S(1)} %get-tuple-element.11) | copy-start | bytes 1966084
  102.0 1.5 %copy-start.3 = (bf16[256,1280]{1,0:T(8,128)(2,1)}, bf16[256,1280]{1,0:T(8,128)(2,1)S(1)}, u32[]{:S(2)}) copy-start(bf16[256,1280]{1,0:T(8,128)(2,1)S(1)} %get-tuple-element.12) | copy-start | bytes 1966084
  117.8 12.4 %copy-start.2 = (bf16[256,1280]{1,0:T(8,128)(2,1)S(1)}, bf16[256,1280]{1,0:T(8,128)(2,1)}, u32[]{:S(2)}) copy-start(bf16[256,1280]{1,0:T(8,128)(2,1)} %copy-done.1) | copy-start | bytes 1966084
  118.6 26.3 %all-to-all-start.6 = ((f16[16,8,640]{2,1,0:T(8,128)(2,1)}), f16[16,8,640]{2,1,0:T(8,128)(2,1)S(1)}, u32[]{:S(2)}, u32[]{:S(2)}) async-start(f16[16,8,640]{2,1,0:T(8,128)(2,1)} %convert_bitcast_fusion), calls=%async_computation.6 | async-start | bytes 327680 | tf_op jit(solution)/shard_map/scatter_hidden_grad/all_to_all | solution.py:31

commit v7 on v6

--- a/solution.py
+++ b/solution.py
@@ -4,6 +4,8 @@
 from jax.sharding import Mesh, PartitionSpec as P
 
 discount = 0.99
+raise_logits = 8.0
+raise_grad = 65536.0
 f32 = jnp.float32
 bf16 = jnp.bfloat16
 f16 = jnp.float16
@@ -33,6 +35,7 @@
 
     keep = discount * (1.0 - terminal.astype(f32))
     carried = jnp.concatenate([jnp.zeros((1,), f32), (keep * cotangent)[:-1]])
+    unit = jnp.maximum(jnp.max(jnp.abs(cotangent)), 1e-30)
     column = jnp.arange(rows, dtype=jnp.int32)
 
     with jax.named_scope("gather_hidden"):
@@ -43,12 +46,12 @@
         far_h = lax.dynamic_slice_in_dim(hidden, (1 - c) * half, half)
         inner = (((1,), (1,)), ((), ()))
         far_l = lax.dot_general(far_h, head_weight, inner, preferred_element_type=f32)
-        far_l = swap(far_l.astype(f16))
+        far_l = swap((far_l * raise_logits).astype(f16))
         near_l = lax.dot_general(near_h, head_weight, inner, preferred_element_type=f32)
         near_l = lax.optimization_barrier(near_l)
-        chip_l = (near_l + far_l.astype(f32)).astype(f16)
+        chip_l = (near_l * raise_logits + far_l.astype(f32)).astype(f16)
         pieces = turn(chip_l.reshape(sz["y"], own, rows), "y")
-        logits = jnp.sum(pieces.astype(f32), axis=0)
+        logits = jnp.sum(pieces.astype(f32), axis=0) * (1.0 / raise_logits)
 
     with jax.named_scope("own_statistics"):
         hit = (cut(targets) - first_row)[:, None] == column
@@ -79,7 +82,8 @@
         hit_all = (targets - first_row)[:, None] == column
         dlogits = jnp.where(hit_all, cotangent[:, None], 0.0)
         dlogits = (dlogits - (carried * factor)[:, None] * raised.astype(f32)).astype(bf16)
-        grad = jnp.dot(dlogits, head_weight, preferred_element_type=f32).astype(f16)
+        grad = jnp.dot(dlogits, head_weight, preferred_element_type=f32)
+        grad = (grad * (raise_grad / unit)).astype(f16)
         outer = (((0,), (0,)), ((), ()))
         weight_grad = lax.dot_general(dlogits, hidden, outer, preferred_element_type=f32)
         weight_grad = weight_grad.astype(bf16)
@@ -88,7 +92,7 @@
         grad = turn(grad.reshape(sz["x"], -1, width), "x")
         grad = jnp.sum(grad.astype(f32), axis=0).astype(f16)
         grad = turn(grad.reshape(sz["z"], -1, width), "z")
-        hidden_grad = jnp.sum(grad.astype(f32), axis=0).astype(bf16)
+        hidden_grad = (jnp.sum(grad.astype(f32), axis=0) * (unit / raise_grad)).astype(bf16)
 
     with jax.named_scope("rewards"):
         next_value = jnp.concatenate([lse[1:], jnp.zeros((1,), f32)])

time: 148 us -> 149 us (level)
  no operation moved by 1% of the time
where the time goes in v7:
time: 149 us; the launch traced here: 147 us
  blocking collectives  58.6 us (39%)
  starting transfers between devices  37.8 us (25%)
  waiting for transfers between devices  32.3 us (22%)
  matrix products  7.49 us (5%)
  other arithmetic  5.83 us (4%)
  local copies, waits for them, and re-layouts  3.4 us (2%)
    all_to_all x1, blocking collectives, spread(): copies = lax.all_to_all(copies, axis, 0, 0, tiled=True)  30.6 us
    all_to_all x4, starting transfers between devices, shards(): turn = lambda v, axis: lax.all_to_all(v, axis, 0, 0, tiled=True)  29.6 us
    all_to_all x4, waiting for transfers between devices, shards(): turn = lambda v, axis: lax.all_to_all(v, axis, 0, 0, tiled=True)  22 us
    all_to_all x1, blocking collectives, shards(): turn = lambda v, axis: lax.all_to_all(v, axis, 0, 0, tiled=True)  14.3 us
    all_gather x1, blocking collectives, shards(): near = lax.all_gather(raised.astype(bf16), 'y', axis=0, tiled=True)  13.6 us
    all_to_all x1, waiting for transfers between devices, spread(): copies = lax.all_to_all(copies, axis, 0, 0, tiled=True)  8.79 us
    all_to_all x1, starting transfers between devices, spread(): copies = lax.all_to_all(copies, axis, 0, 0, tiled=True)  4.29 us
    ppermute x2, starting transfers between devices, shards(): swap = lambda v: lax.ppermute(v, 'c', [(0, 1), (1, 0)])  3.96 us
  transfers between devices with their start and end apart: 7, of which 6 were waited for; matrix products, arithmetic and copies ran while one was open for 4% of the time, Pallas kernels for 0%

profile of v7, /device:TPU:24, one launch (start us, length us, event | category | flops | bytes accessed | tf_op | source)
XLA Modules:
  0.0 146.9 jit_solution(1887069221471186492)
XLA Ops:
  0.6 0.8 broadcast_in_dim.36
  1.5 30.6 %all_to_all.43 = bf16[16,8,640]{2,1,0:T(8,128)(2,1)S(1)} all-to-all(bf16[16,8,640]{2,1,0:T(8,128)(2,1)S(1)} %broadcast_in_dim.36), channel_id=1, replica_groups=mesh['x'=4,'z'=16,'y'=4,'c'=2] {'z'}, dimensions={0} | all-to-all | bytes 327680 | tf_op jit(solution)/shard_map/gather_hidden/all_to_all | solution.py:16
  32.1 0.9 broadcast_in_dim.37
  33.0 4.3 %all-to-all-start.1 = ((bf16[4,128,640]{2,1,0:T(8,128)(2,1)}), bf16[4,128,640]{2,1,0:T(8,128)(2,1)S(1)}, u32[]{:S(2)}, u32[]{:S(2)}) async-start(bf16[4,128,640]{2,1,0:T(8,128)(2,1)} %broadcast_in_dim.37), calls=%async_computation.1 | async-start | bytes 1310720 | tf_op jit(solution)/shard_map/gather_hidden/all_to_all | solution.py:16
  37.3 8.8 %all-to-all-done.1 = bf16[4,128,640]{2,1,0:T(8,128)(2,1)S(1)} async-done(((bf16[4,128,640]{2,1,0:T(8,128)(2,1)}), bf16[4,128,640]{2,1,0:T(8,128)(2,1)S(1)}, u32[]{:S(2)}, u32[]{:S(2)}) %all-to-all-start.1) | async-done | bytes 655392 | tf_op jit(solution)/shard_map/gather_hidden/all_to_all | solution.py:16
  46.1 1.5 %fusion = f16[256,1280]{1,0:T(8,128)(2,1)} fusion(bf16[1280,640]{1,0:T(8,128)(2,1)S(1)} %copy-done, bf16[512,640]{1,0:T(8,128)(2,1)S(1)} %bitcast.15, s32[]{:T(128)S(6)} %select_n.30), kind=kOutput, calls=%fused_computation.4 | convolution fusion | flops 420085760 | bytes 2621444 | tf_op jit(solution)/shard_map/logits/dot_general | solution.py:48
  47.6 1.9 %collective-permute-start = (f16[256,1280]{1,0:T(8,128)(2,1)}, f16[256,1280]{1,0:T(8,128)(2,1)S(1)}, u32[]{:S(2)}, u32[]{:S(2)}) collective-permute-start(f16[256,1280]{1,0:T(8,128)(2,1)} %fusion), channel_id=1, source_target_pairs={{0,1},{1,0},{2,3},{3,2},{4,5},{5,4},{6,7},{7,6},{8,9},{9,8},{10,11... | collective-permute-start | bytes 1966088 | tf_op jit(solution)/shard_map/logits/ppermute | solution.py:32
  49.6 0.7 fusion.3
  50.3 1.5 %collective-permute-done = f16[256,1280]{1,0:T(8,128)(2,1)S(1)} collective-permute-done((f16[256,1280]{1,0:T(8,128)(2,1)}, f16[256,1280]{1,0:T(8,128)(2,1)S(1)}, u32[]{:S(2)}, u32[]{:S(2)}) %collective-permute-start) | collective-permute-done | bytes 655392 | tf_op jit(solution)/shard_map/logits/ppermute | solution.py:32
  51.8 1.1 add_convert_fusion
  52.9 4.7 %all-to-all-start.2 = ((f16[4,64,1280]{2,1,0:T(8,128)(2,1)}), f16[4,64,1280]{2,1,0:T(8,128)(2,1)S(1)}, u32[]{:S(2)}, u32[]{:S(2)}) async-start(f16[4,64,1280]{2,1,0:T(8,128)(2,1)} %bitcast.2), calls=%async_computation.2 | async-start | bytes 1310720 | tf_op jit(solution)/shard_map/logits/all_to_all | solution.py:33
  57.7 9.0 %all-to-all-done.2 = f16[4,64,1280]{2,1,0:T(8,128)(2,1)S(1)} async-done(((f16[4,64,1280]{2,1,0:T(8,128)(2,1)}), f16[4,64,1280]{2,1,0:T(8,128)(2,1)S(1)}, u32[]{:S(2)}, u32[]{:S(2)}) %all-to-all-start.2) | async-done | bytes 655392 | tf_op jit(solution)/shard_map/logits/all_to_all | solution.py:33
  66.8 0.1 multiply_reduce_fusion
  66.9 0.3 fusion.6
  67.3 0.6 broadcast_in_dim.39
  67.9 7.9 %all-to-all-start.3 = ((f32[64,1,128]{2,1,0:T(1,128)}), f32[64,1,128]{2,1,0:T(1,128)S(1)}, u32[]{:S(2)}, u32[]{:S(2)}) async-start(f32[64,1,128]{2,1,0:T(1,128)} %broadcast_in_dim.39), calls=%async_computation.3 | async-start | bytes 65536 | tf_op jit(solution)/shard_map/statistics/all_to_all | solution.py:33
  75.8 13.6 %all_gather.3 = bf16[256,1280]{1,0:T(8,128)(2,1)S(1)} all-gather(bf16[64,1280]{1,0:T(8,128)(2,1)S(1)} %get-tuple-element.13), channel_id=1, replica_groups=mesh['x'=4,'z'=16,'y'=4,'c'=2] {'y'}, dimensions={0}, use_global_device_ids=true | all-gather | bytes 819200 | tf_op jit(solution)/shard_map/gather_raised/all_gather | solution.py:65
  89.5 0.9 all-to-all-done.3
  90.4 0.1 slice_reduce_fusion
  90.6 0.6 broadcast_in_dim.40
  91.2 5.3 %all-to-all-start.4 = ((f32[8,1,256]{2,1,0:T(1,128)}), f32[8,1,256]{2,1,0:T(1,128)S(1)}, u32[]{:S(2)}, u32[]{:S(2)}) async-start(f32[8,1,256]{2,1,0:T(1,128)} %broadcast_in_dim.40), calls=%async_computation.4 | async-start | bytes 16384 | tf_op jit(solution)/shard_map/statistics/all_to_all | solution.py:33
  96.6 2.1 %collective-permute-start.1 = (bf16[256,1280]{1,0:T(8,128)(2,1)S(1)}, bf16[256,1280]{1,0:T(8,128)(2,1)}, u32[]{:S(2)}, u32[]{:S(2)}) collective-permute-start(bf16[256,1280]{1,0:T(8,128)(2,1)S(1)} %all_gather.3), channel_id=1, source_target_pairs={{0,1},{1,0},{2,3},{3,2},{4,5},{5,4},{6,7},{7,6},{8,9},{9,8},{10,11... | collective-permute-start | bytes 1966088 | tf_op jit(solution)/shard_map/gather_raised/ppermute | solution.py:32
  98.6 1.2 all-to-all-done.4
  100.2 1.3 fusion.8
  102.2 1.2 broadcast_select_fusion.1
  103.4 1.5 fusion.1
  104.9 14.3 %all_to_all.44 = f16[4,128,640]{2,1,0:T(8,128)(2,1)S(1)} all-to-all(f16[4,128,640]{2,1,0:T(8,128)(2,1)S(1)} %bitcast.18), channel_id=1, replica_groups=mesh['x'=4,'z'=16,'y'=4,'c'=2] {'x'}, dimensions={0} | all-to-all | bytes 1310720 | tf_op jit(solution)/shard_map/scatter_hidden_grad/all_to_all | solution.py:33
  119.3 0.7 convert_bitcast_fusion
  120.0 11.7 %all-to-all-start.6 = ((f16[16,8,640]{2,1,0:T(8,128)(2,1)}), f16[16,8,640]{2,1,0:T(8,128)(2,1)S(1)}, u32[]{:S(2)}, u32[]{:S(2)}) async-start(f16[16,8,640]{2,1,0:T(8,128)(2,1)} %convert_bitcast_fusion), calls=%async_computation.6 | async-start | bytes 327680 | tf_op jit(solution)/shard_map/scatter_hidden_grad/all_to_all | solution.py:33
  131.7 3.8 %convolution_convert_fusion = bf16[1280,640]{1,0:T(8,128)(2,1)} fusion(bf16[512,640]{1,0:T(8,128)(2,1)S(1)} %bitcast.17, bf16[256,1280]{1,0:T(8,128)(2,1)} %copy-done.3, bf16[256,1280]{1,0:T(8,128)(2,1)S(1)} %copy-done.2, f32[512]{0:T(512)S(1)} %maximum_multiply_fusion.1, f32[512]{0:T(512)S(1)} %copy-done.6, s32[512]{0:T(512)S(1)} %broadcast_subtract_fusion), kind=kOutput, calls=%fused_computation | convolution fusion | flops 845578240 | bytes 3610624 | tf_op jit(solution)/shard_map/products/dot_general | solution.py:88
  135.4 10.9 %all-to-all-done.6 = f16[16,8,640]{2,1,0:T(8,128)(2,1)S(1)} async-done(((f16[16,8,640]{2,1,0:T(8,128)(2,1)}), f16[16,8,640]{2,1,0:T(8,128)(2,1)S(1)}, u32[]{:S(2)}, u32[]{:S(2)}) %all-to-all-start.6) | async-done | bytes 163872 | tf_op jit(solution)/shard_map/scatter_hidden_grad/all_to_all | solution.py:33
  146.3 0.6 multiply_convert_fusion
  (32 shorter events, 1.0 us)
Async XLA Ops:
  0.6 45.5 %copy-start = (bf16[1280,640]{1,0:T(8,128)(2,1)S(1)}, bf16[1280,640]{1,0:T(8,128)(2,1)}, u32[]{:S(2)}) copy-start(bf16[1280,640]{1,0:T(8,128)(2,1)} %param.6) | copy-start | bytes 4915204
  33.0 13.1 %all-to-all-start.1 = ((bf16[4,128,640]{2,1,0:T(8,128)(2,1)}), bf16[4,128,640]{2,1,0:T(8,128)(2,1)S(1)}, u32[]{:S(2)}, u32[]{:S(2)}) async-start(bf16[4,128,640]{2,1,0:T(8,128)(2,1)} %broadcast_in_dim.37), calls=%async_computation.1 | async-start | bytes 1310720 | tf_op jit(solution)/shard_map/gather_hidden/all_to_all | solution.py:16
  47.6 4.2 %collective-permute-start = (f16[256,1280]{1,0:T(8,128)(2,1)}, f16[256,1280]{1,0:T(8,128)(2,1)S(1)}, u32[]{:S(2)}, u32[]{:S(2)}) collective-permute-start(f16[256,1280]{1,0:T(8,128)(2,1)} %fusion), channel_id=1, source_target_pairs={{0,1},{1,0},{2,3},{3,2},{4,5},{5,4},{6,7},{7,6},{8,9},{9,8},{10,11... | collective-permute-start | bytes 1966088 | tf_op jit(solution)/shard_map/logits/ppermute | solution.py:32
  50.3 7.3 %copy-start.4 = (s32[512]{0:T(512)S(1)}, s32[512]{0:T(512)}, u32[]{:S(2)}) copy-start(s32[512]{0:T(512)} %param.7) | copy-start | bytes 6148
  52.9 13.8 %all-to-all-start.2 = ((f16[4,64,1280]{2,1,0:T(8,128)(2,1)}), f16[4,64,1280]{2,1,0:T(8,128)(2,1)S(1)}, u32[]{:S(2)}, u32[]{:S(2)}) async-start(f16[4,64,1280]{2,1,0:T(8,128)(2,1)} %bitcast.2), calls=%async_computation.2 | async-start | bytes 1310720 | tf_op jit(solution)/shard_map/logits/all_to_all | solution.py:33
  57.6 42.6 %copy-start.5 = (s32[512]{0:T(512)S(1)}, s32[512]{0:T(512)}, u32[]{:S(2)}) copy-start(s32[512]{0:T(512)} %param.8) | copy-start | bytes 6148
  57.6 42.6 %copy-start.6 = (f32[512]{0:T(512)S(1)}, f32[512]{0:T(512)}, u32[]{:S(2)}) copy-start(f32[512]{0:T(512)} %param.9) | copy-start | bytes 6148
  67.9 22.5 %all-to-all-start.3 = ((f32[64,1,128]{2,1,0:T(1,128)}), f32[64,1,128]{2,1,0:T(1,128)S(1)}, u32[]{:S(2)}, u32[]{:S(2)}) async-start(f32[64,1,128]{2,1,0:T(1,128)} %broadcast_in_dim.39), calls=%async_computation.3 | async-start | bytes 65536 | tf_op jit(solution)/shard_map/statistics/all_to_all | solution.py:33
  91.2 8.5 %all-to-all-start.4 = ((f32[8,1,256]{2,1,0:T(1,128)}), f32[8,1,256]{2,1,0:T(1,128)S(1)}, u32[]{:S(2)}, u32[]{:S(2)}) async-start(f32[8,1,256]{2,1,0:T(1,128)} %broadcast_in_dim.40), calls=%async_computation.4 | async-start | bytes 16384 | tf_op jit(solution)/shard_map/statistics/all_to_all | solution.py:33
  96.6 5.6 %collective-permute-start.1 = (bf16[256,1280]{1,0:T(8,128)(2,1)S(1)}, bf16[256,1280]{1,0:T(8,128)(2,1)}, u32[]{:S(2)}, u32[]{:S(2)}) collective-permute-start(bf16[256,1280]{1,0:T(8,128)(2,1)S(1)} %all_gather.3), channel_id=1, source_target_pairs={{0,1},{1,0},{2,3},{3,2},{4,5},{5,4},{6,7},{7,6},{8,9},{9,8},{10,11... | collective-permute-start | bytes 1966088 | tf_op jit(solution)/shard_map/gather_raised/ppermute | solution.py:32
  103.4 1.5 %copy-start.1 = (bf16[256,1280]{1,0:T(8,128)(2,1)}, bf16[256,1280]{1,0:T(8,128)(2,1)S(1)}, u32[]{:S(2)}) copy-start(bf16[256,1280]{1,0:T(8,128)(2,1)S(1)} %get-tuple-element.11) | copy-start | bytes 1966084
  103.4 1.5 %copy-start.3 = (bf16[256,1280]{1,0:T(8,128)(2,1)}, bf16[256,1280]{1,0:T(8,128)(2,1)S(1)}, u32[]{:S(2)}) copy-start(bf16[256,1280]{1,0:T(8,128)(2,1)S(1)} %get-tuple-element.12) | copy-start | bytes 1966084
  104.9 26.8 %copy-start.2 = (bf16[256,1280]{1,0:T(8,128)(2,1)S(1)}, bf16[256,1280]{1,0:T(8,128)(2,1)}, u32[]{:S(2)}) copy-start(bf16[256,1280]{1,0:T(8,128)(2,1)} %copy-done.1) | copy-start | bytes 1966084
  120.0 26.3 %all-to-all-start.6 = ((f16[16,8,640]{2,1,0:T(8,128)(2,1)}), f16[16,8,640]{2,1,0:T(8,128)(2,1)S(1)}, u32[]{:S(2)}, u32[]{:S(2)}) async-start(f16[16,8,640]{2,1,0:T(8,128)(2,1)} %convert_bitcast_fusion), calls=%async_computation.6 | async-start | bytes 327680 | tf_op jit(solution)/shard_map/scatter_hidden_grad/all_to_all | solution.py:33

commit v8 on v7

--- a/solution.py
+++ b/solution.py
@@ -36,6 +36,7 @@
     keep = discount * (1.0 - terminal.astype(f32))
     carried = jnp.concatenate([jnp.zeros((1,), f32), (keep * cotangent)[:-1]])
     unit = jnp.maximum(jnp.max(jnp.abs(cotangent)), 1e-30)
+    down, up = lax.optimization_barrier((unit / raise_grad, raise_grad / unit))
     column = jnp.arange(rows, dtype=jnp.int32)
 
     with jax.named_scope("gather_hidden"):
@@ -71,19 +72,19 @@
         top = jnp.max(every[:, :own], axis=0)
         lse = top + jnp.log(jnp.sum(jnp.exp(every[:, :own] - top), axis=0))
         picked = jnp.sum(every[:, own:], axis=0)
-        parts = jnp.concatenate([lse, picked, jnp.exp(own_top - lse), lse])
+        parts = jnp.concatenate([lse, picked, cut(carried) * jnp.exp(own_top - lse), lse])
         parts, _ = lax.optimization_barrier((parts, near))
         parts = turn(jnp.broadcast_to(parts, (n_width, 4 * own)), ("c", "y"))
-        lse, picked, factor, _ = (
+        lse, picked, scale, _ = (
             parts[:, i * own : (i + 1) * own].reshape(tokens) for i in range(4)
         )
 
     with jax.named_scope("products"):
         hit_all = (targets - first_row)[:, None] == column
         dlogits = jnp.where(hit_all, cotangent[:, None], 0.0)
-        dlogits = (dlogits - (carried * factor)[:, None] * raised.astype(f32)).astype(bf16)
+        dlogits = (dlogits - scale[:, None] * raised.astype(f32)).astype(bf16)
         grad = jnp.dot(dlogits, head_weight, preferred_element_type=f32)
-        grad = (grad * (raise_grad / unit)).astype(f16)
+        grad = (grad * up).astype(f16)
         outer = (((0,), (0,)), ((), ()))
         weight_grad = lax.dot_general(dlogits, hidden, outer, preferred_element_type=f32)
         weight_grad = weight_grad.astype(bf16)
@@ -92,7 +93,7 @@
         grad = turn(grad.reshape(sz["x"], -1, width), "x")
         grad = jnp.sum(grad.astype(f32), axis=0).astype(f16)
         grad = turn(grad.reshape(sz["z"], -1, width), "z")
-        hidden_grad = (jnp.sum(grad.astype(f32), axis=0) * (unit / raise_grad)).astype(bf16)
+        hidden_grad = (jnp.sum(grad.astype(f32), axis=0) * down).astype(bf16)
 
     with jax.named_scope("rewards"):
         next_value = jnp.concatenate([lse[1:], jnp.zeros((1,), f32)])

time: 149 us -> 149 us (level)
  transfers between devices with their start and end apart: 7 -> 7, of which waited for: 6 -> 5; matrix products, arithmetic and copies ran while one was open for 4% -> 5% of each run, Pallas kernels for 0% -> 0%
where the time goes in v8:
time: 149 us; the launch traced here: 147 us
  blocking collectives  59.4 us (40%)
  starting transfers between devices  37.8 us (25%)
  waiting for transfers between devices  31.2 us (21%)
  matrix products  7.49 us (5%)
  other arithmetic  5.9 us (4%)
  local copies, waits for them, and re-layouts  3.41 us (2%)
  between operations  1.49 us (1%)
    all_to_all x1, blocking collectives, spread(): copies = lax.all_to_all(copies, axis, 0, 0, tiled=True)  30.6 us
    all_to_all x4, starting transfers between devices, shards(): turn = lambda v, axis: lax.all_to_all(v, axis, 0, 0, tiled=True)  29.7 us
    all_to_all x4, waiting for transfers between devices, shards(): turn = lambda v, axis: lax.all_to_all(v, axis, 0, 0, tiled=True)  20.9 us
    all_to_all x1, blocking collectives, shards(): turn = lambda v, axis: lax.all_to_all(v, axis, 0, 0, tiled=True)  15.1 us
    all_gather x1, blocking collectives, shards(): near = lax.all_gather(raised.astype(bf16), 'y', axis=0, tiled=True)  13.6 us
    all_to_all x1, waiting for transfers between devices, spread(): copies = lax.all_to_all(copies, axis, 0, 0, tiled=True)  8.79 us
    all_to_all x1, starting transfers between devices, spread(): copies = lax.all_to_all(copies, axis, 0, 0, tiled=True)  4.29 us
    ppermute x2, starting transfers between devices, shards(): swap = lambda v: lax.ppermute(v, 'c', [(0, 1), (1, 0)])  3.82 us
  transfers between devices with their start and end apart: 7, of which 5 were waited for; matrix products, arithmetic and copies ran while one was open for 5% of the time, Pallas kernels for 0%

profile of v8, /device:TPU:24, one launch (start us, length us, event | category | flops | bytes accessed | tf_op | source)
XLA Modules:
  0.0 146.7 jit_solution(7798535854112359585)
XLA Ops:
  0.6 0.8 broadcast_in_dim.35
  1.5 30.6 %all_to_all.43 = bf16[16,8,640]{2,1,0:T(8,128)(2,1)S(1)} all-to-all(bf16[16,8,640]{2,1,0:T(8,128)(2,1)S(1)} %broadcast_in_dim.35), channel_id=1, replica_groups=mesh['x'=4,'z'=16,'y'=4,'c'=2] {'z'}, dimensions={0} | all-to-all | bytes 327680 | tf_op jit(solution)/shard_map/gather_hidden/all_to_all | solution.py:16
  32.1 0.9 broadcast_in_dim.36
  33.0 4.3 %all-to-all-start.1 = ((bf16[4,128,640]{2,1,0:T(8,128)(2,1)}), bf16[4,128,640]{2,1,0:T(8,128)(2,1)S(1)}, u32[]{:S(2)}, u32[]{:S(2)}) async-start(bf16[4,128,640]{2,1,0:T(8,128)(2,1)} %broadcast_in_dim.36), calls=%async_computation.1 | async-start | bytes 1310720 | tf_op jit(solution)/shard_map/gather_hidden/all_to_all | solution.py:16
  37.3 8.8 %all-to-all-done.1 = bf16[4,128,640]{2,1,0:T(8,128)(2,1)S(1)} async-done(((bf16[4,128,640]{2,1,0:T(8,128)(2,1)}), bf16[4,128,640]{2,1,0:T(8,128)(2,1)S(1)}, u32[]{:S(2)}, u32[]{:S(2)}) %all-to-all-start.1) | async-done | bytes 655392 | tf_op jit(solution)/shard_map/gather_hidden/all_to_all | solution.py:16
  46.1 1.5 %fusion = f16[256,1280]{1,0:T(8,128)(2,1)} fusion(bf16[1280,640]{1,0:T(8,128)(2,1)S(1)} %copy-done, bf16[512,640]{1,0:T(8,128)(2,1)S(1)} %bitcast.15, s32[]{:T(128)S(6)} %select_n.31), kind=kOutput, calls=%fused_computation.4 | convolution fusion | flops 420085760 | bytes 2621444 | tf_op jit(solution)/shard_map/logits/dot_general | solution.py:49
  47.6 1.9 %collective-permute-start = (f16[256,1280]{1,0:T(8,128)(2,1)}, f16[256,1280]{1,0:T(8,128)(2,1)S(1)}, u32[]{:S(2)}, u32[]{:S(2)}) collective-permute-start(f16[256,1280]{1,0:T(8,128)(2,1)} %fusion), channel_id=1, source_target_pairs={{0,1},{1,0},{2,3},{3,2},{4,5},{5,4},{6,7},{7,6},{8,9},{9,8},{10,11... | collective-permute-start | bytes 1966088 | tf_op jit(solution)/shard_map/logits/ppermute | solution.py:32
  49.6 0.7 fusion.3
  50.3 1.5 %collective-permute-done = f16[256,1280]{1,0:T(8,128)(2,1)S(1)} collective-permute-done((f16[256,1280]{1,0:T(8,128)(2,1)}, f16[256,1280]{1,0:T(8,128)(2,1)S(1)}, u32[]{:S(2)}, u32[]{:S(2)}) %collective-permute-start) | collective-permute-done | bytes 655392 | tf_op jit(solution)/shard_map/logits/ppermute | solution.py:32
  51.8 1.1 add_convert_fusion
  52.9 4.7 %all-to-all-start.2 = ((f16[4,64,1280]{2,1,0:T(8,128)(2,1)}), f16[4,64,1280]{2,1,0:T(8,128)(2,1)S(1)}, u32[]{:S(2)}, u32[]{:S(2)}) async-start(f16[4,64,1280]{2,1,0:T(8,128)(2,1)} %bitcast.2), calls=%async_computation.2 | async-start | bytes 1310720 | tf_op jit(solution)/shard_map/logits/all_to_all | solution.py:33
  57.7 0.6 abs_reduce_fusion
  58.3 8.4 %all-to-all-done.2 = f16[4,64,1280]{2,1,0:T(8,128)(2,1)S(1)} async-done(((f16[4,64,1280]{2,1,0:T(8,128)(2,1)}), f16[4,64,1280]{2,1,0:T(8,128)(2,1)S(1)}, u32[]{:S(2)}, u32[]{:S(2)}) %all-to-all-start.2) | async-done | bytes 655392 | tf_op jit(solution)/shard_map/logits/all_to_all | solution.py:33
  66.8 0.1 multiply_reduce_fusion
  66.9 0.3 fusion.6
  67.3 0.6 broadcast_in_dim.38
  67.9 7.9 %all-to-all-start.3 = ((f32[64,1,128]{2,1,0:T(1,128)}), f32[64,1,128]{2,1,0:T(1,128)S(1)}, u32[]{:S(2)}, u32[]{:S(2)}) async-start(f32[64,1,128]{2,1,0:T(1,128)} %broadcast_in_dim.38), calls=%async_computation.3 | async-start | bytes 65536 | tf_op jit(solution)/shard_map/statistics/all_to_all | solution.py:33
  75.8 13.6 %all_gather.3 = bf16[256,1280]{1,0:T(8,128)(2,1)S(1)} all-gather(bf16[64,1280]{1,0:T(8,128)(2,1)S(1)} %get-tuple-element.17), channel_id=1, replica_groups=mesh['x'=4,'z'=16,'y'=4,'c'=2] {'y'}, dimensions={0}, use_global_device_ids=true | all-gather | bytes 819200 | tf_op jit(solution)/shard_map/gather_raised/all_gather | solution.py:66
  89.5 1.9 %collective-permute-start.1 = (bf16[256,1280]{1,0:T(8,128)(2,1)S(1)}, bf16[256,1280]{1,0:T(8,128)(2,1)}, u32[]{:S(2)}, u32[]{:S(2)}) collective-permute-start(bf16[256,1280]{1,0:T(8,128)(2,1)S(1)} %all_gather.3), channel_id=1, source_target_pairs={{0,1},{1,0},{2,3},{3,2},{4,5},{5,4},{6,7},{7,6},{8,9},{9,8},{10,11... | collective-permute-start | bytes 1966088 | tf_op jit(solution)/shard_map/gather_raised/ppermute | solution.py:32
  91.4 0.1 slice_reduce_fusion
  91.7 0.6 broadcast_in_dim.39
  92.3 5.4 %all-to-all-start.4 = ((f32[8,1,256]{2,1,0:T(1,128)}), f32[8,1,256]{2,1,0:T(1,128)S(1)}, u32[]{:S(2)}, u32[]{:S(2)}) async-start(f32[8,1,256]{2,1,0:T(1,128)} %broadcast_in_dim.39), calls=%async_computation.4 | async-start | bytes 16384 | tf_op jit(solution)/shard_map/statistics/all_to_all | solution.py:33
  98.4 2.5 %all-to-all-done.4 = f32[8,1,256]{2,1,0:T(1,128)S(1)} async-done(((f32[8,1,256]{2,1,0:T(1,128)}), f32[8,1,256]{2,1,0:T(1,128)S(1)}, u32[]{:S(2)}, u32[]{:S(2)}) %all-to-all-start.4) | async-done | bytes 8224 | tf_op jit(solution)/shard_map/statistics/all_to_all | solution.py:33
  101.1 1.2 broadcast_select_fusion.1
  102.3 1.5 %fusion.1 = f16[512,640]{1,0:T(8,128)(2,1)S(1)} fusion(bf16[1280,640]{1,0:T(8,128)(2,1)S(1)} %copy-done, f32[]{:T(128)S(6)} %div.7, bf16[256,1280]{1,0:T(8,128)(2,1)S(1)} %get-tuple-element.16, bf16[256,1280]{1,0:T(8,128)(2,1)S(1)} %get-tuple-element.15, f32[512]{0:T(512)S(1)} %mul.82, f32[512]{0:T(512)S(1)} %copy-done.6, s32[512]{0:T(512)S(1)} %broadcast_subtract_fusion), kind=kOutput, calls=%fused_computation.6 | convolution fusion | flops 845414400 | bytes 3610628 | tf_op jit(solution)/shard_map/products/dot_general | solution.py:86
  103.8 15.1 %all_to_all.44 = f16[4,128,640]{2,1,0:T(8,128)(2,1)S(1)} all-to-all(f16[4,128,640]{2,1,0:T(8,128)(2,1)S(1)} %bitcast.18), channel_id=1, replica_groups=mesh['x'=4,'z'=16,'y'=4,'c'=2] {'x'}, dimensions={0} | all-to-all | bytes 1310720 | tf_op jit(solution)/shard_map/scatter_hidden_grad/all_to_all | solution.py:33
  119.0 0.7 convert_bitcast_fusion
  119.7 11.7 %all-to-all-start.6 = ((f16[16,8,640]{2,1,0:T(8,128)(2,1)}), f16[16,8,640]{2,1,0:T(8,128)(2,1)S(1)}, u32[]{:S(2)}, u32[]{:S(2)}) async-start(f16[16,8,640]{2,1,0:T(8,128)(2,1)} %convert_bitcast_fusion), calls=%async_computation.6 | async-start | bytes 327680 | tf_op jit(solution)/shard_map/scatter_hidden_grad/all_to_all | solution.py:33
  131.6 0.7 fusion.7
  132.3 3.8 %convolution_convert_fusion = bf16[1280,640]{1,0:T(8,128)(2,1)} fusion(bf16[512,640]{1,0:T(8,128)(2,1)S(1)} %bitcast.17, bf16[256,1280]{1,0:T(8,128)(2,1)} %copy-done.3, bf16[256,1280]{1,0:T(8,128)(2,1)S(1)} %copy-done.2, f32[512]{0:T(512)S(1)} %mul.82, f32[512]{0:T(512)S(1)} %copy-done.6, s32[512]{0:T(512)S(1)} %broadcast_subtract_fusion), kind=kOutput, calls=%fused_computation | convolution fusion | flops 845578240 | bytes 3610624 | tf_op jit(solution)/shard_map/products/dot_general | solution.py:89
  136.0 10.0 %all-to-all-done.6 = f16[16,8,640]{2,1,0:T(8,128)(2,1)S(1)} async-done(((f16[16,8,640]{2,1,0:T(8,128)(2,1)}), f16[16,8,640]{2,1,0:T(8,128)(2,1)S(1)}, u32[]{:S(2)}, u32[]{:S(2)}) %all-to-all-start.6) | async-done | bytes 163872 | tf_op jit(solution)/shard_map/scatter_hidden_grad/all_to_all | solution.py:33
  146.1 0.6 multiply_convert_fusion
  (33 shorter events, 1.0 us)
Async XLA Ops:
  0.6 45.5 %copy-start = (bf16[1280,640]{1,0:T(8,128)(2,1)S(1)}, bf16[1280,640]{1,0:T(8,128)(2,1)}, u32[]{:S(2)}) copy-start(bf16[1280,640]{1,0:T(8,128)(2,1)} %param.6) | copy-start | bytes 4915204
  33.0 13.1 %all-to-all-start.1 = ((bf16[4,128,640]{2,1,0:T(8,128)(2,1)}), bf16[4,128,640]{2,1,0:T(8,128)(2,1)S(1)}, u32[]{:S(2)}, u32[]{:S(2)}) async-start(bf16[4,128,640]{2,1,0:T(8,128)(2,1)} %broadcast_in_dim.36), calls=%async_computation.1 | async-start | bytes 1310720 | tf_op jit(solution)/shard_map/gather_hidden/all_to_all | solution.py:16
  47.6 4.2 %collective-permute-start = (f16[256,1280]{1,0:T(8,128)(2,1)}, f16[256,1280]{1,0:T(8,128)(2,1)S(1)}, u32[]{:S(2)}, u32[]{:S(2)}) collective-permute-start(f16[256,1280]{1,0:T(8,128)(2,1)} %fusion), channel_id=1, source_target_pairs={{0,1},{1,0},{2,3},{3,2},{4,5},{5,4},{6,7},{7,6},{8,9},{9,8},{10,11... | collective-permute-start | bytes 1966088 | tf_op jit(solution)/shard_map/logits/ppermute | solution.py:32
  50.3 7.3 %copy-start.5 = (s32[512]{0:T(512)S(1)}, s32[512]{0:T(512)}, u32[]{:S(2)}) copy-start(s32[512]{0:T(512)} %param.7) | copy-start | bytes 6148
  50.3 7.4 %copy-start.4 = (s32[512]{0:T(512)S(1)}, s32[512]{0:T(512)}, u32[]{:S(2)}) copy-start(s32[512]{0:T(512)} %param.8) | copy-start | bytes 6148
  50.3 7.4 %copy-start.6 = (f32[512]{0:T(512)S(1)}, f32[512]{0:T(512)}, u32[]{:S(2)}) copy-start(f32[512]{0:T(512)} %param.9) | copy-start | bytes 6148
  52.9 13.8 %all-to-all-start.2 = ((f16[4,64,1280]{2,1,0:T(8,128)(2,1)}), f16[4,64,1280]{2,1,0:T(8,128)(2,1)S(1)}, u32[]{:S(2)}, u32[]{:S(2)}) async-start(f16[4,64,1280]{2,1,0:T(8,128)(2,1)} %bitcast.2), calls=%async_computation.2 | async-start | bytes 1310720 | tf_op jit(solution)/shard_map/logits/all_to_all | solution.py:33
  67.9 23.5 %all-to-all-start.3 = ((f32[64,1,128]{2,1,0:T(1,128)}), f32[64,1,128]{2,1,0:T(1,128)S(1)}, u32[]{:S(2)}, u32[]{:S(2)}) async-start(f32[64,1,128]{2,1,0:T(1,128)} %broadcast_in_dim.38), calls=%async_computation.3 | async-start | bytes 65536 | tf_op jit(solution)/shard_map/statistics/all_to_all | solution.py:33
  89.5 11.6 %collective-permute-start.1 = (bf16[256,1280]{1,0:T(8,128)(2,1)S(1)}, bf16[256,1280]{1,0:T(8,128)(2,1)}, u32[]{:S(2)}, u32[]{:S(2)}) collective-permute-start(bf16[256,1280]{1,0:T(8,128)(2,1)S(1)} %all_gather.3), channel_id=1, source_target_pairs={{0,1},{1,0},{2,3},{3,2},{4,5},{5,4},{6,7},{7,6},{8,9},{9,8},{10,11... | collective-permute-start | bytes 1966088 | tf_op jit(solution)/shard_map/gather_raised/ppermute | solution.py:32
  92.3 8.6 %all-to-all-start.4 = ((f32[8,1,256]{2,1,0:T(1,128)}), f32[8,1,256]{2,1,0:T(1,128)S(1)}, u32[]{:S(2)}, u32[]{:S(2)}) async-start(f32[8,1,256]{2,1,0:T(1,128)} %broadcast_in_dim.39), calls=%async_computation.4 | async-start | bytes 16384 | tf_op jit(solution)/shard_map/statistics/all_to_all | solution.py:33
  102.3 1.5 %copy-start.1 = (bf16[256,1280]{1,0:T(8,128)(2,1)}, bf16[256,1280]{1,0:T(8,128)(2,1)S(1)}, u32[]{:S(2)}) copy-start(bf16[256,1280]{1,0:T(8,128)(2,1)S(1)} %get-tuple-element.15) | copy-start | bytes 1966084
  102.3 1.5 %copy-start.3 = (bf16[256,1280]{1,0:T(8,128)(2,1)}, bf16[256,1280]{1,0:T(8,128)(2,1)S(1)}, u32[]{:S(2)}) copy-start(bf16[256,1280]{1,0:T(8,128)(2,1)S(1)} %get-tuple-element.16) | copy-start | bytes 1966084
  103.8 28.5 %copy-start.2 = (bf16[256,1280]{1,0:T(8,128)(2,1)S(1)}, bf16[256,1280]{1,0:T(8,128)(2,1)}, u32[]{:S(2)}) copy-start(bf16[256,1280]{1,0:T(8,128)(2,1)} %copy-done.1) | copy-start | bytes 1966084
  119.7 26.3 %all-to-all-start.6 = ((f16[16,8,640]{2,1,0:T(8,128)(2,1)}), f16[16,8,640]{2,1,0:T(8,128)(2,1)S(1)}, u32[]{:S(2)}, u32[]{:S(2)}) async-start(f16[16,8,640]{2,1,0:T(8,128)(2,1)} %convert_bitcast_fusion), calls=%async_computation.6 | async-start | bytes 327680 | tf_op jit(solution)/shard_map/scatter_hidden_grad/all_to_all | solution.py:33

commit v9 on v8

--- a/solution.py
+++ b/solution.py
@@ -64,8 +64,6 @@
 
     with jax.named_scope("gather_raised"):
         near = lax.all_gather(raised.astype(bf16), "y", axis=0, tiled=True)
-        far = swap(near)
-        raised = jnp.concatenate([jnp.where(is_low, near, far), jnp.where(is_low, far, near)])
 
     with jax.named_scope("statistics"):
         every = turn(mine, ("z", "x"))
@@ -73,7 +71,9 @@
         lse = top + jnp.log(jnp.sum(jnp.exp(every[:, :own] - top), axis=0))
         picked = jnp.sum(every[:, own:], axis=0)
         parts = jnp.concatenate([lse, picked, cut(carried) * jnp.exp(own_top - lse), lse])
-        parts, _ = lax.optimization_barrier((parts, near))
+        parts, near = lax.optimization_barrier((parts, near))
+        far = swap(near)
+        raised = jnp.concatenate([jnp.where(is_low, near, far), jnp.where(is_low, far, near)])
         parts = turn(jnp.broadcast_to(parts, (n_width, 4 * own)), ("c", "y"))
         lse, picked, scale, _ = (
             parts[:, i * own : (i + 1) * own].reshape(tokens) for i in range(4)

time: 149 us -> 149 us (level)
  transfers between devices with their start and end apart: 7 -> 7, of which waited for: 5 -> 6; matrix products, arithmetic and copies ran while one was open for 5% -> 5% of each run, Pallas kernels for 0% -> 0%
where the time goes in v9:
time: 149 us; the launch traced here: 147 us
  blocking collectives  58.6 us (39%)
  starting transfers between devices  37.7 us (25%)
  waiting for transfers between devices  32.1 us (22%)
  matrix products  7.49 us (5%)
  other arithmetic  5.9 us (4%)
  local copies, waits for them, and re-layouts  3.4 us (2%)
    all_to_all x1, blocking collectives, spread(): copies = lax.all_to_all(copies, axis, 0, 0, tiled=True)  30.6 us
    all_to_all x4, starting transfers between devices, shards(): turn = lambda v, axis: lax.all_to_all(v, axis, 0, 0, tiled=True)  29.6 us
    all_to_all x4, waiting for transfers between devices, shards(): turn = lambda v, axis: lax.all_to_all(v, axis, 0, 0, tiled=True)  21.8 us
    all_to_all x1, blocking collectives, shards(): turn = lambda v, axis: lax.all_to_all(v, axis, 0, 0, tiled=True)  14.3 us
    all_gather x1, blocking collectives, shards(): near = lax.all_gather(raised.astype(bf16), 'y', axis=0, tiled=True)  13.6 us
    all_to_all x1, waiting for transfers between devices, spread(): copies = lax.all_to_all(copies, axis, 0, 0, tiled=True)  8.79 us
    all_to_all x1, starting transfers between devices, spread(): copies = lax.all_to_all(copies, axis, 0, 0, tiled=True)  4.29 us
    ppermute x2, starting transfers between devices, shards(): swap = lambda v: lax.ppermute(v, 'c', [(0, 1), (1, 0)])  3.83 us
  transfers between devices with their start and end apart: 7, of which 6 were waited for; matrix products, arithmetic and copies ran while one was open for 5% of the time, Pallas kernels for 0%

profile of v9, /device:TPU:24, one launch (start us, length us, event | category | flops | bytes accessed | tf_op | source)
XLA Modules:
  0.0 146.7 jit_solution(17016247477335637184)
XLA Ops:
  0.6 0.8 broadcast_in_dim.35
  1.5 30.6 %all_to_all.43 = bf16[16,8,640]{2,1,0:T(8,128)(2,1)S(1)} all-to-all(bf16[16,8,640]{2,1,0:T(8,128)(2,1)S(1)} %broadcast_in_dim.35), channel_id=1, replica_groups=mesh['x'=4,'z'=16,'y'=4,'c'=2] {'z'}, dimensions={0} | all-to-all | bytes 327680 | tf_op jit(solution)/shard_map/gather_hidden/all_to_all | solution.py:16
  32.1 0.9 broadcast_in_dim.36
  33.0 4.3 %all-to-all-start.1 = ((bf16[4,128,640]{2,1,0:T(8,128)(2,1)}), bf16[4,128,640]{2,1,0:T(8,128)(2,1)S(1)}, u32[]{:S(2)}, u32[]{:S(2)}) async-start(bf16[4,128,640]{2,1,0:T(8,128)(2,1)} %broadcast_in_dim.36), calls=%async_computation.1 | async-start | bytes 1310720 | tf_op jit(solution)/shard_map/gather_hidden/all_to_all | solution.py:16
  37.3 8.8 %all-to-all-done.1 = bf16[4,128,640]{2,1,0:T(8,128)(2,1)S(1)} async-done(((bf16[4,128,640]{2,1,0:T(8,128)(2,1)}), bf16[4,128,640]{2,1,0:T(8,128)(2,1)S(1)}, u32[]{:S(2)}, u32[]{:S(2)}) %all-to-all-start.1) | async-done | bytes 655392 | tf_op jit(solution)/shard_map/gather_hidden/all_to_all | solution.py:16
  46.1 1.5 %fusion = f16[256,1280]{1,0:T(8,128)(2,1)} fusion(bf16[1280,640]{1,0:T(8,128)(2,1)S(1)} %copy-done, bf16[512,640]{1,0:T(8,128)(2,1)S(1)} %bitcast.15, s32[]{:T(128)S(6)} %select_n.31), kind=kOutput, calls=%fused_computation.4 | convolution fusion | flops 420085760 | bytes 2621444 | tf_op jit(solution)/shard_map/logits/dot_general | solution.py:49
  47.6 1.9 %collective-permute-start = (f16[256,1280]{1,0:T(8,128)(2,1)}, f16[256,1280]{1,0:T(8,128)(2,1)S(1)}, u32[]{:S(2)}, u32[]{:S(2)}) collective-permute-start(f16[256,1280]{1,0:T(8,128)(2,1)} %fusion), channel_id=1, source_target_pairs={{0,1},{1,0},{2,3},{3,2},{4,5},{5,4},{6,7},{7,6},{8,9},{9,8},{10,11... | collective-permute-start | bytes 1966088 | tf_op jit(solution)/shard_map/logits/ppermute | solution.py:32
  49.6 0.7 fusion.3
  50.3 1.5 %collective-permute-done = f16[256,1280]{1,0:T(8,128)(2,1)S(1)} collective-permute-done((f16[256,1280]{1,0:T(8,128)(2,1)}, f16[256,1280]{1,0:T(8,128)(2,1)S(1)}, u32[]{:S(2)}, u32[]{:S(2)}) %collective-permute-start) | collective-permute-done | bytes 655392 | tf_op jit(solution)/shard_map/logits/ppermute | solution.py:32
  51.8 1.1 add_convert_fusion
  52.9 4.7 %all-to-all-start.2 = ((f16[4,64,1280]{2,1,0:T(8,128)(2,1)}), f16[4,64,1280]{2,1,0:T(8,128)(2,1)S(1)}, u32[]{:S(2)}, u32[]{:S(2)}) async-start(f16[4,64,1280]{2,1,0:T(8,128)(2,1)} %bitcast.2), calls=%async_computation.2 | async-start | bytes 1310720 | tf_op jit(solution)/shard_map/logits/all_to_all | solution.py:33
  57.7 0.6 abs_reduce_fusion
  58.3 8.4 %all-to-all-done.2 = f16[4,64,1280]{2,1,0:T(8,128)(2,1)S(1)} async-done(((f16[4,64,1280]{2,1,0:T(8,128)(2,1)}), f16[4,64,1280]{2,1,0:T(8,128)(2,1)S(1)}, u32[]{:S(2)}, u32[]{:S(2)}) %all-to-all-start.2) | async-done | bytes 655392 | tf_op jit(solution)/shard_map/logits/all_to_all | solution.py:33
  66.8 0.1 multiply_reduce_fusion
  66.9 0.3 fusion.6
  67.3 0.6 broadcast_in_dim.38
  67.9 7.9 %all-to-all-start.3 = ((f32[64,1,128]{2,1,0:T(1,128)}), f32[64,1,128]{2,1,0:T(1,128)S(1)}, u32[]{:S(2)}, u32[]{:S(2)}) async-start(f32[64,1,128]{2,1,0:T(1,128)} %broadcast_in_dim.38), calls=%async_computation.3 | async-start | bytes 65536 | tf_op jit(solution)/shard_map/statistics/all_to_all | solution.py:33
  75.8 13.6 %all_gather.3 = bf16[256,1280]{1,0:T(8,128)(2,1)S(1)} all-gather(bf16[64,1280]{1,0:T(8,128)(2,1)S(1)} %get-tuple-element.19), channel_id=1, replica_groups=mesh['x'=4,'z'=16,'y'=4,'c'=2] {'y'}, dimensions={0}, use_global_device_ids=true | all-gather | bytes 819200 | tf_op jit(solution)/shard_map/gather_raised/all_gather | solution.py:66
  89.5 0.9 all-to-all-done.3
  90.7 1.9 %collective-permute-start.1 = (bf16[256,1280]{1,0:T(8,128)(2,1)S(1)}, bf16[256,1280]{1,0:T(8,128)(2,1)}, u32[]{:S(2)}, u32[]{:S(2)}) collective-permute-start(bf16[256,1280]{1,0:T(8,128)(2,1)S(1)} %all_gather.3), channel_id=1, source_target_pairs={{0,1},{1,0},{2,3},{3,2},{4,5},{5,4},{6,7},{7,6},{8,9},{9,8},{10,11... | collective-permute-start | bytes 1966088 | tf_op jit(solution)/shard_map/statistics/ppermute | solution.py:32
  92.6 0.6 broadcast_in_dim.39
  93.2 5.3 %all-to-all-start.4 = ((f32[8,1,256]{2,1,0:T(1,128)}), f32[8,1,256]{2,1,0:T(1,128)S(1)}, u32[]{:S(2)}, u32[]{:S(2)}) async-start(f32[8,1,256]{2,1,0:T(1,128)} %broadcast_in_dim.39), calls=%async_computation.4 | async-start | bytes 16384 | tf_op jit(solution)/shard_map/statistics/all_to_all | solution.py:33
  99.2 2.5 %all-to-all-done.4 = f32[8,1,256]{2,1,0:T(1,128)S(1)} async-done(((f32[8,1,256]{2,1,0:T(1,128)}), f32[8,1,256]{2,1,0:T(1,128)S(1)}, u32[]{:S(2)}, u32[]{:S(2)}) %all-to-all-start.4) | async-done | bytes 8224 | tf_op jit(solution)/shard_map/statistics/all_to_all | solution.py:33
  101.9 1.2 broadcast_select_fusion.1
  103.1 1.5 %fusion.1 = f16[512,640]{1,0:T(8,128)(2,1)S(1)} fusion(bf16[1280,640]{1,0:T(8,128)(2,1)S(1)} %copy-done, f32[]{:T(128)S(6)} %div.7, bf16[256,1280]{1,0:T(8,128)(2,1)S(1)} %get-tuple-element.18, bf16[256,1280]{1,0:T(8,128)(2,1)S(1)} %get-tuple-element.17, f32[512]{0:T(512)S(1)} %mul.82, f32[512]{0:T(512)S(1)} %copy-done.6, s32[512]{0:T(512)S(1)} %broadcast_subtract_fusion), kind=kOutput, calls=%fused_computation.6 | convolution fusion | flops 845414400 | bytes 3610628 | tf_op jit(solution)/shard_map/products/dot_general | solution.py:86
  104.6 14.3 %all_to_all.44 = f16[4,128,640]{2,1,0:T(8,128)(2,1)S(1)} all-to-all(f16[4,128,640]{2,1,0:T(8,128)(2,1)S(1)} %bitcast.18), channel_id=1, replica_groups=mesh['x'=4,'z'=16,'y'=4,'c'=2] {'x'}, dimensions={0} | all-to-all | bytes 1310720 | tf_op jit(solution)/shard_map/scatter_hidden_grad/all_to_all | solution.py:33
  119.0 0.7 convert_bitcast_fusion
  119.7 11.7 %all-to-all-start.6 = ((f16[16,8,640]{2,1,0:T(8,128)(2,1)}), f16[16,8,640]{2,1,0:T(8,128)(2,1)S(1)}, u32[]{:S(2)}, u32[]{:S(2)}) async-start(f16[16,8,640]{2,1,0:T(8,128)(2,1)} %convert_bitcast_fusion), calls=%async_computation.6 | async-start | bytes 327680 | tf_op jit(solution)/shard_map/scatter_hidden_grad/all_to_all | solution.py:33
  131.6 0.7 fusion.7
  132.3 3.8 %convolution_convert_fusion = bf16[1280,640]{1,0:T(8,128)(2,1)} fusion(bf16[512,640]{1,0:T(8,128)(2,1)S(1)} %bitcast.17, bf16[256,1280]{1,0:T(8,128)(2,1)} %copy-done.3, bf16[256,1280]{1,0:T(8,128)(2,1)S(1)} %copy-done.2, f32[512]{0:T(512)S(1)} %mul.82, f32[512]{0:T(512)S(1)} %copy-done.6, s32[512]{0:T(512)S(1)} %broadcast_subtract_fusion), kind=kOutput, calls=%fused_computation | convolution fusion | flops 845578240 | bytes 3610624 | tf_op jit(solution)/shard_map/products/dot_general | solution.py:89
  136.0 10.0 %all-to-all-done.6 = f16[16,8,640]{2,1,0:T(8,128)(2,1)S(1)} async-done(((f16[16,8,640]{2,1,0:T(8,128)(2,1)}), f16[16,8,640]{2,1,0:T(8,128)(2,1)S(1)}, u32[]{:S(2)}, u32[]{:S(2)}) %all-to-all-start.6) | async-done | bytes 163872 | tf_op jit(solution)/shard_map/scatter_hidden_grad/all_to_all | solution.py:33
  146.1 0.6 multiply_convert_fusion
  (33 shorter events, 1.1 us)
Async XLA Ops:
  0.6 45.5 %copy-start = (bf16[1280,640]{1,0:T(8,128)(2,1)S(1)}, bf16[1280,640]{1,0:T(8,128)(2,1)}, u32[]{:S(2)}) copy-start(bf16[1280,640]{1,0:T(8,128)(2,1)} %param.6) | copy-start | bytes 4915204
  33.0 13.1 %all-to-all-start.1 = ((bf16[4,128,640]{2,1,0:T(8,128)(2,1)}), bf16[4,128,640]{2,1,0:T(8,128)(2,1)S(1)}, u32[]{:S(2)}, u32[]{:S(2)}) async-start(bf16[4,128,640]{2,1,0:T(8,128)(2,1)} %broadcast_in_dim.36), calls=%async_computation.1 | async-start | bytes 1310720 | tf_op jit(solution)/shard_map/gather_hidden/all_to_all | solution.py:16
  47.6 4.2 %collective-permute-start = (f16[256,1280]{1,0:T(8,128)(2,1)}, f16[256,1280]{1,0:T(8,128)(2,1)S(1)}, u32[]{:S(2)}, u32[]{:S(2)}) collective-permute-start(f16[256,1280]{1,0:T(8,128)(2,1)} %fusion), channel_id=1, source_target_pairs={{0,1},{1,0},{2,3},{3,2},{4,5},{5,4},{6,7},{7,6},{8,9},{9,8},{10,11... | collective-permute-start | bytes 1966088 | tf_op jit(solution)/shard_map/logits/ppermute | solution.py:32
  50.3 7.3 %copy-start.5 = (s32[512]{0:T(512)S(1)}, s32[512]{0:T(512)}, u32[]{:S(2)}) copy-start(s32[512]{0:T(512)} %param.7) | copy-start | bytes 6148
  50.3 7.4 %copy-start.4 = (s32[512]{0:T(512)S(1)}, s32[512]{0:T(512)}, u32[]{:S(2)}) copy-start(s32[512]{0:T(512)} %param.8) | copy-start | bytes 6148
  50.3 7.4 %copy-start.6 = (f32[512]{0:T(512)S(1)}, f32[512]{0:T(512)}, u32[]{:S(2)}) copy-start(f32[512]{0:T(512)} %param.9) | copy-start | bytes 6148
  52.9 13.8 %all-to-all-start.2 = ((f16[4,64,1280]{2,1,0:T(8,128)(2,1)}), f16[4,64,1280]{2,1,0:T(8,128)(2,1)S(1)}, u32[]{:S(2)}, u32[]{:S(2)}) async-start(f16[4,64,1280]{2,1,0:T(8,128)(2,1)} %bitcast.2), calls=%async_computation.2 | async-start | bytes 1310720 | tf_op jit(solution)/shard_map/logits/all_to_all | solution.py:33
  67.9 22.5 %all-to-all-start.3 = ((f32[64,1,128]{2,1,0:T(1,128)}), f32[64,1,128]{2,1,0:T(1,128)S(1)}, u32[]{:S(2)}, u32[]{:S(2)}) async-start(f32[64,1,128]{2,1,0:T(1,128)} %broadcast_in_dim.38), calls=%async_computation.3 | async-start | bytes 65536 | tf_op jit(solution)/shard_map/statistics/all_to_all | solution.py:33
  90.7 11.2 %collective-permute-start.1 = (bf16[256,1280]{1,0:T(8,128)(2,1)S(1)}, bf16[256,1280]{1,0:T(8,128)(2,1)}, u32[]{:S(2)}, u32[]{:S(2)}) collective-permute-start(bf16[256,1280]{1,0:T(8,128)(2,1)S(1)} %all_gather.3), channel_id=1, source_target_pairs={{0,1},{1,0},{2,3},{3,2},{4,5},{5,4},{6,7},{7,6},{8,9},{9,8},{10,11... | collective-permute-start | bytes 1966088 | tf_op jit(solution)/shard_map/statistics/ppermute | solution.py:32
  93.2 8.5 %all-to-all-start.4 = ((f32[8,1,256]{2,1,0:T(1,128)}), f32[8,1,256]{2,1,0:T(1,128)S(1)}, u32[]{:S(2)}, u32[]{:S(2)}) async-start(f32[8,1,256]{2,1,0:T(1,128)} %broadcast_in_dim.39), calls=%async_computation.4 | async-start | bytes 16384 | tf_op jit(solution)/shard_map/statistics/all_to_all | solution.py:33
  103.1 1.5 %copy-start.1 = (bf16[256,1280]{1,0:T(8,128)(2,1)}, bf16[256,1280]{1,0:T(8,128)(2,1)S(1)}, u32[]{:S(2)}) copy-start(bf16[256,1280]{1,0:T(8,128)(2,1)S(1)} %get-tuple-element.17) | copy-start | bytes 1966084
  103.1 1.5 %copy-start.3 = (bf16[256,1280]{1,0:T(8,128)(2,1)}, bf16[256,1280]{1,0:T(8,128)(2,1)S(1)}, u32[]{:S(2)}) copy-start(bf16[256,1280]{1,0:T(8,128)(2,1)S(1)} %get-tuple-element.18) | copy-start | bytes 1966084
  104.6 27.6 %copy-start.2 = (bf16[256,1280]{1,0:T(8,128)(2,1)S(1)}, bf16[256,1280]{1,0:T(8,128)(2,1)}, u32[]{:S(2)}) copy-start(bf16[256,1280]{1,0:T(8,128)(2,1)} %copy-done.1) | copy-start | bytes 1966084
  119.7 26.3 %all-to-all-start.6 = ((f16[16,8,640]{2,1,0:T(8,128)(2,1)}), f16[16,8,640]{2,1,0:T(8,128)(2,1)S(1)}, u32[]{:S(2)}, u32[]{:S(2)}) async-start(f16[16,8,640]{2,1,0:T(8,128)(2,1)} %convert_bitcast_fusion), calls=%async_computation.6 | async-start | bytes 327680 | tf_op jit(solution)/shard_map/scatter_hidden_grad/all_to_all | solution.py:33

commit v10 on v8

--- a/solution.py
+++ b/solution.py
@@ -40,7 +40,7 @@
     column = jnp.arange(rows, dtype=jnp.int32)
 
     with jax.named_scope("gather_hidden"):
-        hidden = spread(spread(hidden_states, "z"), "x")
+        hidden = lax.all_gather(spread(hidden_states, "z"), "x", axis=0, tiled=True)
 
     with jax.named_scope("logits"):
         near_h = lax.dynamic_slice_in_dim(hidden, c * half, half)

time: 149 us -> 149 us (level)
  blocking collectives: 59.4 us -> 42.9 us
  starting transfers between devices: 37.8 us -> 47.9 us
  waiting for transfers between devices: 31.2 us -> 38.1 us
    all_to_all x1 -> x0, blocking collectives: 30.6 us -> none  [spread(): copies = lax.all_to_all(copies, axis, 0, 0, tiled=True)]
    all_gather x0 -> x1, blocking collectives: none -> 14.1 us  [shards(): hidden = lax.all_gather(spread(hidden_states, 'z'), 'x', axis=0, tiled=True)]
    all_to_all x1, starting transfers between devices: 4.29 us -> 15.2 us  [spread(): copies = lax.all_to_all(copies, axis, 0, 0, tiled=True)]
    all_to_all x1, waiting for transfers between devices: 8.79 us -> 15.6 us  [spread(): copies = lax.all_to_all(copies, axis, 0, 0, tiled=True)]
where the time goes in v10:
time: 149 us; the launch traced here: 147 us
  starting transfers between devices  47.9 us (32%)
  blocking collectives  42.9 us (29%)
  waiting for transfers between devices  38.1 us (26%)
  matrix products  7.49 us (5%)
  other arithmetic  5.9 us (4%)
  local copies, waits for them, and re-layouts  3.18 us (2%)
  between operations  1.5 us (1%)
    all_to_all x4, starting transfers between devices, shards(): turn = lambda v, axis: lax.all_to_all(v, axis, 0, 0, tiled=True)  28.9 us
    all_to_all x4, waiting for transfers between devices, shards(): turn = lambda v, axis: lax.all_to_all(v, axis, 0, 0, tiled=True)  20.9 us
    all_to_all x1, waiting for transfers between devices, spread(): copies = lax.all_to_all(copies, axis, 0, 0, tiled=True)  15.6 us
    all_to_all x1, starting transfers between devices, spread(): copies = lax.all_to_all(copies, axis, 0, 0, tiled=True)  15.2 us
    all_to_all x1, blocking collectives, shards(): turn = lambda v, axis: lax.all_to_all(v, axis, 0, 0, tiled=True)  15.1 us
    all_gather x1, blocking collectives, shards(): hidden = lax.all_gather(spread(hidden_states, 'z'), 'x', axis=0, tiled=True)  14.1 us
    all_gather x1, blocking collectives, shards(): near = lax.all_gather(raised.astype(bf16), 'y', axis=0, tiled=True)  13.6 us
    ppermute x2, starting transfers between devices, shards(): swap = lambda v: lax.ppermute(v, 'c', [(0, 1), (1, 0)])  3.82 us
  transfers between devices with their start and end apart: 7, of which 5 were waited for; matrix products, arithmetic and copies ran while one was open for 5% of the time, Pallas kernels for 0%

profile of v10, /device:TPU:24, one launch (start us, length us, event | category | flops | bytes accessed | tf_op | source)
XLA Modules:
  0.0 146.9 jit_solution(15482430438130475578)
XLA Ops:
  0.6 1.5 %broadcast_in_dim.32 = bf16[16,8,640]{2,1,0:T(8,128)(2,1)} broadcast(bf16[8,640]{1,0:T(8,128)(2,1)} %param.5), dimensions={1,2} | broadcast | bytes 174080 | tf_op jit(solution)/shard_map/gather_hidden/broadcast_in_dim | solution.py:15
  2.1 15.2 %all-to-all-start = ((bf16[16,8,640]{2,1,0:T(8,128)(2,1)}), bf16[16,8,640]{2,1,0:T(8,128)(2,1)S(1)}, u32[]{:S(2)}, u32[]{:S(2)}) async-start(bf16[16,8,640]{2,1,0:T(8,128)(2,1)} %broadcast_in_dim.32), calls=%async_computation | async-start | bytes 327680 | tf_op jit(solution)/shard_map/gather_hidden/all_to_all | solution.py:16
  17.4 15.6 %all-to-all-done = bf16[16,8,640]{2,1,0:T(8,128)(2,1)S(1)} async-done(((bf16[16,8,640]{2,1,0:T(8,128)(2,1)}), bf16[16,8,640]{2,1,0:T(8,128)(2,1)S(1)}, u32[]{:S(2)}, u32[]{:S(2)}) %all-to-all-start) | async-done | bytes 163872 | tf_op jit(solution)/shard_map/gather_hidden/all_to_all | solution.py:16
  33.0 14.1 %all_gather.6 = bf16[512,640]{1,0:T(8,128)(2,1)S(1)} all-gather(bf16[128,640]{1,0:T(8,128)(2,1)S(1)} %bitcast.15), channel_id=1, replica_groups=mesh['x'=4,'z'=16,'y'=4,'c'=2] {'x'}, dimensions={0}, use_global_device_ids=true | all-gather | bytes 819200 | tf_op jit(solution)/shard_map/gather_hidden/all_gather | solution.py:43
  47.1 1.6 %fusion = f16[256,1280]{1,0:T(8,128)(2,1)} fusion(bf16[1280,640]{1,0:T(8,128)(2,1)S(1)} %copy-done, bf16[512,640]{1,0:T(8,128)(2,1)S(1)} %all_gather.6, s32[]{:T(128)S(6)} %select_n.31), kind=kOutput, calls=%fused_computation.4 | convolution fusion | flops 420085760 | bytes 2621444 | tf_op jit(solution)/shard_map/logits/dot_general | solution.py:49
  48.6 1.9 %collective-permute-start = (f16[256,1280]{1,0:T(8,128)(2,1)}, f16[256,1280]{1,0:T(8,128)(2,1)S(1)}, u32[]{:S(2)}, u32[]{:S(2)}) collective-permute-start(f16[256,1280]{1,0:T(8,128)(2,1)} %fusion), channel_id=1, source_target_pairs={{0,1},{1,0},{2,3},{3,2},{4,5},{5,4},{6,7},{7,6},{8,9},{9,8},{10,11... | collective-permute-start | bytes 1966088 | tf_op jit(solution)/shard_map/logits/ppermute | solution.py:32
  50.5 0.7 fusion.3
  51.3 1.5 %collective-permute-done = f16[256,1280]{1,0:T(8,128)(2,1)S(1)} collective-permute-done((f16[256,1280]{1,0:T(8,128)(2,1)}, f16[256,1280]{1,0:T(8,128)(2,1)S(1)}, u32[]{:S(2)}, u32[]{:S(2)}) %collective-permute-start) | collective-permute-done | bytes 655392 | tf_op jit(solution)/shard_map/logits/ppermute | solution.py:32
  52.8 1.1 add_convert_fusion
  53.9 4.7 %all-to-all-start.1 = ((f16[4,64,1280]{2,1,0:T(8,128)(2,1)}), f16[4,64,1280]{2,1,0:T(8,128)(2,1)S(1)}, u32[]{:S(2)}, u32[]{:S(2)}) async-start(f16[4,64,1280]{2,1,0:T(8,128)(2,1)} %bitcast.1), calls=%async_computation.1 | async-start | bytes 1310720 | tf_op jit(solution)/shard_map/logits/all_to_all | solution.py:33
  58.7 0.6 abs_reduce_fusion
  59.3 8.4 %all-to-all-done.1 = f16[4,64,1280]{2,1,0:T(8,128)(2,1)S(1)} async-done(((f16[4,64,1280]{2,1,0:T(8,128)(2,1)}), f16[4,64,1280]{2,1,0:T(8,128)(2,1)S(1)}, u32[]{:S(2)}, u32[]{:S(2)}) %all-to-all-start.1) | async-done | bytes 655392 | tf_op jit(solution)/shard_map/logits/all_to_all | solution.py:33
  67.8 0.1 multiply_reduce_fusion
  67.9 0.3 fusion.6
  68.3 0.6 broadcast_in_dim.34
  68.9 7.1 %all-to-all-start.2 = ((f32[64,1,128]{2,1,0:T(1,128)}), f32[64,1,128]{2,1,0:T(1,128)S(1)}, u32[]{:S(2)}, u32[]{:S(2)}) async-start(f32[64,1,128]{2,1,0:T(1,128)} %broadcast_in_dim.34), calls=%async_computation.2 | async-start | bytes 65536 | tf_op jit(solution)/shard_map/statistics/all_to_all | solution.py:33
  76.1 13.6 %all_gather.7 = bf16[256,1280]{1,0:T(8,128)(2,1)S(1)} all-gather(bf16[64,1280]{1,0:T(8,128)(2,1)S(1)} %get-tuple-element.17), channel_id=1, replica_groups=mesh['x'=4,'z'=16,'y'=4,'c'=2] {'y'}, dimensions={0}, use_global_device_ids=true | all-gather | bytes 819200 | tf_op jit(solution)/shard_map/gather_raised/all_gather | solution.py:66
  89.7 1.9 %collective-permute-start.1 = (bf16[256,1280]{1,0:T(8,128)(2,1)S(1)}, bf16[256,1280]{1,0:T(8,128)(2,1)}, u32[]{:S(2)}, u32[]{:S(2)}) collective-permute-start(bf16[256,1280]{1,0:T(8,128)(2,1)S(1)} %all_gather.7), channel_id=1, source_target_pairs={{0,1},{1,0},{2,3},{3,2},{4,5},{5,4},{6,7},{7,6},{8,9},{9,8},{10,11... | collective-permute-start | bytes 1966088 | tf_op jit(solution)/shard_map/gather_raised/ppermute | solution.py:32
  91.6 0.1 slice_reduce_fusion
  91.9 0.6 broadcast_in_dim.35
  92.5 5.4 %all-to-all-start.3 = ((f32[8,1,256]{2,1,0:T(1,128)}), f32[8,1,256]{2,1,0:T(1,128)S(1)}, u32[]{:S(2)}, u32[]{:S(2)}) async-start(f32[8,1,256]{2,1,0:T(1,128)} %broadcast_in_dim.35), calls=%async_computation.3 | async-start | bytes 16384 | tf_op jit(solution)/shard_map/statistics/all_to_all | solution.py:33
  98.6 2.5 %all-to-all-done.3 = f32[8,1,256]{2,1,0:T(1,128)S(1)} async-done(((f32[8,1,256]{2,1,0:T(1,128)}), f32[8,1,256]{2,1,0:T(1,128)S(1)}, u32[]{:S(2)}, u32[]{:S(2)}) %all-to-all-start.3) | async-done | bytes 8224 | tf_op jit(solution)/shard_map/statistics/all_to_all | solution.py:33
  101.3 1.2 broadcast_select_fusion.1
  102.5 1.5 %fusion.1 = f16[512,640]{1,0:T(8,128)(2,1)S(1)} fusion(bf16[1280,640]{1,0:T(8,128)(2,1)S(1)} %copy-done, f32[]{:T(128)S(6)} %div.7, bf16[256,1280]{1,0:T(8,128)(2,1)S(1)} %get-tuple-element.16, bf16[256,1280]{1,0:T(8,128)(2,1)S(1)} %get-tuple-element.15, f32[512]{0:T(512)S(1)} %mul.82, f32[512]{0:T(512)S(1)} %copy-done.6, s32[512]{0:T(512)S(1)} %broadcast_subtract_fusion), kind=kOutput, calls=%fused_computation.6 | convolution fusion | flops 845414400 | bytes 3610628 | tf_op jit(solution)/shard_map/products/dot_general | solution.py:86
  104.0 15.1 %all_to_all.38 = f16[4,128,640]{2,1,0:T(8,128)(2,1)S(1)} all-to-all(f16[4,128,640]{2,1,0:T(8,128)(2,1)S(1)} %bitcast.14), channel_id=1, replica_groups=mesh['x'=4,'z'=16,'y'=4,'c'=2] {'x'}, dimensions={0} | all-to-all | bytes 1310720 | tf_op jit(solution)/shard_map/scatter_hidden_grad/all_to_all | solution.py:33
  119.1 0.1 convert_reduce_fusion
  119.2 0.7 convert_bitcast_fusion
  119.9 11.7 %all-to-all-start.5 = ((f16[16,8,640]{2,1,0:T(8,128)(2,1)}), f16[16,8,640]{2,1,0:T(8,128)(2,1)S(1)}, u32[]{:S(2)}, u32[]{:S(2)}) async-start(f16[16,8,640]{2,1,0:T(8,128)(2,1)} %convert_bitcast_fusion), calls=%async_computation.5 | async-start | bytes 327680 | tf_op jit(solution)/shard_map/scatter_hidden_grad/all_to_all | solution.py:33
  131.8 0.7 fusion.7
  132.5 3.8 %convolution_convert_fusion = bf16[1280,640]{1,0:T(8,128)(2,1)} fusion(bf16[512,640]{1,0:T(8,128)(2,1)S(1)} %all_gather.6, bf16[256,1280]{1,0:T(8,128)(2,1)} %copy-done.3, bf16[256,1280]{1,0:T(8,128)(2,1)S(1)} %copy-done.2, f32[512]{0:T(512)S(1)} %mul.82, f32[512]{0:T(512)S(1)} %copy-done.6, s32[512]{0:T(512)S(1)} %broadcast_subtract_fusion), kind=kOutput, calls=%fused_computation | convolution fusion | flops 845578240 | bytes 3610624 | tf_op jit(solution)/shard_map/products/dot_general | solution.py:89
  136.2 10.0 %all-to-all-done.5 = f16[16,8,640]{2,1,0:T(8,128)(2,1)S(1)} async-done(((f16[16,8,640]{2,1,0:T(8,128)(2,1)}), f16[16,8,640]{2,1,0:T(8,128)(2,1)S(1)}, u32[]{:S(2)}, u32[]{:S(2)}) %all-to-all-start.5) | async-done | bytes 163872 | tf_op jit(solution)/shard_map/scatter_hidden_grad/all_to_all | solution.py:33
  146.3 0.6 multiply_convert_fusion
  (32 shorter events, 1.0 us)
Async XLA Ops:
  0.6 46.4 %copy-start = (bf16[1280,640]{1,0:T(8,128)(2,1)S(1)}, bf16[1280,640]{1,0:T(8,128)(2,1)}, u32[]{:S(2)}) copy-start(bf16[1280,640]{1,0:T(8,128)(2,1)} %param.6) | copy-start | bytes 4915204
  2.1 30.8 %all-to-all-start = ((bf16[16,8,640]{2,1,0:T(8,128)(2,1)}), bf16[16,8,640]{2,1,0:T(8,128)(2,1)S(1)}, u32[]{:S(2)}, u32[]{:S(2)}) async-start(bf16[16,8,640]{2,1,0:T(8,128)(2,1)} %broadcast_in_dim.32), calls=%async_computation | async-start | bytes 327680 | tf_op jit(solution)/shard_map/gather_hidden/all_to_all | solution.py:16
  48.6 4.2 %collective-permute-start = (f16[256,1280]{1,0:T(8,128)(2,1)}, f16[256,1280]{1,0:T(8,128)(2,1)S(1)}, u32[]{:S(2)}, u32[]{:S(2)}) collective-permute-start(f16[256,1280]{1,0:T(8,128)(2,1)} %fusion), channel_id=1, source_target_pairs={{0,1},{1,0},{2,3},{3,2},{4,5},{5,4},{6,7},{7,6},{8,9},{9,8},{10,11... | collective-permute-start | bytes 1966088 | tf_op jit(solution)/shard_map/logits/ppermute | solution.py:32
  51.3 7.3 %copy-start.5 = (s32[512]{0:T(512)S(1)}, s32[512]{0:T(512)}, u32[]{:S(2)}) copy-start(s32[512]{0:T(512)} %param.7) | copy-start | bytes 6148
  51.3 7.4 %copy-start.4 = (s32[512]{0:T(512)S(1)}, s32[512]{0:T(512)}, u32[]{:S(2)}) copy-start(s32[512]{0:T(512)} %param.8) | copy-start | bytes 6148
  51.3 7.4 %copy-start.6 = (f32[512]{0:T(512)S(1)}, f32[512]{0:T(512)}, u32[]{:S(2)}) copy-start(f32[512]{0:T(512)} %param.9) | copy-start | bytes 6148
  53.9 13.8 %all-to-all-start.1 = ((f16[4,64,1280]{2,1,0:T(8,128)(2,1)}), f16[4,64,1280]{2,1,0:T(8,128)(2,1)S(1)}, u32[]{:S(2)}, u32[]{:S(2)}) async-start(f16[4,64,1280]{2,1,0:T(8,128)(2,1)} %bitcast.1), calls=%async_computation.1 | async-start | bytes 1310720 | tf_op jit(solution)/shard_map/logits/all_to_all | solution.py:33
  68.9 22.7 %all-to-all-start.2 = ((f32[64,1,128]{2,1,0:T(1,128)}), f32[64,1,128]{2,1,0:T(1,128)S(1)}, u32[]{:S(2)}, u32[]{:S(2)}) async-start(f32[64,1,128]{2,1,0:T(1,128)} %broadcast_in_dim.34), calls=%async_computation.2 | async-start | bytes 65536 | tf_op jit(solution)/shard_map/statistics/all_to_all | solution.py:33
  89.7 11.6 %collective-permute-start.1 = (bf16[256,1280]{1,0:T(8,128)(2,1)S(1)}, bf16[256,1280]{1,0:T(8,128)(2,1)}, u32[]{:S(2)}, u32[]{:S(2)}) collective-permute-start(bf16[256,1280]{1,0:T(8,128)(2,1)S(1)} %all_gather.7), channel_id=1, source_target_pairs={{0,1},{1,0},{2,3},{3,2},{4,5},{5,4},{6,7},{7,6},{8,9},{9,8},{10,11... | collective-permute-start | bytes 1966088 | tf_op jit(solution)/shard_map/gather_raised/ppermute | solution.py:32
  92.5 8.6 %all-to-all-start.3 = ((f32[8,1,256]{2,1,0:T(1,128)}), f32[8,1,256]{2,1,0:T(1,128)S(1)}, u32[]{:S(2)}, u32[]{:S(2)}) async-start(f32[8,1,256]{2,1,0:T(1,128)} %broadcast_in_dim.35), calls=%async_computation.3 | async-start | bytes 16384 | tf_op jit(solution)/shard_map/statistics/all_to_all | solution.py:33
  102.5 1.5 %copy-start.1 = (bf16[256,1280]{1,0:T(8,128)(2,1)}, bf16[256,1280]{1,0:T(8,128)(2,1)S(1)}, u32[]{:S(2)}) copy-start(bf16[256,1280]{1,0:T(8,128)(2,1)S(1)} %get-tuple-element.15) | copy-start | bytes 1966084
  102.5 1.5 %copy-start.3 = (bf16[256,1280]{1,0:T(8,128)(2,1)}, bf16[256,1280]{1,0:T(8,128)(2,1)S(1)}, u32[]{:S(2)}) copy-start(bf16[256,1280]{1,0:T(8,128)(2,1)S(1)} %get-tuple-element.16) | copy-start | bytes 1966084
  104.0 28.5 %copy-start.2 = (bf16[256,1280]{1,0:T(8,128)(2,1)S(1)}, bf16[256,1280]{1,0:T(8,128)(2,1)}, u32[]{:S(2)}) copy-start(bf16[256,1280]{1,0:T(8,128)(2,1)} %copy-done.1) | copy-start | bytes 1966084
  119.9 26.3 %all-to-all-start.5 = ((f16[16,8,640]{2,1,0:T(8,128)(2,1)}), f16[16,8,640]{2,1,0:T(8,128)(2,1)S(1)}, u32[]{:S(2)}, u32[]{:S(2)}) async-start(f16[16,8,640]{2,1,0:T(8,128)(2,1)} %convert_bitcast_fusion), calls=%async_computation.5 | async-start | bytes 327680 | tf_op jit(solution)/shard_map/scatter_hidden_grad/all_to_all | solution.py:33

commit v11 on v8

--- a/solution.py
+++ b/solution.py
@@ -66,6 +66,7 @@
         near = lax.all_gather(raised.astype(bf16), "y", axis=0, tiled=True)
         far = swap(near)
         raised = jnp.concatenate([jnp.where(is_low, near, far), jnp.where(is_low, far, near)])
+        raised = lax.optimization_barrier(raised)
 
     with jax.named_scope("statistics"):
         every = turn(mine, ("z", "x"))

time: 149 us -> 149 us (level)
  no operation moved by 1% of the time
where the time goes in v11:
time: 149 us; the launch traced here: 147 us
  blocking collectives  59.3 us (40%)
  starting transfers between devices  37.8 us (25%)
  waiting for transfers between devices  31 us (21%)
  matrix products  7.72 us (5%)
  other arithmetic  5.99 us (4%)
  local copies, waits for them, and re-layouts  3.39 us (2%)
    all_to_all x1, blocking collectives, spread(): copies = lax.all_to_all(copies, axis, 0, 0, tiled=True)  30.6 us
    all_to_all x4, starting transfers between devices, shards(): turn = lambda v, axis: lax.all_to_all(v, axis, 0, 0, tiled=True)  29.7 us
    all_to_all x4, waiting for transfers between devices, shards(): turn = lambda v, axis: lax.all_to_all(v, axis, 0, 0, tiled=True)  20.7 us
    all_to_all x1, blocking collectives, shards(): turn = lambda v, axis: lax.all_to_all(v, axis, 0, 0, tiled=True)  15 us
    all_gather x1, blocking collectives, shards(): near = lax.all_gather(raised.astype(bf16), 'y', axis=0, tiled=True)  13.6 us
    all_to_all x1, waiting for transfers between devices, spread(): copies = lax.all_to_all(copies, axis, 0, 0, tiled=True)  8.79 us
    all_to_all x1, starting transfers between devices, spread(): copies = lax.all_to_all(copies, axis, 0, 0, tiled=True)  4.29 us
    dot_general x1, matrix products, shards(): lax.dot_general(dlogits, hidden, outer, preferred_element_type=f32)  3.99 us
  transfers between devices with their start and end apart: 7, of which 5 were waited for; matrix products, arithmetic and copies ran while one was open for 5% of the time, Pallas kernels for 0%

profile of v11, /device:TPU:24, one launch (start us, length us, event | category | flops | bytes accessed | tf_op | source)
XLA Modules:
  0.0 146.6 jit_solution(9002286370134604699)
XLA Ops:
  0.6 0.8 broadcast_in_dim.35
  1.5 30.6 %all_to_all.43 = bf16[16,8,640]{2,1,0:T(8,128)(2,1)S(1)} all-to-all(bf16[16,8,640]{2,1,0:T(8,128)(2,1)S(1)} %broadcast_in_dim.35), channel_id=1, replica_groups=mesh['x'=4,'z'=16,'y'=4,'c'=2] {'z'}, dimensions={0} | all-to-all | bytes 327680 | tf_op jit(solution)/shard_map/gather_hidden/all_to_all | solution.py:16
  32.1 0.9 broadcast_in_dim.36
  33.0 4.3 %all-to-all-start.1 = ((bf16[4,128,640]{2,1,0:T(8,128)(2,1)}), bf16[4,128,640]{2,1,0:T(8,128)(2,1)S(1)}, u32[]{:S(2)}, u32[]{:S(2)}) async-start(bf16[4,128,640]{2,1,0:T(8,128)(2,1)} %broadcast_in_dim.36), calls=%async_computation.1 | async-start | bytes 1310720 | tf_op jit(solution)/shard_map/gather_hidden/all_to_all | solution.py:16
  37.3 8.8 %all-to-all-done.1 = bf16[4,128,640]{2,1,0:T(8,128)(2,1)S(1)} async-done(((bf16[4,128,640]{2,1,0:T(8,128)(2,1)}), bf16[4,128,640]{2,1,0:T(8,128)(2,1)S(1)}, u32[]{:S(2)}, u32[]{:S(2)}) %all-to-all-start.1) | async-done | bytes 655392 | tf_op jit(solution)/shard_map/gather_hidden/all_to_all | solution.py:16
  46.1 1.5 %fusion = f16[256,1280]{1,0:T(8,128)(2,1)} fusion(bf16[1280,640]{1,0:T(8,128)(2,1)S(1)} %copy-done, bf16[512,640]{1,0:T(8,128)(2,1)S(1)} %bitcast.15, s32[]{:T(128)S(6)} %select_n.31), kind=kOutput, calls=%fused_computation.4 | convolution fusion | flops 420085760 | bytes 2621444 | tf_op jit(solution)/shard_map/logits/dot_general | solution.py:49
  47.6 1.9 %collective-permute-start = (f16[256,1280]{1,0:T(8,128)(2,1)}, f16[256,1280]{1,0:T(8,128)(2,1)S(1)}, u32[]{:S(2)}, u32[]{:S(2)}) collective-permute-start(f16[256,1280]{1,0:T(8,128)(2,1)} %fusion), channel_id=1, source_target_pairs={{0,1},{1,0},{2,3},{3,2},{4,5},{5,4},{6,7},{7,6},{8,9},{9,8},{10,11... | collective-permute-start | bytes 1966088 | tf_op jit(solution)/shard_map/logits/ppermute | solution.py:32
  49.6 0.7 fusion.3
  50.3 1.5 %collective-permute-done = f16[256,1280]{1,0:T(8,128)(2,1)S(1)} collective-permute-done((f16[256,1280]{1,0:T(8,128)(2,1)}, f16[256,1280]{1,0:T(8,128)(2,1)S(1)}, u32[]{:S(2)}, u32[]{:S(2)}) %collective-permute-start) | collective-permute-done | bytes 655392 | tf_op jit(solution)/shard_map/logits/ppermute | solution.py:32
  51.8 1.1 add_convert_fusion
  52.9 4.7 %all-to-all-start.2 = ((f16[4,64,1280]{2,1,0:T(8,128)(2,1)}), f16[4,64,1280]{2,1,0:T(8,128)(2,1)S(1)}, u32[]{:S(2)}, u32[]{:S(2)}) async-start(f16[4,64,1280]{2,1,0:T(8,128)(2,1)} %bitcast.2), calls=%async_computation.2 | async-start | bytes 1310720 | tf_op jit(solution)/shard_map/logits/all_to_all | solution.py:33
  57.7 0.6 abs_reduce_fusion
  58.3 8.4 %all-to-all-done.2 = f16[4,64,1280]{2,1,0:T(8,128)(2,1)S(1)} async-done(((f16[4,64,1280]{2,1,0:T(8,128)(2,1)}), f16[4,64,1280]{2,1,0:T(8,128)(2,1)S(1)}, u32[]{:S(2)}, u32[]{:S(2)}) %all-to-all-start.2) | async-done | bytes 655392 | tf_op jit(solution)/shard_map/logits/all_to_all | solution.py:33
  66.8 0.1 multiply_reduce_fusion
  66.9 0.3 fusion.6
  67.3 0.6 broadcast_in_dim.38
  67.9 7.9 %all-to-all-start.3 = ((f32[64,1,128]{2,1,0:T(1,128)}), f32[64,1,128]{2,1,0:T(1,128)S(1)}, u32[]{:S(2)}, u32[]{:S(2)}) async-start(f32[64,1,128]{2,1,0:T(1,128)} %broadcast_in_dim.38), calls=%async_computation.3 | async-start | bytes 65536 | tf_op jit(solution)/shard_map/statistics/all_to_all | solution.py:33
  75.8 13.6 %all_gather.3 = bf16[256,1280]{1,0:T(8,128)(2,1)S(1)} all-gather(bf16[64,1280]{1,0:T(8,128)(2,1)S(1)} %get-tuple-element.17), channel_id=1, replica_groups=mesh['x'=4,'z'=16,'y'=4,'c'=2] {'y'}, dimensions={0}, use_global_device_ids=true | all-gather | bytes 819200 | tf_op jit(solution)/shard_map/gather_raised/all_gather | solution.py:66
  89.5 1.9 %collective-permute-start.1 = (bf16[256,1280]{1,0:T(8,128)(2,1)S(1)}, bf16[256,1280]{1,0:T(8,128)(2,1)}, u32[]{:S(2)}, u32[]{:S(2)}) collective-permute-start(bf16[256,1280]{1,0:T(8,128)(2,1)S(1)} %all_gather.3), channel_id=1, source_target_pairs={{0,1},{1,0},{2,3},{3,2},{4,5},{5,4},{6,7},{7,6},{8,9},{9,8},{10,11... | collective-permute-start | bytes 1966088 | tf_op jit(solution)/shard_map/gather_raised/ppermute | solution.py:32
  91.4 0.1 slice_reduce_fusion
  91.7 0.6 broadcast_in_dim.39
  92.3 5.4 %all-to-all-start.4 = ((f32[8,1,256]{2,1,0:T(1,128)}), f32[8,1,256]{2,1,0:T(1,128)S(1)}, u32[]{:S(2)}, u32[]{:S(2)}) async-start(f32[8,1,256]{2,1,0:T(1,128)} %broadcast_in_dim.39), calls=%async_computation.4 | async-start | bytes 16384 | tf_op jit(solution)/shard_map/statistics/all_to_all | solution.py:33
  98.4 2.5 %all-to-all-done.4 = f32[8,1,256]{2,1,0:T(1,128)S(1)} async-done(((f32[8,1,256]{2,1,0:T(1,128)}), f32[8,1,256]{2,1,0:T(1,128)S(1)}, u32[]{:S(2)}, u32[]{:S(2)}) %all-to-all-start.4) | async-done | bytes 8224 | tf_op jit(solution)/shard_map/statistics/all_to_all | solution.py:33
  101.1 1.2 broadcast_select_fusion.1
  102.4 1.5 %fusion.1 = f16[512,640]{1,0:T(8,128)(2,1)S(1)} fusion(bf16[1280,640]{1,0:T(8,128)(2,1)S(1)} %copy-done, f32[]{:T(128)S(6)} %div.7, bf16[512,1280]{1,0:T(8,128)(2,1)S(1)} %pad_maximum_fusion, f32[512]{0:T(512)S(1)} %mul.82, f32[512]{0:T(512)S(1)} %copy-done.4, s32[512]{0:T(512)S(1)} %broadcast_subtract_fusion), kind=kOutput, calls=%fused_computation.6 | convolution fusion | flops 843448320 | bytes 3610628 | tf_op jit(solution)/shard_map/products/dot_general | solution.py:87
  103.9 15.0 %all_to_all.44 = f16[4,128,640]{2,1,0:T(8,128)(2,1)S(1)} all-to-all(f16[4,128,640]{2,1,0:T(8,128)(2,1)S(1)} %bitcast.18), channel_id=1, replica_groups=mesh['x'=4,'z'=16,'y'=4,'c'=2] {'x'}, dimensions={0} | all-to-all | bytes 1310720 | tf_op jit(solution)/shard_map/scatter_hidden_grad/all_to_all | solution.py:33
  119.0 0.7 convert_bitcast_fusion
  119.6 11.7 %all-to-all-start.6 = ((f16[16,8,640]{2,1,0:T(8,128)(2,1)}), f16[16,8,640]{2,1,0:T(8,128)(2,1)S(1)}, u32[]{:S(2)}, u32[]{:S(2)}) async-start(f16[16,8,640]{2,1,0:T(8,128)(2,1)} %convert_bitcast_fusion), calls=%async_computation.6 | async-start | bytes 327680 | tf_op jit(solution)/shard_map/scatter_hidden_grad/all_to_all | solution.py:33
  131.5 0.7 fusion.7
  132.2 4.0 %convolution_convert_fusion = bf16[1280,640]{1,0:T(8,128)(2,1)} fusion(bf16[512,640]{1,0:T(8,128)(2,1)S(1)} %bitcast.17, bf16[512,1280]{1,0:T(8,128)(2,1)} %copy-done.1, f32[512]{0:T(512)S(1)} %mul.82, f32[512]{0:T(512)S(1)} %copy-done.4, s32[512]{0:T(512)S(1)} %broadcast_subtract_fusion), kind=kOutput, calls=%fused_computation | convolution fusion | flops 843612160 | bytes 3610624 | tf_op jit(solution)/shard_map/products/dot_general | solution.py:90
  136.2 9.8 %all-to-all-done.6 = f16[16,8,640]{2,1,0:T(8,128)(2,1)S(1)} async-done(((f16[16,8,640]{2,1,0:T(8,128)(2,1)}), f16[16,8,640]{2,1,0:T(8,128)(2,1)S(1)}, u32[]{:S(2)}, u32[]{:S(2)}) %all-to-all-start.6) | async-done | bytes 163872 | tf_op jit(solution)/shard_map/scatter_hidden_grad/all_to_all | solution.py:33
  146.0 0.6 multiply_convert_fusion
  (30 shorter events, 1.1 us)
Async XLA Ops:
  0.6 45.5 %copy-start = (bf16[1280,640]{1,0:T(8,128)(2,1)S(1)}, bf16[1280,640]{1,0:T(8,128)(2,1)}, u32[]{:S(2)}) copy-start(bf16[1280,640]{1,0:T(8,128)(2,1)} %param.6) | copy-start | bytes 4915204
  33.0 13.1 %all-to-all-start.1 = ((bf16[4,128,640]{2,1,0:T(8,128)(2,1)}), bf16[4,128,640]{2,1,0:T(8,128)(2,1)S(1)}, u32[]{:S(2)}, u32[]{:S(2)}) async-start(bf16[4,128,640]{2,1,0:T(8,128)(2,1)} %broadcast_in_dim.36), calls=%async_computation.1 | async-start | bytes 1310720 | tf_op jit(solution)/shard_map/gather_hidden/all_to_all | solution.py:16
  47.6 4.2 %collective-permute-start = (f16[256,1280]{1,0:T(8,128)(2,1)}, f16[256,1280]{1,0:T(8,128)(2,1)S(1)}, u32[]{:S(2)}, u32[]{:S(2)}) collective-permute-start(f16[256,1280]{1,0:T(8,128)(2,1)} %fusion), channel_id=1, source_target_pairs={{0,1},{1,0},{2,3},{3,2},{4,5},{5,4},{6,7},{7,6},{8,9},{9,8},{10,11... | collective-permute-start | bytes 1966088 | tf_op jit(solution)/shard_map/logits/ppermute | solution.py:32
  50.3 7.3 %copy-start.3 = (s32[512]{0:T(512)S(1)}, s32[512]{0:T(512)}, u32[]{:S(2)}) copy-start(s32[512]{0:T(512)} %param.7) | copy-start | bytes 6148
  50.3 7.4 %copy-start.2 = (s32[512]{0:T(512)S(1)}, s32[512]{0:T(512)}, u32[]{:S(2)}) copy-start(s32[512]{0:T(512)} %param.8) | copy-start | bytes 6148
  50.3 7.4 %copy-start.4 = (f32[512]{0:T(512)S(1)}, f32[512]{0:T(512)}, u32[]{:S(2)}) copy-start(f32[512]{0:T(512)} %param.9) | copy-start | bytes 6148
  52.9 13.8 %all-to-all-start.2 = ((f16[4,64,1280]{2,1,0:T(8,128)(2,1)}), f16[4,64,1280]{2,1,0:T(8,128)(2,1)S(1)}, u32[]{:S(2)}, u32[]{:S(2)}) async-start(f16[4,64,1280]{2,1,0:T(8,128)(2,1)} %bitcast.2), calls=%async_computation.2 | async-start | bytes 1310720 | tf_op jit(solution)/shard_map/logits/all_to_all | solution.py:33
  67.9 23.5 %all-to-all-start.3 = ((f32[64,1,128]{2,1,0:T(1,128)}), f32[64,1,128]{2,1,0:T(1,128)S(1)}, u32[]{:S(2)}, u32[]{:S(2)}) async-start(f32[64,1,128]{2,1,0:T(1,128)} %broadcast_in_dim.38), calls=%async_computation.3 | async-start | bytes 65536 | tf_op jit(solution)/shard_map/statistics/all_to_all | solution.py:33
  89.5 11.6 %collective-permute-start.1 = (bf16[256,1280]{1,0:T(8,128)(2,1)S(1)}, bf16[256,1280]{1,0:T(8,128)(2,1)}, u32[]{:S(2)}, u32[]{:S(2)}) collective-permute-start(bf16[256,1280]{1,0:T(8,128)(2,1)S(1)} %all_gather.3), channel_id=1, source_target_pairs={{0,1},{1,0},{2,3},{3,2},{4,5},{5,4},{6,7},{7,6},{8,9},{9,8},{10,11... | collective-permute-start | bytes 1966088 | tf_op jit(solution)/shard_map/gather_raised/ppermute | solution.py:32
  92.3 8.6 %all-to-all-start.4 = ((f32[8,1,256]{2,1,0:T(1,128)}), f32[8,1,256]{2,1,0:T(1,128)S(1)}, u32[]{:S(2)}, u32[]{:S(2)}) async-start(f32[8,1,256]{2,1,0:T(1,128)} %broadcast_in_dim.39), calls=%async_computation.4 | async-start | bytes 16384 | tf_op jit(solution)/shard_map/statistics/all_to_all | solution.py:33
  102.4 1.5 %copy-start.1 = (bf16[512,1280]{1,0:T(8,128)(2,1)}, bf16[512,1280]{1,0:T(8,128)(2,1)S(1)}, u32[]{:S(2)}) copy-start(bf16[512,1280]{1,0:T(8,128)(2,1)S(1)} %pad_maximum_fusion) | copy-start | bytes 3932164
  119.6 26.3 %all-to-all-start.6 = ((f16[16,8,640]{2,1,0:T(8,128)(2,1)}), f16[16,8,640]{2,1,0:T(8,128)(2,1)S(1)}, u32[]{:S(2)}, u32[]{:S(2)}) async-start(f16[16,8,640]{2,1,0:T(8,128)(2,1)} %convert_bitcast_fusion), calls=%async_computation.6 | async-start | bytes 327680 | tf_op jit(solution)/shard_map/scatter_hidden_grad/all_to_all | solution.py:33

commit v12 on v10

--- a/solution.py
+++ b/solution.py
@@ -35,12 +35,14 @@
 
     keep = discount * (1.0 - terminal.astype(f32))
     carried = jnp.concatenate([jnp.zeros((1,), f32), (keep * cotangent)[:-1]])
-    unit = jnp.maximum(jnp.max(jnp.abs(cotangent)), 1e-30)
-    down, up = lax.optimization_barrier((unit / raise_grad, raise_grad / unit))
     column = jnp.arange(rows, dtype=jnp.int32)
 
     with jax.named_scope("gather_hidden"):
         hidden = lax.all_gather(spread(hidden_states, "z"), "x", axis=0, tiled=True)
+
+    hidden, held = lax.optimization_barrier((hidden, cotangent))
+    unit = jnp.maximum(jnp.max(jnp.abs(held)), 1e-30)
+    down, up = lax.optimization_barrier((unit / raise_grad, raise_grad / unit))
 
     with jax.named_scope("logits"):
         near_h = lax.dynamic_slice_in_dim(hidden, c * half, half)

time: 149 us -> 149 us (level)
  no operation moved by 1% of the time
where the time goes in v12:
time: 149 us; the launch traced here: 147 us
  starting transfers between devices  47.9 us (32%)
  blocking collectives  42.9 us (29%)
  waiting for transfers between devices  38 us (26%)
  matrix products  7.49 us (5%)
  other arithmetic  5.91 us (4%)
  local copies, waits for them, and re-layouts  3.18 us (2%)
  between operations  1.52 us (1%)
    all_to_all x4, starting transfers between devices, shards(): turn = lambda v, axis: lax.all_to_all(v, axis, 0, 0, tiled=True)  28.9 us
    all_to_all x4, waiting for transfers between devices, shards(): turn = lambda v, axis: lax.all_to_all(v, axis, 0, 0, tiled=True)  20.9 us
    all_to_all x1, waiting for transfers between devices, spread(): copies = lax.all_to_all(copies, axis, 0, 0, tiled=True)  15.6 us
    all_to_all x1, starting transfers between devices, spread(): copies = lax.all_to_all(copies, axis, 0, 0, tiled=True)  15.2 us
    all_to_all x1, blocking collectives, shards(): turn = lambda v, axis: lax.all_to_all(v, axis, 0, 0, tiled=True)  15.1 us
    all_gather x1, blocking collectives, shards(): hidden = lax.all_gather(spread(hidden_states, 'z'), 'x', axis=0, tiled=True)  14.1 us
    all_gather x1, blocking collectives, shards(): near = lax.all_gather(raised.astype(bf16), 'y', axis=0, tiled=True)  13.6 us
    ppermute x2, starting transfers between devices, shards(): swap = lambda v: lax.ppermute(v, 'c', [(0, 1), (1, 0)])  3.82 us
  transfers between devices with their start and end apart: 7, of which 5 were waited for; matrix products, arithmetic and copies ran while one was open for 5% of the time, Pallas kernels for 0%

profile of v12, /device:TPU:24, one launch (start us, length us, event | category | flops | bytes accessed | tf_op | source)
XLA Modules:
  0.0 146.9 jit_solution(14769262522842276308)
XLA Ops:
  0.6 1.5 %broadcast_in_dim.32 = bf16[16,8,640]{2,1,0:T(8,128)(2,1)} broadcast(bf16[8,640]{1,0:T(8,128)(2,1)} %param.5), dimensions={1,2} | broadcast | bytes 174080 | tf_op jit(solution)/shard_map/gather_hidden/broadcast_in_dim | solution.py:15
  2.1 15.2 %all-to-all-start = ((bf16[16,8,640]{2,1,0:T(8,128)(2,1)}), bf16[16,8,640]{2,1,0:T(8,128)(2,1)S(1)}, u32[]{:S(2)}, u32[]{:S(2)}) async-start(bf16[16,8,640]{2,1,0:T(8,128)(2,1)} %broadcast_in_dim.32), calls=%async_computation | async-start | bytes 327680 | tf_op jit(solution)/shard_map/gather_hidden/all_to_all | solution.py:16
  17.4 15.6 %all-to-all-done = bf16[16,8,640]{2,1,0:T(8,128)(2,1)S(1)} async-done(((bf16[16,8,640]{2,1,0:T(8,128)(2,1)}), bf16[16,8,640]{2,1,0:T(8,128)(2,1)S(1)}, u32[]{:S(2)}, u32[]{:S(2)}) %all-to-all-start) | async-done | bytes 163872 | tf_op jit(solution)/shard_map/gather_hidden/all_to_all | solution.py:16
  33.0 14.1 %all_gather.6 = bf16[512,640]{1,0:T(8,128)(2,1)S(1)} all-gather(bf16[128,640]{1,0:T(8,128)(2,1)S(1)} %bitcast.15), channel_id=1, replica_groups=mesh['x'=4,'z'=16,'y'=4,'c'=2] {'x'}, dimensions={0}, use_global_device_ids=true | all-gather | bytes 819200 | tf_op jit(solution)/shard_map/gather_hidden/all_gather | solution.py:41
  47.1 1.6 %fusion = f16[256,1280]{1,0:T(8,128)(2,1)} fusion(bf16[1280,640]{1,0:T(8,128)(2,1)S(1)} %copy-done, bf16[512,640]{1,0:T(8,128)(2,1)S(1)} %all_gather.6, s32[]{:T(128)S(6)} %select_n.31), kind=kOutput, calls=%fused_computation.4 | convolution fusion | flops 420085760 | bytes 2621444 | tf_op jit(solution)/shard_map/logits/dot_general | solution.py:51
  48.6 1.9 %collective-permute-start = (f16[256,1280]{1,0:T(8,128)(2,1)}, f16[256,1280]{1,0:T(8,128)(2,1)S(1)}, u32[]{:S(2)}, u32[]{:S(2)}) collective-permute-start(f16[256,1280]{1,0:T(8,128)(2,1)} %fusion), channel_id=1, source_target_pairs={{0,1},{1,0},{2,3},{3,2},{4,5},{5,4},{6,7},{7,6},{8,9},{9,8},{10,11... | collective-permute-start | bytes 1966088 | tf_op jit(solution)/shard_map/logits/ppermute | solution.py:32
  50.5 0.7 fusion.3
  51.3 1.5 %collective-permute-done = f16[256,1280]{1,0:T(8,128)(2,1)S(1)} collective-permute-done((f16[256,1280]{1,0:T(8,128)(2,1)}, f16[256,1280]{1,0:T(8,128)(2,1)S(1)}, u32[]{:S(2)}, u32[]{:S(2)}) %collective-permute-start) | collective-permute-done | bytes 655392 | tf_op jit(solution)/shard_map/logits/ppermute | solution.py:32
  52.8 1.1 add_convert_fusion
  53.9 4.7 %all-to-all-start.1 = ((f16[4,64,1280]{2,1,0:T(8,128)(2,1)}), f16[4,64,1280]{2,1,0:T(8,128)(2,1)S(1)}, u32[]{:S(2)}, u32[]{:S(2)}) async-start(f16[4,64,1280]{2,1,0:T(8,128)(2,1)} %bitcast.1), calls=%async_computation.1 | async-start | bytes 1310720 | tf_op jit(solution)/shard_map/logits/all_to_all | solution.py:33
  58.8 8.9 %all-to-all-done.1 = f16[4,64,1280]{2,1,0:T(8,128)(2,1)S(1)} async-done(((f16[4,64,1280]{2,1,0:T(8,128)(2,1)}), f16[4,64,1280]{2,1,0:T(8,128)(2,1)S(1)}, u32[]{:S(2)}, u32[]{:S(2)}) %all-to-all-start.1) | async-done | bytes 655392 | tf_op jit(solution)/shard_map/logits/all_to_all | solution.py:33
  67.8 0.1 multiply_reduce_fusion
  67.9 0.3 fusion.6
  68.3 0.6 broadcast_in_dim.34
  68.9 7.1 %all-to-all-start.2 = ((f32[64,1,128]{2,1,0:T(1,128)}), f32[64,1,128]{2,1,0:T(1,128)S(1)}, u32[]{:S(2)}, u32[]{:S(2)}) async-start(f32[64,1,128]{2,1,0:T(1,128)} %broadcast_in_dim.34), calls=%async_computation.2 | async-start | bytes 65536 | tf_op jit(solution)/shard_map/statistics/all_to_all | solution.py:33
  76.1 13.6 %all_gather.7 = bf16[256,1280]{1,0:T(8,128)(2,1)S(1)} all-gather(bf16[64,1280]{1,0:T(8,128)(2,1)S(1)} %get-tuple-element.21), channel_id=1, replica_groups=mesh['x'=4,'z'=16,'y'=4,'c'=2] {'y'}, dimensions={0}, use_global_device_ids=true | all-gather | bytes 819200 | tf_op jit(solution)/shard_map/gather_raised/all_gather | solution.py:68
  89.7 1.9 %collective-permute-start.1 = (bf16[256,1280]{1,0:T(8,128)(2,1)S(1)}, bf16[256,1280]{1,0:T(8,128)(2,1)}, u32[]{:S(2)}, u32[]{:S(2)}) collective-permute-start(bf16[256,1280]{1,0:T(8,128)(2,1)S(1)} %all_gather.7), channel_id=1, source_target_pairs={{0,1},{1,0},{2,3},{3,2},{4,5},{5,4},{6,7},{7,6},{8,9},{9,8},{10,11... | collective-permute-start | bytes 1966088 | tf_op jit(solution)/shard_map/gather_raised/ppermute | solution.py:32
  91.6 0.1 slice_reduce_fusion
  91.9 0.6 broadcast_in_dim.35
  92.5 5.4 %all-to-all-start.3 = ((f32[8,1,256]{2,1,0:T(1,128)}), f32[8,1,256]{2,1,0:T(1,128)S(1)}, u32[]{:S(2)}, u32[]{:S(2)}) async-start(f32[8,1,256]{2,1,0:T(1,128)} %broadcast_in_dim.35), calls=%async_computation.3 | async-start | bytes 16384 | tf_op jit(solution)/shard_map/statistics/all_to_all | solution.py:33
  97.9 0.6 abs_reduce_fusion
  99.2 1.9 %all-to-all-done.3 = f32[8,1,256]{2,1,0:T(1,128)S(1)} async-done(((f32[8,1,256]{2,1,0:T(1,128)}), f32[8,1,256]{2,1,0:T(1,128)S(1)}, u32[]{:S(2)}, u32[]{:S(2)}) %all-to-all-start.3) | async-done | bytes 8224 | tf_op jit(solution)/shard_map/statistics/all_to_all | solution.py:33
  101.3 1.2 broadcast_select_fusion.1
  102.5 1.5 %fusion.1 = f16[512,640]{1,0:T(8,128)(2,1)S(1)} fusion(bf16[1280,640]{1,0:T(8,128)(2,1)S(1)} %copy-done, f32[]{:T(128)S(6)} %div.7, bf16[256,1280]{1,0:T(8,128)(2,1)S(1)} %get-tuple-element.20, bf16[256,1280]{1,0:T(8,128)(2,1)S(1)} %get-tuple-element.19, f32[512]{0:T(512)S(1)} %mul.82, f32[512]{0:T(512)S(1)} %copy-done.5, s32[512]{0:T(512)S(1)} %broadcast_subtract_fusion), kind=kOutput, calls=%fused_computation.6 | convolution fusion | flops 845414400 | bytes 3610628 | tf_op jit(solution)/shard_map/products/dot_general | solution.py:88
  104.0 15.1 %all_to_all.38 = f16[4,128,640]{2,1,0:T(8,128)(2,1)S(1)} all-to-all(f16[4,128,640]{2,1,0:T(8,128)(2,1)S(1)} %bitcast.14), channel_id=1, replica_groups=mesh['x'=4,'z'=16,'y'=4,'c'=2] {'x'}, dimensions={0} | all-to-all | bytes 1310720 | tf_op jit(solution)/shard_map/scatter_hidden_grad/all_to_all | solution.py:33
  119.1 0.1 convert_reduce_fusion
  119.2 0.7 convert_bitcast_fusion
  119.9 11.7 %all-to-all-start.5 = ((f16[16,8,640]{2,1,0:T(8,128)(2,1)}), f16[16,8,640]{2,1,0:T(8,128)(2,1)S(1)}, u32[]{:S(2)}, u32[]{:S(2)}) async-start(f16[16,8,640]{2,1,0:T(8,128)(2,1)} %convert_bitcast_fusion), calls=%async_computation.5 | async-start | bytes 327680 | tf_op jit(solution)/shard_map/scatter_hidden_grad/all_to_all | solution.py:33
  131.8 0.7 fusion.7
  132.5 3.8 %convolution_convert_fusion = bf16[1280,640]{1,0:T(8,128)(2,1)} fusion(bf16[512,640]{1,0:T(8,128)(2,1)S(1)} %all_gather.6, bf16[256,1280]{1,0:T(8,128)(2,1)} %copy-done.3, bf16[256,1280]{1,0:T(8,128)(2,1)S(1)} %copy-done.2, f32[512]{0:T(512)S(1)} %mul.82, f32[512]{0:T(512)S(1)} %copy-done.5, s32[512]{0:T(512)S(1)} %broadcast_subtract_fusion), kind=kOutput, calls=%fused_computation | convolution fusion | flops 845578240 | bytes 3610624 | tf_op jit(solution)/shard_map/products/dot_general | solution.py:91
  136.2 10.0 %all-to-all-done.5 = f16[16,8,640]{2,1,0:T(8,128)(2,1)S(1)} async-done(((f16[16,8,640]{2,1,0:T(8,128)(2,1)}), f16[16,8,640]{2,1,0:T(8,128)(2,1)S(1)}, u32[]{:S(2)}, u32[]{:S(2)}) %all-to-all-start.5) | async-done | bytes 163872 | tf_op jit(solution)/shard_map/scatter_hidden_grad/all_to_all | solution.py:33
  146.3 0.6 multiply_convert_fusion
  (33 shorter events, 1.0 us)
Async XLA Ops:
  0.6 46.4 %copy-start = (bf16[1280,640]{1,0:T(8,128)(2,1)S(1)}, bf16[1280,640]{1,0:T(8,128)(2,1)}, u32[]{:S(2)}) copy-start(bf16[1280,640]{1,0:T(8,128)(2,1)} %param.6) | copy-start | bytes 4915204
  2.1 30.8 %all-to-all-start = ((bf16[16,8,640]{2,1,0:T(8,128)(2,1)}), bf16[16,8,640]{2,1,0:T(8,128)(2,1)S(1)}, u32[]{:S(2)}, u32[]{:S(2)}) async-start(bf16[16,8,640]{2,1,0:T(8,128)(2,1)} %broadcast_in_dim.32), calls=%async_computation | async-start | bytes 327680 | tf_op jit(solution)/shard_map/gather_hidden/all_to_all | solution.py:16
  48.6 4.2 %collective-permute-start = (f16[256,1280]{1,0:T(8,128)(2,1)}, f16[256,1280]{1,0:T(8,128)(2,1)S(1)}, u32[]{:S(2)}, u32[]{:S(2)}) collective-permute-start(f16[256,1280]{1,0:T(8,128)(2,1)} %fusion), channel_id=1, source_target_pairs={{0,1},{1,0},{2,3},{3,2},{4,5},{5,4},{6,7},{7,6},{8,9},{9,8},{10,11... | collective-permute-start | bytes 1966088 | tf_op jit(solution)/shard_map/logits/ppermute | solution.py:32
  51.3 7.3 %copy-start.4 = (s32[512]{0:T(512)S(1)}, s32[512]{0:T(512)}, u32[]{:S(2)}) copy-start(s32[512]{0:T(512)} %param.8) | copy-start | bytes 6148
  51.3 7.3 %copy-start.5 = (f32[512]{0:T(512)S(1)}, f32[512]{0:T(512)}, u32[]{:S(2)}) copy-start(f32[512]{0:T(512)} %param.9) | copy-start | bytes 6148
  51.3 7.3 %copy-start.6 = (s32[512]{0:T(512)S(1)}, s32[512]{0:T(512)}, u32[]{:S(2)}) copy-start(s32[512]{0:T(512)} %param.7) | copy-start | bytes 6148
  53.9 13.8 %all-to-all-start.1 = ((f16[4,64,1280]{2,1,0:T(8,128)(2,1)}), f16[4,64,1280]{2,1,0:T(8,128)(2,1)S(1)}, u32[]{:S(2)}, u32[]{:S(2)}) async-start(f16[4,64,1280]{2,1,0:T(8,128)(2,1)} %bitcast.1), calls=%async_computation.1 | async-start | bytes 1310720 | tf_op jit(solution)/shard_map/logits/all_to_all | solution.py:33
  68.9 22.7 %all-to-all-start.2 = ((f32[64,1,128]{2,1,0:T(1,128)}), f32[64,1,128]{2,1,0:T(1,128)S(1)}, u32[]{:S(2)}, u32[]{:S(2)}) async-start(f32[64,1,128]{2,1,0:T(1,128)} %broadcast_in_dim.34), calls=%async_computation.2 | async-start | bytes 65536 | tf_op jit(solution)/shard_map/statistics/all_to_all | solution.py:33
  89.7 11.6 %collective-permute-start.1 = (bf16[256,1280]{1,0:T(8,128)(2,1)S(1)}, bf16[256,1280]{1,0:T(8,128)(2,1)}, u32[]{:S(2)}, u32[]{:S(2)}) collective-permute-start(bf16[256,1280]{1,0:T(8,128)(2,1)S(1)} %all_gather.7), channel_id=1, source_target_pairs={{0,1},{1,0},{2,3},{3,2},{4,5},{5,4},{6,7},{7,6},{8,9},{9,8},{10,11... | collective-permute-start | bytes 1966088 | tf_op jit(solution)/shard_map/gather_raised/ppermute | solution.py:32
  92.5 8.6 %all-to-all-start.3 = ((f32[8,1,256]{2,1,0:T(1,128)}), f32[8,1,256]{2,1,0:T(1,128)S(1)}, u32[]{:S(2)}, u32[]{:S(2)}) async-start(f32[8,1,256]{2,1,0:T(1,128)} %broadcast_in_dim.35), calls=%async_computation.3 | async-start | bytes 16384 | tf_op jit(solution)/shard_map/statistics/all_to_all | solution.py:33
  102.5 1.5 %copy-start.1 = (bf16[256,1280]{1,0:T(8,128)(2,1)}, bf16[256,1280]{1,0:T(8,128)(2,1)S(1)}, u32[]{:S(2)}) copy-start(bf16[256,1280]{1,0:T(8,128)(2,1)S(1)} %get-tuple-element.19) | copy-start | bytes 1966084
  102.5 1.5 %copy-start.3 = (bf16[256,1280]{1,0:T(8,128)(2,1)}, bf16[256,1280]{1,0:T(8,128)(2,1)S(1)}, u32[]{:S(2)}) copy-start(bf16[256,1280]{1,0:T(8,128)(2,1)S(1)} %get-tuple-element.20) | copy-start | bytes 1966084
  104.0 28.5 %copy-start.2 = (bf16[256,1280]{1,0:T(8,128)(2,1)S(1)}, bf16[256,1280]{1,0:T(8,128)(2,1)}, u32[]{:S(2)}) copy-start(bf16[256,1280]{1,0:T(8,128)(2,1)} %copy-done.1) | copy-start | bytes 1966084
  119.9 26.3 %all-to-all-start.5 = ((f16[16,8,640]{2,1,0:T(8,128)(2,1)}), f16[16,8,640]{2,1,0:T(8,128)(2,1)S(1)}, u32[]{:S(2)}, u32[]{:S(2)}) async-start(f16[16,8,640]{2,1,0:T(8,128)(2,1)} %convert_bitcast_fusion), calls=%async_computation.5 | async-start | bytes 327680 | tf_op jit(solution)/shard_map/scatter_hidden_grad/all_to_all | solution.py:33
